TPU v7x, 128 devices: a whole 4x4x4 slice. The times are simulated.
128 devices in a mesh: dp: 4 (over z_hi, core), ctx: 32 (over z_lo, x, y).
Axes of the slice: x: 4, y: 4, z: 4 (z_hi: 2, z_lo: 2; z = z_hi * 2 + z_lo), core: 2. Of those that a mesh axis runs over, the one named last changes fastest.
Arguments:
- series: bfloat16 [4, 16384, 512], P('dp', 'ctx'), may hold values from -12 to 12
- w_query: bfloat16 [512, 512], replicated, may hold values from -0.375 to 0.375
- w_key: bfloat16 [512, 512], replicated, may hold values from -0.375 to 0.375
- w_value: bfloat16 [512, 512], replicated, may hold values from -0.25 to 0.25
- w_out: bfloat16 [512, 512], replicated, may hold values from -0.25 to 0.25
- cotangent: bfloat16 [4, 16384, 512], P('dp', 'ctx'), may hold values from -6 to 6
Outputs:
- output: bfloat16 [4, 16384, 512], P('dp', 'ctx')
- input_grad: bfloat16 [4, 16384, 512], P('dp', 'ctx')
- grad_query: float32 [512, 512], P(None, ('dp', 'ctx'))
- grad_key: float32 [512, 512], P(None, ('dp', 'ctx'))
- grad_value: float32 [512, 512], P(None, ('dp', 'ctx'))
- grad_out: float32 [512, 512], P(None, ('dp', 'ctx'))
All inputs are finite; a program needn't handle non-finite values.
Results may differ from a plain program's by a relative error of at most 0.034.
Values may be sent and summed in bfloat16 or wider, within the bound.
No kernel may reach another device: no remote copies, remote signals or barrier semaphores. Data moves between devices by JAX's collectives and lax.ppermute only.
A program may use at most 192 MiB of HBM per device.

v0:
```python
import math

import jax
import jax.numpy as jnp
from jax import lax
from jax.sharding import PartitionSpec as P

HEADS = 8


def passed_along(value, axis, steps):
    count = lax.axis_size(axis)
    initial, last = (max(0, -steps), min(count, count - steps))
    return lax.ppermute(value, axis, [(source, source + steps) for source in range(initial, last)])


def by_heads(block, heads):
    return block.reshape(block.shape[0], heads, block.shape[1] // heads)


def scores_for(queries, keys, score_scale):
    return (
        jnp.einsum("qhd,khd->hqk", queries, keys, preferred_element_type=jnp.float32) * score_scale
    )


def contract_rows(left, right):
    return lax.dot_general(
        left, right, (((0,), (0,)), ((), ())), preferred_element_type=jnp.float32
    )


def times_transpose(left, right):
    return lax.dot_general(
        left, right, (((1,), (1,)), ((), ())), preferred_element_type=jnp.float32
    )


def backward_terms(queries, keys, values, out_grads, log_totals, row_deltas, allowed, score_scale):
    scores = jnp.where(allowed, scores_for(queries, keys, score_scale), -jnp.inf)
    weights = jnp.exp(scores - log_totals[:, :, None])
    weight_grads = jnp.einsum("qhd,khd->hqk", out_grads, values, preferred_element_type=jnp.float32)
    score_grads = (weights * (weight_grads - row_deltas[:, :, None])).astype(jnp.bfloat16)
    return (weights.astype(jnp.bfloat16), score_grads)


def far_terms(weights, score_grads, queries, out_grads, distance, heads):
    key_part = jnp.einsum(
        "hqk,qhd->khd", score_grads, by_heads(queries, heads), preferred_element_type=jnp.float32
    )
    value_part = jnp.einsum(
        "hqk,qhd->khd", weights, by_heads(out_grads, heads), preferred_element_type=jnp.float32
    )
    key_gain, value_gain = (
        passed_along(key_part.astype(jnp.bfloat16), "ctx", -distance).astype(key_part.dtype),
        passed_along(value_part.astype(jnp.bfloat16), "ctx", -distance).astype(value_part.dtype),
    )
    return (key_gain, value_gain)


def body(series, w_query, w_key, w_value, w_out, cotangent):
    inputs = series[0]
    upstream = cotangent[0]
    length = inputs.shape[0]
    width = inputs.shape[1]
    heads = HEADS
    head_size = width // heads
    score_scale = 1.0 / math.sqrt(head_size)
    queries = jnp.dot(inputs, w_query, preferred_element_type=jnp.float32).astype(jnp.bfloat16)
    keys = jnp.dot(inputs, w_key, preferred_element_type=jnp.float32).astype(jnp.bfloat16)
    values = jnp.dot(inputs, w_value, preferred_element_type=jnp.float32).astype(jnp.bfloat16)
    position = lax.axis_index("ctx")
    extent = lax.axis_size("ctx")
    query_heads = by_heads(queries, heads)
    causal = lax.broadcasted_iota(jnp.int32, (1, length, length), 1) >= lax.broadcasted_iota(
        jnp.int32, (1, length, length), 2
    )
    blocks = [(by_heads(keys, heads), by_heads(values, heads), causal, 0)]
    distance = 1
    while distance < extent:
        far_keys, far_values = passed_along((keys, values), "ctx", distance)
        blocks.append(
            (by_heads(far_keys, heads), by_heads(far_values, heads), position >= distance, distance)
        )
        distance = distance * 2
    log_totals = None
    for key_heads, value_heads, allowed, distance in blocks:
        scores = jnp.where(allowed, scores_for(query_heads, key_heads, score_scale), -jnp.inf)
        largest = jnp.max(scores, axis=2)
        anchor = jnp.where(largest > -jnp.inf, largest, 0.0)
        partial_log = anchor + jnp.log(jnp.sum(jnp.exp(scores - anchor[:, :, None]), axis=2))
        log_totals = partial_log if log_totals is None else jnp.logaddexp(log_totals, partial_log)
    mixed = jnp.zeros((length, heads, head_size), jnp.float32)
    for key_heads, value_heads, allowed, distance in blocks:
        scores = jnp.where(allowed, scores_for(query_heads, key_heads, score_scale), -jnp.inf)
        weights = jnp.exp(scores - log_totals[:, :, None]).astype(jnp.bfloat16)
        mixed = mixed + jnp.einsum(
            "hqk,khd->qhd", weights, value_heads, preferred_element_type=jnp.float32
        )
    attended = mixed.reshape(length, width).astype(jnp.bfloat16)
    output = jnp.dot(attended, w_out, preferred_element_type=jnp.float32).astype(jnp.bfloat16)
    out_grads = times_transpose(upstream, w_out).astype(jnp.bfloat16)
    products = out_grads.astype(jnp.float32) * attended.astype(jnp.float32)
    row_deltas = jnp.sum(products.reshape(length, heads, head_size), axis=2).T
    grad_heads = by_heads(out_grads, heads)
    query_total = jnp.zeros((length, heads, head_size), jnp.float32)
    key_total = jnp.zeros((length, heads, head_size), jnp.float32)
    value_total = jnp.zeros((length, heads, head_size), jnp.float32)
    for key_heads, value_heads, allowed, distance in blocks:
        weights, score_grads = backward_terms(
            query_heads,
            key_heads,
            value_heads,
            grad_heads,
            log_totals,
            row_deltas,
            allowed,
            score_scale,
        )
        query_total = query_total + jnp.einsum(
            "hqk,khd->qhd", score_grads, key_heads, preferred_element_type=jnp.float32
        )
        if distance == 0:
            key_total = jnp.einsum(
                "hqk,qhd->khd", score_grads, query_heads, preferred_element_type=jnp.float32
            )
            value_total = jnp.einsum(
                "hqk,qhd->khd", weights, grad_heads, preferred_element_type=jnp.float32
            )
        else:
            key_gain, value_gain = far_terms(
                weights, score_grads, queries, out_grads, distance, heads
            )
            key_total = key_total + key_gain
            value_total = value_total + value_gain
    query_grad = (query_total * score_scale).reshape(length, width).astype(jnp.bfloat16)
    key_grad = (key_total * score_scale).reshape(length, width).astype(jnp.bfloat16)
    value_grad = value_total.reshape(length, width).astype(jnp.bfloat16)
    input_grad = (
        times_transpose(query_grad, w_query)
        + times_transpose(key_grad, w_key)
        + times_transpose(value_grad, w_value)
    ).astype(jnp.bfloat16)
    grad_query, grad_key, grad_value, grad_out = (
        lax.psum_scatter(
            contract_rows(inputs, query_grad), ("dp", "ctx"), scatter_dimension=1, tiled=True
        ),
        lax.psum_scatter(
            contract_rows(inputs, key_grad), ("dp", "ctx"), scatter_dimension=1, tiled=True
        ),
        lax.psum_scatter(
            contract_rows(inputs, value_grad), ("dp", "ctx"), scatter_dimension=1, tiled=True
        ),
        lax.psum_scatter(
            contract_rows(attended, upstream), ("dp", "ctx"), scatter_dimension=1, tiled=True
        ),
    )
    return (output[None], input_grad[None], grad_query, grad_key, grad_value, grad_out)


def solution(mesh):
    return jax.shard_map(
        body,
        mesh=mesh,
        in_specs=(P("dp", "ctx", None), P(), P(), P(), P(), P("dp", "ctx", None)),
        out_specs=(
            P("dp", "ctx", None),
            P("dp", "ctx", None),
            P(None, ("dp", "ctx")),
            P(None, ("dp", "ctx")),
            P(None, ("dp", "ctx")),
            P(None, ("dp", "ctx")),
        ),
        check_vma=False,
    )
```

profile of v0, /device:TPU:0, one launch (start us, length us, event | category | flops | bytes accessed | tf_op | source)
XLA Modules:
  0.0 559.8 jit_solution(3014465553364868531)
XLA Ops:
  10.5 4.7 collective-permute-start.9
  15.3 5.7 %collective-permute-start.8 = (bf16[512,512]{0,1:T(8,128)(2,1)}, bf16[512,512]{0,1:T(8,128)(2,1)}, u32[]{:S(2)}, u32[]{:S(2)}) collective-permute-start(bf16[512,512]{0,1:T(8,128)(2,1)} %convolution_convert_fusion.14), channel_id=1, source_target_pairs={{0,8},{1,9},{2,10},{3,11},{4,12},{5,13},{6,14},{7,15},{8,16},{9,17... | collective-permute-start | bytes 1572872 | tf_op jit(solution)/shard_map/ppermute | solution.py:14
  25.8 5.1 collective-permute-start.1
  39.9 12.6 %collective-permute-done = bf16[512,512]{0,1:T(8,128)(2,1)S(1)} collective-permute-done((bf16[512,512]{0,1:T(8,128)(2,1)S(1)}, bf16[512,512]{0,1:T(8,128)(2,1)S(1)}, u32[]{:S(2)}, u32[]{:S(2)}) %collective-permute-start) | collective-permute-done | bytes 524320 | tf_op jit(solution)/shard_map/ppermute | solution.py:14
  52.5 21.0 %collective-permute-start.3 = (bf16[512,512]{0,1:T(8,128)(2,1)S(1)}, bf16[512,512]{0,1:T(8,128)(2,1)S(1)}, u32[]{:S(2)}, u32[]{:S(2)}) collective-permute-start(bf16[512,512]{0,1:T(8,128)(2,1)S(1)} %convolution_convert_fusion.12), channel_id=1, source_target_pairs={{0,8},{1,9},{2,10},{3,11},{4,12},{5,13},{6,14},{7,15},{8,16},{9,17... | collective-permute-start | bytes 1572872 | tf_op jit(solution)/shard_map/ppermute | solution.py:14
  77.5 18.6 %collective-permute-done.2 = bf16[512,512]{0,1:T(8,128)(2,1)S(1)} collective-permute-done((bf16[512,512]{0,1:T(8,128)(2,1)S(1)}, bf16[512,512]{0,1:T(8,128)(2,1)S(1)}, u32[]{:S(2)}, u32[]{:S(2)}) %collective-permute-start.2) | collective-permute-done | bytes 524320 | tf_op jit(solution)/shard_map/ppermute | solution.py:14
  102.0 5.7 %collective-permute-start.4 = (bf16[512,512]{0,1:T(8,128)(2,1)S(1)}, bf16[512,512]{0,1:T(8,128)(2,1)S(1)}, u32[]{:S(2)}, u32[]{:S(2)}) collective-permute-start(bf16[512,512]{0,1:T(8,128)(2,1)S(1)} %convolution_convert_fusion.12), channel_id=1, source_target_pairs={{0,16},{1,17},{2,18},{3,19},{4,20},{5,21},{6,22},{7,23},{8,24},{9,... | collective-permute-start | bytes 1572872 | tf_op jit(solution)/shard_map/ppermute | solution.py:14
  112.2 16.2 %collective-permute-done.4 = bf16[512,512]{0,1:T(8,128)(2,1)S(1)} collective-permute-done((bf16[512,512]{0,1:T(8,128)(2,1)S(1)}, bf16[512,512]{0,1:T(8,128)(2,1)S(1)}, u32[]{:S(2)}, u32[]{:S(2)}) %collective-permute-start.4) | collective-permute-done | bytes 524320 | tf_op jit(solution)/shard_map/ppermute | solution.py:14
  134.5 5.8 %exponential_reduce_fusion.2 = (f32[8,512]{1,0:T(8,128)S(1)}, f32[8,512]{1,0:T(8,128)S(1)}) fusion(f32[8,512,512]{1,2,0:T(8,128)} %get-tuple-element.15, f32[8,512]{1,0:T(8,128)S(1)} %compare_select_fusion.2, pred[]{:T(512)S(6)} %ge.26, f32[8,512]{1,0:T(8,128)S(1)} %compare_select_fusion.3, f32[8,512,512]{1,2,0:T(8,128)S(1)} %get-tuple-element.17, pred[]{:T(512)S(6)} %ge.25), kind=kLoop, calls=%fused_computation.16 | loop fusion | flops 16769024 | bytes 16842754 | tf_op jit(solution)/shard_map/reduce_sum | solution.py:91
  140.3 7.7 %exponential_reduce_fusion = (f32[8,512]{1,0:T(8,128)S(1)}, f32[8,512]{1,0:T(8,128)S(1)}) fusion(f32[8,512,512]{1,2,0:T(8,128)} %get-tuple-element.11, f32[8,512]{1,0:T(8,128)S(1)} %compare_select_fusion, pred[]{:T(512)S(6)} %ge.28, f32[8,512]{1,0:T(8,128)S(1)} %compare_select_fusion.1, f32[8,512,512]{1,2,0:T(8,128)} %get-tuple-element.13, pred[]{:T(512)S(6)} %ge.27), kind=kLoop, calls=%fused_computation.12 | loop fusion | flops 16769024 | bytes 16842754 | tf_op jit(solution)/shard_map/reduce_sum | solution.py:91
  157.1 5.5 fusion.50
  162.6 6.5 %fusion.47 = f32[8,64,512]{2,1,0:T(8,128)} fusion(bf16[512,8,64]{0,2,1:T(8,128)(2,1)} %bitcast.12, f32[8,512,512]{1,2,0:T(8,128)} %get-tuple-element.13, f32[8,512]{1,0:T(8,128)S(1)} %add_select_fusion, pred[]{:T(512)S(6)} %ge.27), kind=kOutput, calls=%fused_computation.99 | convolution fusion | flops 276824064 | bytes 9977857 | tf_op jit(solution)/shard_map/hqk,khd->qhd/dot_general | solution.py:97
  178.1 6.2 %fusion.33 = bf16[512,8,64]{0,2,1:T(8,128)(2,1)} fusion(bf16[512,8,64]{0,2,1:T(8,128)(2,1)S(1)} %bitcast.198, f32[8,512,512]{1,2,0:T(8,128)} %get-tuple-element.11, f32[8,512]{1,0:T(8,128)S(1)} %add_select_fusion, pred[]{:T(512)S(6)} %ge.28), kind=kOutput, calls=%fused_computation.83 | convolution fusion | flops 277086208 | bytes 9453569 | tf_op jit(solution)/shard_map/hqk,qhd->khd/dot_general | solution.py:51
  184.3 6.7 %multiply_convert_fusion = bf16[8,512,512]{1,2,0:T(8,128)(2,1)} fusion(f32[8,512,512]{1,2,0:T(8,128)} %get-tuple-element.11, f32[8,512]{1,0:T(8,128)S(1)} %bitcast.210, f32[8,512]{1,0:T(8,128)S(1)} %add_select_fusion, pred[]{:T(512)S(6)} %ge.28, bf16[512,8,64]{0,2,1:T(8,128)(2,1)S(1)} %bitcast.199, bf16[512,8,64]{0,2,1:T(8,128)(2,1)} %bitcast.13), kind=kOutput, calls=%fused_computation | convolution fusion | flops 281018368 | bytes 13664257 | tf_op jit(solution)/shard_map/qhd,khd->hqk/dot_general | solution.py:42
  198.4 6.0 %fusion.32 = bf16[512,8,64]{0,2,1:T(8,128)(2,1)} fusion(bf16[512,8,64]{0,2,1:T(8,128)(2,1)S(1)} %bitcast.200, f32[8,512,512]{1,2,0:T(8,128)} %get-tuple-element.13, f32[8,512]{1,0:T(8,128)S(1)} %add_select_fusion, pred[]{:T(512)S(6)} %ge.27), kind=kOutput, calls=%fused_computation.82 | convolution fusion | flops 277086208 | bytes 9453569 | tf_op jit(solution)/shard_map/hqk,qhd->khd/dot_general | solution.py:51
  204.4 6.3 %multiply_convert_fusion.1 = bf16[8,512,512]{1,2,0:T(8,128)(2,1)} fusion(f32[8,512,512]{1,2,0:T(8,128)} %get-tuple-element.13, f32[8,512]{1,0:T(8,128)S(1)} %bitcast.211, f32[8,512]{1,0:T(8,128)S(1)} %add_select_fusion, pred[]{:T(512)S(6)} %ge.27, bf16[512,8,64]{0,2,1:T(8,128)(2,1)S(1)} %bitcast.201, bf16[512,8,64]{0,2,1:T(8,128)(2,1)} %bitcast.12), kind=kOutput, calls=%fused_computation.1 | convolution fusion | flops 281018368 | bytes 13664257 | tf_op jit(solution)/shard_map/qhd,khd->hqk/dot_general | solution.py:42
  218.2 6.0 %fusion.31 = bf16[512,8,64]{0,2,1:T(8,128)(2,1)} fusion(bf16[512,8,64]{0,2,1:T(8,128)(2,1)S(1)} %bitcast.204, f32[8,512,512]{1,2,0:T(8,128)} %get-tuple-element.15, f32[8,512]{1,0:T(8,128)S(1)} %add_select_fusion, pred[]{:T(512)S(6)} %ge.26), kind=kOutput, calls=%fused_computation.81 | convolution fusion | flops 277086208 | bytes 9453569 | tf_op jit(solution)/shard_map/hqk,qhd->khd/dot_general | solution.py:51
  224.3 6.3 %multiply_convert_fusion.2 = bf16[8,512,512]{1,2,0:T(8,128)(2,1)} fusion(f32[8,512,512]{1,2,0:T(8,128)} %get-tuple-element.15, f32[8,512]{1,0:T(8,128)S(1)} %bitcast.212, f32[8,512]{1,0:T(8,128)S(1)} %add_select_fusion, pred[]{:T(512)S(6)} %ge.26, bf16[512,8,64]{0,2,1:T(8,128)(2,1)S(1)} %bitcast.205, bf16[512,8,64]{0,2,1:T(8,128)(2,1)} %bitcast.11), kind=kOutput, calls=%fused_computation.2 | convolution fusion | flops 281018368 | bytes 13664257 | tf_op jit(solution)/shard_map/qhd,khd->hqk/dot_general | solution.py:42
  240.7 5.1 multiply_convert_fusion.3
  272.0 10.6 %collective-permute-done.15 = bf16[512,8,64]{0,2,1:T(8,128)(2,1)S(1)} collective-permute-done((bf16[512,8,64]{0,2,1:T(8,128)(2,1)S(1)}, bf16[512,8,64]{0,2,1:T(8,128)(2,1)S(1)}, u32[]{:S(2)}, u32[]{:S(2)}) %collective-permute-start.15) | collective-permute-done | bytes 524320 | tf_op jit(solution)/shard_map/ppermute | solution.py:14
  285.1 11.1 %collective-permute-done.17 = bf16[512,8,64]{0,2,1:T(8,128)(2,1)S(1)} collective-permute-done((bf16[512,8,64]{0,2,1:T(8,128)(2,1)S(1)}, bf16[512,8,64]{0,2,1:T(8,128)(2,1)S(1)}, u32[]{:S(2)}, u32[]{:S(2)}) %collective-permute-start.17) | collective-permute-done | bytes 524320 | tf_op jit(solution)/shard_map/ppermute | solution.py:14
  307.6 22.8 %collective-permute-done.12 = bf16[512,8,64]{0,2,1:T(8,128)(2,1)S(1)} collective-permute-done((bf16[512,8,64]{0,2,1:T(8,128)(2,1)S(1)}, bf16[512,8,64]{0,2,1:T(8,128)(2,1)S(1)}, u32[]{:S(2)}, u32[]{:S(2)}) %collective-permute-start.12) | collective-permute-done | bytes 524320 | tf_op jit(solution)/shard_map/ppermute | solution.py:14
  330.4 17.0 %collective-permute-done.14 = bf16[512,8,64]{0,2,1:T(8,128)(2,1)S(1)} collective-permute-done((bf16[512,8,64]{0,2,1:T(8,128)(2,1)S(1)}, bf16[512,8,64]{0,2,1:T(8,128)(2,1)S(1)}, u32[]{:S(2)}, u32[]{:S(2)}) %collective-permute-start.14) | collective-permute-done | bytes 524320 | tf_op jit(solution)/shard_map/ppermute | solution.py:14
  357.2 190.3 %all-reduce.7.cloned.1.call-done = (f32[512,512]{0,1:T(8,128)}, f32[512,512]{0,1:T(8,128)}, f32[512,512]{0,1:T(8,128)}, f32[512,512]{0,1:T(8,128)}) async-done(((f32[512,512]{0,1:T(8,128)}, f32[512,512]{0,1:T(8,128)}, f32[512,512]{0,1:T(8,128)}, f32[512,512]{0,1:T(8,128)}), (f32[512,512]{0,1:T(8,128)}, f32[512,512]{0,1:T(8,128)}, f32[512,512]{0,1:T(8,128)}, ...) | async-done | bytes 4194320
  (146 shorter events, 135.3 us)
Async XLA Ops:
  7.2 540.3 %all-reduce.7.cloned.1.call-start = ((), (), s32[]{:S(2)}) async-start(), calls=%async_computation | async-start | bytes 8388608
  10.5 158.5 %collective-permute-start.9 = (bf16[512,512]{0,1:T(8,128)(2,1)}, bf16[512,512]{0,1:T(8,128)(2,1)}, u32[]{:S(2)}, u32[]{:S(2)}) collective-permute-start(bf16[512,512]{0,1:T(8,128)(2,1)} %convolution_convert_fusion.14), channel_id=1, source_target_pairs={{0,16},{1,17},{2,18},{3,19},{4,20},{5,21},{6,22},{7,23},{8,24},{9,... | collective-permute-start | bytes 1572872 | tf_op jit(solution)/shard_map/ppermute | solution.py:14
  15.3 147.3 %collective-permute-start.8 = (bf16[512,512]{0,1:T(8,128)(2,1)}, bf16[512,512]{0,1:T(8,128)(2,1)}, u32[]{:S(2)}, u32[]{:S(2)}) collective-permute-start(bf16[512,512]{0,1:T(8,128)(2,1)} %convolution_convert_fusion.14), channel_id=1, source_target_pairs={{0,8},{1,9},{2,10},{3,11},{4,12},{5,13},{6,14},{7,15},{8,16},{9,17... | collective-permute-start | bytes 1572872 | tf_op jit(solution)/shard_map/ppermute | solution.py:14
  21.0 136.0 %collective-permute-start.7 = (bf16[512,512]{0,1:T(8,128)(2,1)}, bf16[512,512]{0,1:T(8,128)(2,1)}, u32[]{:S(2)}, u32[]{:S(2)}) collective-permute-start(bf16[512,512]{0,1:T(8,128)(2,1)} %convolution_convert_fusion.14), channel_id=1, source_target_pairs={{0,4},{1,5},{2,6},{3,7},{4,8},{5,9},{6,10},{7,11},{8,12},{9,13},{1... | collective-permute-start | bytes 1572872 | tf_op jit(solution)/shard_map/ppermute | solution.py:14
  25.8 49.0 %collective-permute-start.1 = (bf16[512,512]{0,1:T(8,128)(2,1)S(1)}, bf16[512,512]{0,1:T(8,128)(2,1)S(1)}, u32[]{:S(2)}, u32[]{:S(2)}) collective-permute-start(bf16[512,512]{0,1:T(8,128)(2,1)S(1)} %convolution_convert_fusion.12), channel_id=1, source_target_pairs={{0,2},{1,3},{2,4},{3,5},{4,6},{5,7},{6,8},{7,9},{8,10},{9,11},{10,... | collective-permute-start | bytes 1572872 | tf_op jit(solution)/shard_map/ppermute | solution.py:14
  31.0 21.6 %collective-permute-start = (bf16[512,512]{0,1:T(8,128)(2,1)S(1)}, bf16[512,512]{0,1:T(8,128)(2,1)S(1)}, u32[]{:S(2)}, u32[]{:S(2)}) collective-permute-start(bf16[512,512]{0,1:T(8,128)(2,1)S(1)} %convolution_convert_fusion.12), channel_id=1, source_target_pairs={{0,1},{1,2},{2,3},{3,4},{4,5},{5,6},{6,7},{7,8},{8,9},{9,10},{10,1... | collective-permute-start | bytes 1572872 | tf_op jit(solution)/shard_map/ppermute | solution.py:14
  52.5 49.5 %collective-permute-start.3 = (bf16[512,512]{0,1:T(8,128)(2,1)S(1)}, bf16[512,512]{0,1:T(8,128)(2,1)S(1)}, u32[]{:S(2)}, u32[]{:S(2)}) collective-permute-start(bf16[512,512]{0,1:T(8,128)(2,1)S(1)} %convolution_convert_fusion.12), channel_id=1, source_target_pairs={{0,8},{1,9},{2,10},{3,11},{4,12},{5,13},{6,14},{7,15},{8,16},{9,17... | collective-permute-start | bytes 1572872 | tf_op jit(solution)/shard_map/ppermute | solution.py:14
  74.9 21.2 %collective-permute-start.2 = (bf16[512,512]{0,1:T(8,128)(2,1)S(1)}, bf16[512,512]{0,1:T(8,128)(2,1)S(1)}, u32[]{:S(2)}, u32[]{:S(2)}) collective-permute-start(bf16[512,512]{0,1:T(8,128)(2,1)S(1)} %convolution_convert_fusion.12), channel_id=1, source_target_pairs={{0,4},{1,5},{2,6},{3,7},{4,8},{5,9},{6,10},{7,11},{8,12},{9,13},{1... | collective-permute-start | bytes 1572872 | tf_op jit(solution)/shard_map/ppermute | solution.py:14
  96.1 77.0 %collective-permute-start.6 = (bf16[512,512]{0,1:T(8,128)(2,1)}, bf16[512,512]{0,1:T(8,128)(2,1)S(1)}, u32[]{:S(2)}, u32[]{:S(2)}) collective-permute-start(bf16[512,512]{0,1:T(8,128)(2,1)} %convolution_convert_fusion.14), channel_id=1, source_target_pairs={{0,2},{1,3},{2,4},{3,5},{4,6},{5,7},{6,8},{7,9},{8,10},{9,11},{10,... | collective-permute-start | bytes 1572872 | tf_op jit(solution)/shard_map/ppermute | solution.py:14
  102.0 26.5 %collective-permute-start.4 = (bf16[512,512]{0,1:T(8,128)(2,1)S(1)}, bf16[512,512]{0,1:T(8,128)(2,1)S(1)}, u32[]{:S(2)}, u32[]{:S(2)}) collective-permute-start(bf16[512,512]{0,1:T(8,128)(2,1)S(1)} %convolution_convert_fusion.12), channel_id=1, source_target_pairs={{0,16},{1,17},{2,18},{3,19},{4,20},{5,21},{6,22},{7,23},{8,24},{9,... | collective-permute-start | bytes 1572872 | tf_op jit(solution)/shard_map/ppermute | solution.py:14
  128.4 26.4 %collective-permute-start.5 = (bf16[512,512]{0,1:T(8,128)(2,1)}, bf16[512,512]{0,1:T(8,128)(2,1)S(1)}, u32[]{:S(2)}, u32[]{:S(2)}) collective-permute-start(bf16[512,512]{0,1:T(8,128)(2,1)} %convolution_convert_fusion.14), channel_id=1, source_target_pairs={{0,1},{1,2},{2,3},{3,4},{4,5},{5,6},{6,7},{7,8},{8,9},{9,10},{10,1... | collective-permute-start | bytes 1572872 | tf_op jit(solution)/shard_map/ppermute | solution.py:14
  260.0 22.6 %collective-permute-start.15 = (bf16[512,8,64]{0,2,1:T(8,128)(2,1)S(1)}, bf16[512,8,64]{0,2,1:T(8,128)(2,1)S(1)}, u32[]{:S(2)}, u32[]{:S(2)}) collective-permute-start(bf16[512,8,64]{0,2,1:T(8,128)(2,1)S(1)} %fusion.29), channel_id=1, source_target_pairs={{1,0},{2,1},{3,2},{4,3},{5,4},{6,5},{7,6},{8,7},{9,8},{10,9},{11,1... | collective-permute-start | bytes 1572872 | tf_op jit(solution)/shard_map/ppermute | solution.py:14
  261.3 22.6 %collective-permute-start.16 = (bf16[512,8,64]{0,2,1:T(8,128)(2,1)S(1)}, bf16[512,8,64]{0,2,1:T(8,128)(2,1)S(1)}, u32[]{:S(2)}, u32[]{:S(2)}) collective-permute-start(bf16[512,8,64]{0,2,1:T(8,128)(2,1)S(1)} %copy-done.21), channel_id=1, source_target_pairs={{2,0},{3,1},{4,2},{5,3},{6,4},{7,5},{8,6},{9,7},{10,8},{11,9},{12,... | collective-permute-start | bytes 1572872 | tf_op jit(solution)/shard_map/ppermute | solution.py:14
  262.6 33.7 %collective-permute-start.17 = (bf16[512,8,64]{0,2,1:T(8,128)(2,1)S(1)}, bf16[512,8,64]{0,2,1:T(8,128)(2,1)S(1)}, u32[]{:S(2)}, u32[]{:S(2)}) collective-permute-start(bf16[512,8,64]{0,2,1:T(8,128)(2,1)S(1)} %copy-done.20), channel_id=1, source_target_pairs={{4,0},{5,1},{6,2},{7,3},{8,4},{9,5},{10,6},{11,7},{12,8},{13,9},{1... | collective-permute-start | bytes 1572872 | tf_op jit(solution)/shard_map/ppermute | solution.py:14
  263.9 33.7 %collective-permute-start.18 = (bf16[512,8,64]{0,2,1:T(8,128)(2,1)S(1)}, bf16[512,8,64]{0,2,1:T(8,128)(2,1)S(1)}, u32[]{:S(2)}, u32[]{:S(2)}) collective-permute-start(bf16[512,8,64]{0,2,1:T(8,128)(2,1)S(1)} %copy-done.19), channel_id=1, source_target_pairs={{8,0},{9,1},{10,2},{11,3},{12,4},{13,5},{14,6},{15,7},{16,8},{17,9... | collective-permute-start | bytes 1572872 | tf_op jit(solution)/shard_map/ppermute | solution.py:14
  265.2 33.7 %collective-permute-start.19 = (bf16[512,8,64]{0,2,1:T(8,128)(2,1)S(1)}, bf16[512,8,64]{0,2,1:T(8,128)(2,1)S(1)}, u32[]{:S(2)}, u32[]{:S(2)}) collective-permute-start(bf16[512,8,64]{0,2,1:T(8,128)(2,1)S(1)} %copy-done.16), channel_id=1, source_target_pairs={{16,0},{17,1},{18,2},{19,3},{20,4},{21,5},{22,6},{23,7},{24,8},{25... | collective-permute-start | bytes 1572872 | tf_op jit(solution)/shard_map/ppermute | solution.py:14
  268.2 32.2 %copy-start.26 = (bf16[512,512]{0,1:T(8,128)(2,1)S(1)}, bf16[512,512]{0,1:T(8,128)(2,1)}, u32[]{:S(2)}) copy-start(bf16[512,512]{0,1:T(8,128)(2,1)} %copy-done.22) | copy-start | bytes 1572868
  282.6 25.1 %collective-permute-start.10 = (bf16[512,8,64]{0,2,1:T(8,128)(2,1)S(1)}, bf16[512,8,64]{0,2,1:T(8,128)(2,1)S(1)}, u32[]{:S(2)}, u32[]{:S(2)}) collective-permute-start(bf16[512,8,64]{0,2,1:T(8,128)(2,1)S(1)} %fusion.24), channel_id=1, source_target_pairs={{1,0},{2,1},{3,2},{4,3},{5,4},{6,5},{7,6},{8,7},{9,8},{10,9},{11,1... | collective-permute-start | bytes 1572872 | tf_op jit(solution)/shard_map/ppermute | solution.py:14
  283.8 23.8 %collective-permute-start.11 = (bf16[512,8,64]{0,2,1:T(8,128)(2,1)S(1)}, bf16[512,8,64]{0,2,1:T(8,128)(2,1)S(1)}, u32[]{:S(2)}, u32[]{:S(2)}) collective-permute-start(bf16[512,8,64]{0,2,1:T(8,128)(2,1)S(1)} %fusion.25), channel_id=1, source_target_pairs={{2,0},{3,1},{4,2},{5,3},{6,4},{7,5},{8,6},{9,7},{10,8},{11,9},{12,... | collective-permute-start | bytes 1572872 | tf_op jit(solution)/shard_map/ppermute | solution.py:14
  296.3 34.1 %collective-permute-start.12 = (bf16[512,8,64]{0,2,1:T(8,128)(2,1)S(1)}, bf16[512,8,64]{0,2,1:T(8,128)(2,1)S(1)}, u32[]{:S(2)}, u32[]{:S(2)}) collective-permute-start(bf16[512,8,64]{0,2,1:T(8,128)(2,1)S(1)} %copy-done.10), channel_id=1, source_target_pairs={{4,0},{5,1},{6,2},{7,3},{8,4},{9,5},{10,6},{11,7},{12,8},{13,9},{1... | collective-permute-start | bytes 1572872 | tf_op jit(solution)/shard_map/ppermute | solution.py:14
  297.6 32.8 %collective-permute-start.13 = (bf16[512,8,64]{0,2,1:T(8,128)(2,1)S(1)}, bf16[512,8,64]{0,2,1:T(8,128)(2,1)S(1)}, u32[]{:S(2)}, u32[]{:S(2)}) collective-permute-start(bf16[512,8,64]{0,2,1:T(8,128)(2,1)S(1)} %copy-done.9), channel_id=1, source_target_pairs={{8,0},{9,1},{10,2},{11,3},{12,4},{13,5},{14,6},{15,7},{16,8},{17,9... | collective-permute-start | bytes 1572872 | tf_op jit(solution)/shard_map/ppermute | solution.py:14
  298.9 48.5 %collective-permute-start.14 = (bf16[512,8,64]{0,2,1:T(8,128)(2,1)S(1)}, bf16[512,8,64]{0,2,1:T(8,128)(2,1)S(1)}, u32[]{:S(2)}, u32[]{:S(2)}) collective-permute-start(bf16[512,8,64]{0,2,1:T(8,128)(2,1)S(1)} %copy-done.8), channel_id=1, source_target_pairs={{16,0},{17,1},{18,2},{19,3},{20,4},{21,5},{22,6},{23,7},{24,8},{25... | collective-permute-start | bytes 1572872 | tf_op jit(solution)/shard_map/ppermute | solution.py:14
  303.0 45.9 %copy-start.5 = (bf16[512,8,64]{0,2,1:T(8,128)(2,1)}, bf16[512,8,64]{0,2,1:T(8,128)(2,1)S(1)}, u32[]{:S(2)}) copy-start(bf16[512,8,64]{0,2,1:T(8,128)(2,1)S(1)} %add_convert_fusion) | copy-start | bytes 1572868
  304.6 48.3 %copy-start.4 = (bf16[512,512]{1,0:T(8,128)(2,1)S(1)}, bf16[512,512]{1,0:T(8,128)(2,1)}, u32[]{:S(2)}) copy-start(bf16[512,512]{1,0:T(8,128)(2,1)} %param.7) | copy-start | bytes 1572868
  (28 other events, 277.7 us)
Sparse Core Ops, SparseCore 0:
  350.5 196.9 all-reduce.6
where the time goes:
time: 569 us; the launch traced here: 560 us
  waiting for transfers between devices  302 us (53%)
  matrix products  153 us (27%)
  starting transfers between devices  65.4 us (11%)
  other arithmetic  17.1 us (3%)
  between operations  15 us (3%)
  local copies, waits for them, and re-layouts  7.18 us (1%)
    unnamed x2, waiting for transfers between devices  190 us
    ppermute x20, waiting for transfers between devices, passed_along(): lax.ppermute(value, axis, [(source, source + steps) for source in range(i...  112 us
    ppermute x20, starting transfers between devices, passed_along(): lax.ppermute(value, axis, [(source, source + steps) for source in range(i...  65.4 us
    dot_general x6, matrix products, backward_terms(): jnp.einsum('qhd,khd->hqk', out_grads, values, preferred_element_type=jnp....  32.6 us
    dot_general x6, matrix products, body(): jnp.einsum('hqk,khd->qhd', weights, value_heads, preferred_element_type=j...  25.1 us
    dot_general x5, matrix products, far_terms(): jnp.einsum('hqk,qhd->khd', weights, by_heads(out_grads, heads), preferred...  23.9 us
    dot_general x6, matrix products, scores_for(): jnp.einsum('qhd,khd->hqk', queries, keys, preferred_element_type=jnp.floa...  21 us
    reduce_sum x3, other arithmetic, body(): jnp.sum(jnp.exp(scores - anchor[:, :, None]), axis=2)  16.9 us
  transfers between devices with their start and end apart: 21, of which 9 were waited for; matrix products, arithmetic and copies ran while one was open for 14% of the time, Pallas kernels for 0%

commit v1 on v0

v1 whole, which is shorter than its diff:
```python
import functools

import jax
import jax.numpy as jnp
from jax import lax
from jax.experimental import pallas as pl
from jax.experimental.pallas import tpu as pltpu
from jax.sharding import PartitionSpec as P

HEADS = 8
SIZE = 64
F32 = jnp.float32
BF16 = jnp.bfloat16
LOW = -3.0e38
CHUNK = 256
MIB = 2**20


def dot(left, right, left_dim, right_dim):
    return lax.dot_general(
        left, right, (((left_dim,), (right_dim,)), ((), ())), preferred_element_type=F32
    )


def whole(shape):
    return pl.BlockSpec(shape, lambda *_: (0,) * len(shape))


def head_rows(width):
    return pl.BlockSpec((SIZE, width), lambda h: (h, 0))


def head_stat(width):
    return pl.BlockSpec((1, 1, width), lambda h: (h, 0, 0))


SCALAR = pl.BlockSpec(memory_space=pltpu.SMEM)


def params(mib=16):
    return pltpu.CompilerParams(vmem_limit_bytes=mib * MIB)


def cost(matmuls, nbytes=0, exps=0):
    return pl.CostEstimate(
        flops=int(matmuls * 2**24), bytes_accessed=int(nbytes) // 8, transcendentals=0
    )


def project_kernel(x_ref, cot_ref, wq_ref, wo_ref, q_ref, do_ref):
    q_ref[...] = dot(wq_ref[...], x_ref[...], 1, 1).astype(BF16) * jnp.asarray(0.125, BF16)
    do_ref[...] = dot(wo_ref[...], cot_ref[...], 1, 1).astype(BF16)


def project(x, cot, wq_t, w_out):
    n, d = x.shape
    return pl.pallas_call(
        project_kernel,
        out_shape=(jax.ShapeDtypeStruct((d, n), BF16), jax.ShapeDtypeStruct((d, n), BF16)),
        compiler_params=params(),
        cost_estimate=cost(2 * 4),
        name="project",
    )(x, cot, wq_t, w_out)


def forward_kernel(own, seen_ref, x_ref, wk_ref, wv_ref, q_ref, p_ref, m_ref, l_ref, o_ref, k_ref, v_ref):
    head = pl.program_id(0)
    seen = seen_ref[0] > 0

    @pl.when(jnp.logical_and(seen, head == 0))
    def _():
        k_ref[...] = dot(wk_ref[...], x_ref[...], 1, 1).astype(BF16)
        v_ref[...] = dot(wv_ref[...], x_ref[...], 1, 1).astype(BF16)

    @pl.when(seen)
    def _():
        rows = pl.ds(pl.multiple_of(head * SIZE, SIZE), SIZE)
        keys = k_ref[rows, :]
        ones = jnp.ones((16, keys.shape[1]), BF16)
        values = jnp.concatenate([v_ref[rows, :], ones], axis=0)
        for start in range(0, q_ref.shape[1], CHUNK):
            cols = slice(start, start + CHUNK)
            known = min(start + CHUNK, keys.shape[1]) if own else keys.shape[1]
            scores = dot(keys[:, :known], q_ref[:, cols], 0, 0)
            if own:
                at_key = lax.broadcasted_iota(jnp.int32, scores.shape, 0)
                at_query = lax.broadcasted_iota(jnp.int32, scores.shape, 1) + start
                scores = jnp.where(at_key <= at_query, scores, LOW)
            largest = jnp.max(scores, axis=0, keepdims=True)
            weights = jnp.exp(scores - largest).astype(BF16)
            mixed = dot(values[:, :known], weights, 1, 0)
            p_ref[0, :known, cols] = weights
            if known < keys.shape[1]:
                p_ref[0, known:, cols] = jnp.zeros((keys.shape[1] - known, CHUNK), BF16)
            m_ref[0, :, cols] = largest
            l_ref[0, :, cols] = mixed[SIZE : SIZE + 1, :]
            o_ref[:, cols] = mixed[:SIZE, :]

    @pl.when(jnp.logical_not(seen))
    def _():
        m_ref[...] = jnp.full(m_ref.shape, LOW, F32)
        l_ref[...] = jnp.zeros(l_ref.shape, F32)
        o_ref[...] = jnp.zeros(o_ref.shape, F32)


def forward(own, seen, x, wk_t, wv_t, q_t):
    n, d = x.shape
    return pl.pallas_call(
        functools.partial(forward_kernel, own),
        grid=(HEADS,),
        out_shape=(
            jax.ShapeDtypeStruct((HEADS, n, n), BF16),
            jax.ShapeDtypeStruct((HEADS, 1, n), F32),
            jax.ShapeDtypeStruct((HEADS, 1, n), F32),
            jax.ShapeDtypeStruct((d, n), F32),
            jax.ShapeDtypeStruct((d, n), BF16),
            jax.ShapeDtypeStruct((d, n), BF16),
        ),
        in_specs=[SCALAR, whole((n, d)), whole((d, d)), whole((d, d)), head_rows(n)],
        out_specs=[
            pl.BlockSpec((1, n, n), lambda h: (h, 0, 0)),
            head_stat(n),
            head_stat(n),
            head_rows(n),
            whole((d, n)),
            whole((d, n)),
        ],
        compiler_params=params(),
        cost_estimate=cost(2 * 4 + 2, 7 * MIB, HEADS * n * n),
        name="forward_own" if own else "forward_far",
    )(seen, x, wk_t, wv_t, q_t)


def join_kernel(count, *refs):
    ms, ls, os = refs[:count], refs[count : 2 * count], refs[2 * count : 3 * count]
    do_ref, wo_ref, cot_ref = refs[3 * count : 3 * count + 3]
    att_ref, out_ref, delta_ref = refs[3 * count + 3 : 3 * count + 6]
    cs = refs[3 * count + 6 :]
    for head in range(HEADS):
        rows = slice(head * SIZE, (head + 1) * SIZE)
        largest = functools.reduce(jnp.maximum, [m[head] for m in ms])
        factors = [jnp.exp(m[head] - largest) for m in ms]
        total = functools.reduce(jnp.add, [f * l[head] for f, l in zip(factors, ls)])
        inverse = 1.0 / total
        mixed = None
        for f, o, c in zip(factors, os, cs):
            f = f * inverse
            c[head] = f
            term = o[rows, :] * f
            mixed = term if mixed is None else mixed + term
        attended = mixed.astype(BF16)
        att_ref[rows, :] = attended
        products = attended.astype(F32) * do_ref[rows, :].astype(F32)
        delta_ref[head] = jnp.sum(products, axis=0, keepdims=True)
    out_ref[...] = dot(att_ref[...], wo_ref[...], 0, 0).astype(BF16)


def join(stats, do_t, w_out, cot):
    d, n = do_t.shape
    count = len(stats)
    row = jax.ShapeDtypeStruct((HEADS, 1, n), F32)
    return pl.pallas_call(
        functools.partial(join_kernel, count),
        out_shape=(
            jax.ShapeDtypeStruct((d, n), BF16),
            jax.ShapeDtypeStruct((n, d), BF16),
            row,
        )
        + (row,) * count,
        compiler_params=params(),
        cost_estimate=cost(4, 8 * MIB),
        name="join",
    )(*[s[0] for s in stats], *[s[1] for s in stats], *[s[2] for s in stats], do_t, w_out, cot)


def backward_kernel(
    last, carried, seen_ref, p_ref, k_ref, v_ref, q_ref, do_ref, c_ref, delta_ref, wk_ref, wv_ref, wq_ref, acc_ref,
    *rest,
):
    carry_refs, rest = rest[:carried], rest[carried:]
    dq_ref, dk_ref, dv_ref, dx_ref, *scratch = rest
    head = pl.program_id(0)
    seen = seen_ref[0] > 0

    @pl.when(seen)
    def _():
        rows = pl.ds(pl.multiple_of(head * SIZE, SIZE), SIZE)
        keys = k_ref[...]
        values = v_ref[...]
        factor = c_ref[0]
        scaled_q = (q_ref[...].astype(F32) * factor).astype(BF16)
        scaled_do = (do_ref[...].astype(F32) * factor).astype(BF16)
        dk = jnp.zeros(keys.shape, F32)
        dv = jnp.zeros(keys.shape, F32)
        for start in range(0, q_ref.shape[1], CHUNK):
            cols = slice(start, start + CHUNK)
            weights = p_ref[0, :, cols]
            grads = dot(values, do_ref[:, cols], 0, 0) - delta_ref[0, :, cols]
            grads = weights * grads.astype(BF16)
            dq_ref[:, cols] = acc_ref[:, cols] + dot(keys, grads, 1, 0) * factor[:, cols]
            dk = dk + dot(scaled_q[:, cols], grads, 1, 1)
            dv = dv + dot(scaled_do[:, cols], weights, 1, 1)
        dk_ref[rows, :] = dk.astype(BF16)
        dv_ref[rows, :] = dv.astype(BF16)
        if last:
            (all_dq,) = scratch
            all_dq[rows, :] = (dq_ref[...] * 0.125).astype(BF16)

    @pl.when(jnp.logical_not(seen))
    def _():
        rows = pl.ds(pl.multiple_of(head * SIZE, SIZE), SIZE)
        dq_ref[...] = acc_ref[...]
        dk_ref[rows, :] = jnp.zeros(k_ref.shape, BF16)
        dv_ref[rows, :] = jnp.zeros(k_ref.shape, BF16)

    @pl.when(head == HEADS - 1)
    def _():
        total = dot(dk_ref[...], wk_ref[...], 0, 0) + dot(dv_ref[...], wv_ref[...], 0, 0)
        if last:
            (all_dq,) = scratch
            total = total + dot(all_dq[...], wq_ref[...], 0, 0)
        for place, carry_ref in enumerate(carry_refs):
            total = total + jnp.where(seen_ref[1 + place] > 0, carry_ref[...], 0).astype(F32)
        dx_ref[...] = total.astype(dx_ref.dtype)


def backward(last, seen, p, k, v, q_t, do_t, c, delta, wk_t, wv_t, wq_t, acc, *carry):
    d, n = q_t.shape
    return pl.pallas_call(
        functools.partial(backward_kernel, last, len(carry)),
        grid=(HEADS,),
        out_shape=(
            jax.ShapeDtypeStruct((d, n), F32),
            jax.ShapeDtypeStruct((d, n), BF16),
            jax.ShapeDtypeStruct((d, n), BF16),
            jax.ShapeDtypeStruct((n, d), F32 if last else BF16),
        ),
        in_specs=[
            SCALAR,
            pl.BlockSpec((1, n, n), lambda h: (h, 0, 0)),
            head_rows(n),
            head_rows(n),
            head_rows(n),
            head_rows(n),
            head_stat(n),
            head_stat(n),
            whole((d, d)),
            whole((d, d)),
            whole((d, d)),
            head_rows(n),
        ]
        + [whole((n, d))] * len(carry),
        out_specs=[head_rows(n), whole((d, n)), whole((d, n)), whole((n, d))],
        scratch_shapes=[pltpu.VMEM((d, n), BF16)] if last else [],
        compiler_params=params(),
        cost_estimate=cost(4 * 4 + 2, 10 * MIB),
        name="backward_own" if last else "backward_far",
    )(seen, p, k, v, q_t, do_t, c, delta, wk_t, wv_t, wq_t, acc, *carry)


def weights_kernel(count, *refs):
    xs, dks, dvs = refs[:count], refs[count : 2 * count], refs[2 * count : 3 * count]
    dq_ref, att_ref, cot_ref, g_ref, sums = refs[3 * count :]

    def keep(place, value):
        for owner in range(g_ref.shape[0]):
            sums[owner, 4 * place : 4 * place + 4, :] = value[4 * owner : 4 * owner + 4, :]

    keep(0, dot((dq_ref[...] * 0.125).astype(BF16), xs[0][...], 1, 0))
    for place, parts in ((1, dks), (2, dvs)):
        total = None
        for part, x in zip(parts, xs):
            term = dot(part[...], x[...], 1, 0)
            total = term if total is None else total + term
        keep(place, total)
    keep(3, dot(cot_ref[...], att_ref[...], 0, 1))
    g_ref[...] = sums[...].astype(BF16)


def weight_terms(xs, dks, dvs, dq, att_t, cot):
    n, d = cot.shape
    return pl.pallas_call(
        functools.partial(weights_kernel, len(xs)),
        out_shape=jax.ShapeDtypeStruct((128, 16, d), BF16),
        scratch_shapes=[pltpu.VMEM((128, 16, d), F32)],
        compiler_params=params(32),
        cost_estimate=cost(2 * len(xs) + 2, 12 * MIB),
        name="weight_terms",
    )(*xs, *dks, *dvs, dq, att_t, cot)


def place(z, x, y):
    return (z % 2) * 16 + (x % 4) * 4 + y % 4


def y_ring(value, step):
    pairs = [(place(z, x, y), place(z, x, y + step)) for z in range(2) for x in range(4) for y in range(4)]
    return lax.ppermute(value, "ctx", pairs)


def shifted(value, step):
    return lax.ppermute(
        value, "ctx", [(i, i + step) for i in range(max(0, -step), min(32, 32 - step))]
    )


def body(series, w_query, w_key, w_value, w_out, cotangent):
    x = series[0]
    cot = cotangent[0]
    n, d = x.shape
    position = lax.axis_index("ctx")
    y = position % 4
    x4, x8, x16 = shifted(x, 4), shifted(x, 8), shifted(x, 16)
    wq_t, wk_t, wv_t = w_query.T, w_key.T, w_value.T
    q_t, do_t = project(x, cot, wq_t, w_out)
    order = (0, 4, 16, 8, 1, 2)
    seen = {p: (position >= p).astype(jnp.int32).reshape(1) for p in order}
    held = {0: forward(True, seen[0], x, wk_t, wv_t, q_t)}
    x4, _ = lax.optimization_barrier((x4, held[0][1]))
    x1 = y_ring(jnp.where(y == 3, x4, x), 1)
    x2 = y_ring(jnp.where(y >= 2, x4, x), 2)
    blocks = {0: x, 1: x1, 2: x2, 4: x4, 8: x8, 16: x16}
    for p in order[1:]:
        held[p] = forward(False, seen[p], blocks[p], wk_t, wv_t, q_t)
    att_t, output, delta, *factors = join([held[p][1:4] for p in order], do_t, w_out, cot)
    factor = dict(zip(order, factors))
    dq = jnp.zeros((d, n), F32)
    dk, dv, dx = {}, {}, {}
    back = {}
    for p in (1, 2, 8, 16, 4, 0):
        weights, _, _, _, keys, values = held[p]
        flags, carry = seen[p], ()
        if p == 4:
            wraps = jnp.stack([y == 3, y >= 2]).astype(jnp.int32)
            flags, carry = jnp.concatenate([flags, wraps]), (back[1], back[2])
        dq, dk[p], dv[p], dx[p] = backward(
            p == 0, flags, weights, keys, values, q_t, do_t, factor[p], delta, wk_t, wv_t, wq_t, dq, *carry
        )
        if p in (1, 2):
            back[p] = y_ring(dx[p], -p)
        elif p:
            back[p] = shifted(dx[p], -p)
    terms = weight_terms(
        [blocks[p] for p in order], [dk[p] for p in order], [dv[p] for p in order], dq, att_t, cot
    )
    terms, back[4], back[8], back[16] = lax.optimization_barrier((terms, back[4], back[8], back[16]))
    terms = lax.all_to_all(terms, ("dp", "ctx"), 0, 0, tiled=True)
    grads = jnp.sum(terms.astype(F32), axis=0).reshape(4, 4, d).transpose(0, 2, 1)
    total = dx[0] + back[8].astype(F32) + back[16].astype(F32) + back[4].astype(F32)
    total = total + jnp.where(y < 3, back[1], 0).astype(F32) + jnp.where(y < 2, back[2], 0).astype(F32)
    input_grad = total.astype(BF16)
    return (output[None], input_grad[None], grads[0], grads[1], grads[2], grads[3])


def solution(mesh):
    return jax.shard_map(
        body,
        mesh=mesh,
        in_specs=(P("dp", "ctx", None), P(), P(), P(), P(), P("dp", "ctx", None)),
        out_specs=(
            P("dp", "ctx", None),
            P("dp", "ctx", None),
            P(None, ("dp", "ctx")),
            P(None, ("dp", "ctx")),
            P(None, ("dp", "ctx")),
            P(None, ("dp", "ctx")),
        ),
        check_vma=False,
    )
```

time: 569 us -> 201 us (0.35); the launches traced: 560 us -> 201 us
  waiting for transfers between devices: 302 us -> 58 us
  matrix products: 153 us -> 0 us
  Pallas kernels: 0 us -> 36.4 us
  starting transfers between devices: 65.4 us -> 86.8 us
  between operations: 15 us -> 0.98 us
  other arithmetic: 17.1 us -> 5.52 us
    unnamed x2 -> x0, waiting for transfers between devices: 190 us -> none
    dot_general x48 -> x0, matrix products: 153 us -> none  [the longest x6 32.6 us: backward_terms(): jnp.einsum('qhd,khd->hqk', out_grads, values, preferred_element_type=jnp....]
    ppermute x20 -> x10, waiting for transfers between devices: 112 us -> 31.1 us  [the longest x4 20 us: y_ring(): return lax.ppermute(value, 'ctx', pairs)]
    pallas_call x0 -> x15, Pallas kernels: none -> 36.4 us  [the longest x6 15.5 us: backward(): pl.pallas_call(functools.partial(backward_kernel, last, len(carry)), grid...]
    all_to_all x0 -> x1, starting transfers between devices: none -> 30.6 us  [body(): terms = lax.all_to_all(terms, ('dp', 'ctx'), 0, 0, tiled=True)]
    all_to_all x0 -> x1, waiting for transfers between devices: none -> 26.9 us  [body(): terms = lax.all_to_all(terms, ('dp', 'ctx'), 0, 0, tiled=True)]
    reduce_sum x3 -> x1, other arithmetic: 16.9 us -> 1.95 us  [body(): jnp.sum(terms.astype(F32), axis=0).reshape(4, 4, d).transpose(0, 2, 1)]
    ppermute x20 -> x10, starting transfers between devices: 65.4 us -> 56.2 us  [the longest x4 38.7 us: y_ring(): return lax.ppermute(value, 'ctx', pairs)]
  transfers between devices with their start and end apart: 21 -> 11, of which waited for: 9 -> 7; matrix products, arithmetic and copies ran while one was open for 14% -> 4% of each run, Pallas kernels for 0% -> 15%
where the time goes in v1:
time: 201 us
  starting transfers between devices  86.8 us (43%)
  waiting for transfers between devices  58 us (29%)
  Pallas kernels  36.4 us (18%)
  local copies, waits for them, and re-layouts  12.8 us (6%)
  other arithmetic  5.52 us (3%)
    ppermute x4, starting transfers between devices, y_ring(): return lax.ppermute(value, 'ctx', pairs)  38.7 us
    all_to_all x1, starting transfers between devices, body(): terms = lax.all_to_all(terms, ('dp', 'ctx'), 0, 0, tiled=True)  30.6 us
    all_to_all x1, waiting for transfers between devices, body(): terms = lax.all_to_all(terms, ('dp', 'ctx'), 0, 0, tiled=True)  26.9 us
    ppermute x4, waiting for transfers between devices, y_ring(): return lax.ppermute(value, 'ctx', pairs)  20 us
    ppermute x6, starting transfers between devices, shifted(): lax.ppermute(value, 'ctx', [(i, i + step) for i in range(max(0, -step), m...  17.5 us
    pallas_call x6, Pallas kernels, backward(): pl.pallas_call(functools.partial(backward_kernel, last, len(carry)), grid...  15.5 us
    unnamed x51, local copies, waits for them, and re-layouts  12.1 us
    pallas_call x6, Pallas kernels, forward(): pl.pallas_call(functools.partial(forward_kernel, own), grid=(HEADS,), out...  11.1 us
  transfers between devices with their start and end apart: 11, of which 7 were waited for; matrix products, arithmetic and copies ran while one was open for 4% of the time, Pallas kernels for 15%

profile of v1, /device:TPU:0, one launch (start us, length us, event | category | flops | bytes accessed | tf_op | source)
XLA Modules:
  0.0 200.5 jit_solution(18142515935332737449)
XLA Ops:
  0.6 3.5 %collective-permute-start = (bf16[512,512]{1,0:T(8,128)(2,1)}, bf16[512,512]{1,0:T(8,128)(2,1)S(1)}, u32[]{:S(2)}, u32[]{:S(2)}) collective-permute-start(bf16[512,512]{1,0:T(8,128)(2,1)} %bitcast.58), channel_id=1, source_target_pairs={{0,4},{1,5},{2,6},{3,7},{4,8},{5,9},{6,10},{7,11},{8,12},{9,13},{1... | collective-permute-start | bytes 1572872 | tf_op jit(solution)/shard_map/ppermute | solution.py:302
  4.2 4.6 %collective-permute-start.1 = (bf16[512,512]{1,0:T(8,128)(2,1)}, bf16[512,512]{1,0:T(8,128)(2,1)}, u32[]{:S(2)}, u32[]{:S(2)}) collective-permute-start(bf16[512,512]{1,0:T(8,128)(2,1)} %bitcast.59), channel_id=1, source_target_pairs={{0,16},{1,17},{2,18},{3,19},{4,20},{5,21},{6,22},{7,23},{8,24},{9,... | collective-permute-start | bytes 1572872 | tf_op jit(solution)/shard_map/ppermute | solution.py:302
  8.8 5.5 %collective-permute-start.2 = (bf16[512,512]{1,0:T(8,128)(2,1)}, bf16[512,512]{1,0:T(8,128)(2,1)}, u32[]{:S(2)}, u32[]{:S(2)}) collective-permute-start(bf16[512,512]{1,0:T(8,128)(2,1)} %bitcast.60), channel_id=1, source_target_pairs={{0,8},{1,9},{2,10},{3,11},{4,12},{5,13},{6,14},{7,15},{8,16},{9,17... | collective-permute-start | bytes 1572872 | tf_op jit(solution)/shard_map/ppermute | solution.py:302
  21.9 5.5 %forward_own.1 = (bf16[8,512,512]{2,1,0:T(8,128)(2,1)S(1)}, f32[8,1,512]{2,1,0:T(1,128)S(1)}, f32[8,1,512]{2,1,0:T(1,128)S(1)}, f32[512,512]{1,0:T(8,128)S(1)}, ...) custom-call(s32[1]{0:T(128)} %bitcast.seen_ref, bf16[512,512]{1,0:T(8,128)(2,1)S(1)} %bitcast.62, ...), custom_call_target="tpu_custom_call" | custom-call | flops 167772160 | bytes 917504 | tf_op jit(solution)/shard_map/forward_own/pallas_call | solution.py:108
  27.4 2.1 %copy-done.4 = bf16[8,512,512]{2,1,0:T(8,128)(2,1)} copy-done((bf16[8,512,512]{2,1,0:T(8,128)(2,1)}, bf16[8,512,512]{2,1,0:T(8,128)(2,1)S(1)}, u32[]{:S(2)}) %copy-start.4) | copy-done | bytes 4194328
  31.0 1.6 collective-permute-start.3
  32.6 2.9 %collective-permute-start.4 = (bf16[512,512]{1,0:T(8,128)(2,1)}, bf16[512,512]{1,0:T(8,128)(2,1)}, u32[]{:S(2)}, u32[]{:S(2)}) collective-permute-start(bf16[512,512]{1,0:T(8,128)(2,1)} %get-tuple-element.158), channel_id=1, source_target_pairs={{0,2},{1,3},{2,0},{3,1},{4,6},{5,7},{6,4},{7,5},{8,10},{9,11},{10,... | collective-permute-start | bytes 1572872 | tf_op jit(solution)/shard_map/ppermute | solution.py:298
  35.7 4.9 %collective-permute-done.1.x_ref.refs_2_ = bf16[512,512]{1,0:T(8,128)(2,1)} collective-permute-done((bf16[512,512]{1,0:T(8,128)(2,1)}, bf16[512,512]{1,0:T(8,128)(2,1)}, u32[]{:S(2)}, u32[]{:S(2)}) %collective-permute-start.1) | collective-permute-done | bytes 524320 | tf_op jit(solution)/shard_map/ppermute | solution.py:302
  40.6 1.5 forward_far.6
  42.1 1.3 forward_far.7
  43.4 2.8 %collective-permute-done.3.x_ref.refs_4_ = bf16[512,512]{1,0:T(8,128)(2,1)} collective-permute-done((bf16[512,512]{1,0:T(8,128)(2,1)}, bf16[512,512]{1,0:T(8,128)(2,1)}, u32[]{:S(2)}, u32[]{:S(2)}) %collective-permute-start.3) | collective-permute-done | bytes 524320 | tf_op jit(solution)/shard_map/ppermute | solution.py:298
  47.6 10.3 %collective-permute-done.4.x_ref.refs_5_ = bf16[512,512]{1,0:T(8,128)(2,1)} collective-permute-done((bf16[512,512]{1,0:T(8,128)(2,1)}, bf16[512,512]{1,0:T(8,128)(2,1)}, u32[]{:S(2)}, u32[]{:S(2)}) %collective-permute-start.4) | collective-permute-done | bytes 524320 | tf_op jit(solution)/shard_map/ppermute | solution.py:298
  59.2 1.9 join.1
  63.4 34.2 %collective-permute-start.6 = (bf16[512,512]{1,0:T(8,128)(2,1)S(1)}, bf16[512,512]{1,0:T(8,128)(2,1)S(1)}, u32[]{:S(2)}, u32[]{:S(2)}) collective-permute-start(bf16[512,512]{1,0:T(8,128)(2,1)S(1)} %get-tuple-element.134), channel_id=1, source_target_pairs={{0,2},{1,3},{2,0},{3,1},{4,6},{5,7},{6,4},{7,5},{8,10},{9,11},{10,... | collective-permute-start | bytes 1572872 | tf_op jit(solution)/shard_map/ppermute | solution.py:298
  102.7 2.2 %collective-permute-done.6.rest_1_ = bf16[512,512]{1,0:T(8,128)(2,1)S(1)} collective-permute-done((bf16[512,512]{1,0:T(8,128)(2,1)S(1)}, bf16[512,512]{1,0:T(8,128)(2,1)S(1)}, u32[]{:S(2)}, u32[]{:S(2)}) %collective-permute-start.6) | collective-permute-done | bytes 524320 | tf_op jit(solution)/shard_map/ppermute | solution.py:298
  104.8 4.7 %collective-permute-done.5.rest_0_ = bf16[512,512]{1,0:T(8,128)(2,1)S(1)} collective-permute-done((bf16[512,512]{1,0:T(8,128)(2,1)S(1)}, bf16[512,512]{1,0:T(8,128)(2,1)S(1)}, u32[]{:S(2)}, u32[]{:S(2)}) %collective-permute-start.5) | collective-permute-done | bytes 524320 | tf_op jit(solution)/shard_map/ppermute | solution.py:298
  109.6 1.8 backward_far.9
  112.7 9.3 %backward_own.1 = (f32[512,512]{1,0:T(8,128)S(1)}, bf16[512,512]{1,0:T(8,128)(2,1)S(1)}, bf16[512,512]{1,0:T(8,128)(2,1)S(1)}, f32[512,512]{1,0:T(8,128)S(1)}) custom-call(s32[1]{0:T(128)} %bitcast.seen_ref, bf16[8,512,512]{2,1,0:T(8,128)(2,1)S(1)} %copy-done.5, bf16[512,512]{1,0:T(8,128)(2,1)S(1)} %copy-done.17, bf16[512,512]{1,0:T(8,128)(2,1)S(1)} %copy-done.19, ...), custom_call_target="tpu_custom_call" | custom-call | flops 301989888 | bytes 1310720 | tf_op jit(solution)/shard_map/backward_own/pallas_call | solution.py:229
  123.0 7.1 %weight_terms.1 = bf16[128,16,512]{2,1,0:T(8,128)(2,1)} custom-call(bf16[512,512]{1,0:T(8,128)(2,1)S(1)} %bitcast.63, bf16[512,512]{1,0:T(8,128)(2,1)S(1)} %collective-permute-done.x_ref.refs_1_, bf16[512,512]{1,0:T(8,128)(2,1)} %collective-permute-done.1.x_ref.refs_2_, bf16[512,512]{1,0:T(8,128)(2,1)} %collective-permute-done.2.x_ref.refs_3_, ...), custom_call_target="tpu_custom_call" | custom-call | flops 234881024 | bytes 1572864 | tf_op jit(solution)/shard_map/weight_terms/pallas_call | solution.py:282
  130.1 6.3 %collective-permute-done.9 = bf16[512,512]{1,0:T(8,128)(2,1)S(1)} collective-permute-done((bf16[512,512]{1,0:T(8,128)(2,1)S(1)}, bf16[512,512]{1,0:T(8,128)(2,1)S(1)}, u32[]{:S(2)}, u32[]{:S(2)}) %collective-permute-start.9) | collective-permute-done | bytes 524320 | tf_op jit(solution)/shard_map/ppermute | solution.py:302
  138.0 30.6 %all-to-all-start = ((bf16[128,16,512]{2,1,0:T(8,128)(2,1)}), bf16[128,16,512]{2,1,0:T(8,128)(2,1)}, u32[]{:S(2)}, u32[]{:S(2)}) async-start(bf16[128,16,512]{2,1,0:T(8,128)(2,1)} %weight_terms.1), calls=%async_computation | async-start | bytes 4194304 | tf_op jit(solution)/shard_map/all_to_all | solution.py:347
  168.7 2.3 %fusion = bf16[1,512,512]{2,1,0:T(8,128)(2,1)} fusion(bf16[512,512]{1,0:T(8,128)(2,1)} %collective-permute-done.7, bf16[512,512]{1,0:T(8,128)(2,1)S(1)} %copy-done.21, f32[512,512]{1,0:T(8,128)S(1)} %copy-done.15, bf16[512,512]{1,0:T(8,128)(2,1)S(1)} %copy-done.23, bf16[512,512]{1,0:T(8,128)(2,1)S(1)} %copy-done.7, bf16[512,512]{1,0:T(8,128)(2,1)S(1)} %copy-done.9, ...), kind=kLoop, calls=%fused_computation.2 | loop fusion | flops 3407872 | bytes 4194306 | tf_op jit(solution)/shard_map/broadcast_in_dim | solution.py:352
  171.0 26.9 %all-to-all-done = bf16[128,16,512]{2,1,0:T(8,128)(2,1)} async-done(((bf16[128,16,512]{2,1,0:T(8,128)(2,1)}), bf16[128,16,512]{2,1,0:T(8,128)(2,1)}, u32[]{:S(2)}, u32[]{:S(2)}) %all-to-all-start) | async-done | bytes 2097184 | tf_op jit(solution)/shard_map/all_to_all | solution.py:347
  197.9 2.0 convert_reduce_fusion
  (72 shorter events, 24.0 us)
Async XLA Ops:
  0.6 28.8 %collective-permute-start = (bf16[512,512]{1,0:T(8,128)(2,1)}, bf16[512,512]{1,0:T(8,128)(2,1)S(1)}, u32[]{:S(2)}, u32[]{:S(2)}) collective-permute-start(bf16[512,512]{1,0:T(8,128)(2,1)} %bitcast.58), channel_id=1, source_target_pairs={{0,4},{1,5},{2,6},{3,7},{4,8},{5,9},{6,10},{7,11},{8,12},{9,13},{1... | collective-permute-start | bytes 1572872 | tf_op jit(solution)/shard_map/ppermute | solution.py:302
  4.2 36.5 %collective-permute-start.1 = (bf16[512,512]{1,0:T(8,128)(2,1)}, bf16[512,512]{1,0:T(8,128)(2,1)}, u32[]{:S(2)}, u32[]{:S(2)}) collective-permute-start(bf16[512,512]{1,0:T(8,128)(2,1)} %bitcast.59), channel_id=1, source_target_pairs={{0,16},{1,17},{2,18},{3,19},{4,20},{5,21},{6,22},{7,23},{8,24},{9,... | collective-permute-start | bytes 1572872 | tf_op jit(solution)/shard_map/ppermute | solution.py:302
  8.8 33.3 %collective-permute-start.2 = (bf16[512,512]{1,0:T(8,128)(2,1)}, bf16[512,512]{1,0:T(8,128)(2,1)}, u32[]{:S(2)}, u32[]{:S(2)}) collective-permute-start(bf16[512,512]{1,0:T(8,128)(2,1)} %bitcast.60), channel_id=1, source_target_pairs={{0,8},{1,9},{2,10},{3,11},{4,12},{5,13},{6,14},{7,15},{8,16},{9,17... | collective-permute-start | bytes 1572872 | tf_op jit(solution)/shard_map/ppermute | solution.py:302
  29.4 3.2 %copy-start.18 = (bf16[512,512]{1,0:T(8,128)(2,1)}, bf16[512,512]{1,0:T(8,128)(2,1)S(1)}, u32[]{:S(2)}) copy-start(bf16[512,512]{1,0:T(8,128)(2,1)S(1)} %get-tuple-element.106.v_ref) | copy-start | bytes 1572868
  31.0 15.3 %collective-permute-start.3 = (bf16[512,512]{1,0:T(8,128)(2,1)}, bf16[512,512]{1,0:T(8,128)(2,1)}, u32[]{:S(2)}, u32[]{:S(2)}) collective-permute-start(bf16[512,512]{1,0:T(8,128)(2,1)} %get-tuple-element.159), channel_id=1, source_target_pairs={{0,1},{1,2},{2,3},{3,0},{4,5},{5,6},{6,7},{7,4},{8,9},{9,10},{10,1... | collective-permute-start | bytes 1572872 | tf_op jit(solution)/shard_map/ppermute | solution.py:298
  32.6 25.2 %collective-permute-start.4 = (bf16[512,512]{1,0:T(8,128)(2,1)}, bf16[512,512]{1,0:T(8,128)(2,1)}, u32[]{:S(2)}, u32[]{:S(2)}) collective-permute-start(bf16[512,512]{1,0:T(8,128)(2,1)} %get-tuple-element.158), channel_id=1, source_target_pairs={{0,2},{1,3},{2,0},{3,1},{4,6},{5,7},{6,4},{7,5},{8,10},{9,11},{10,... | collective-permute-start | bytes 1572872 | tf_op jit(solution)/shard_map/ppermute | solution.py:298
  40.6 18.5 %copy-start.3 = (bf16[1,512,512]{2,1,0:T(8,128)(2,1)S(1)}, bf16[1,512,512]{2,1,0:T(8,128)(2,1)}, u32[]{:S(2)}) copy-start(bf16[1,512,512]{2,1,0:T(8,128)(2,1)} %param.11) | copy-start | bytes 1572868
  40.6 18.5 %copy-start.11 = (bf16[512,512]{1,0:T(8,128)(2,1)S(1)}, bf16[512,512]{1,0:T(8,128)(2,1)}, u32[]{:S(2)}) copy-start(bf16[512,512]{1,0:T(8,128)(2,1)} %refs_19_.1) | copy-start | bytes 1572868
  40.6 18.6 %copy-start.13 = (f32[512,512]{1,0:T(8,128)S(1)}, f32[512,512]{1,0:T(8,128)}, u32[]{:S(2)}) copy-start(f32[512,512]{1,0:T(8,128)} %copy-done.12) | copy-start | bytes 3145732
  63.4 41.4 %collective-permute-start.6 = (bf16[512,512]{1,0:T(8,128)(2,1)S(1)}, bf16[512,512]{1,0:T(8,128)(2,1)S(1)}, u32[]{:S(2)}, u32[]{:S(2)}) collective-permute-start(bf16[512,512]{1,0:T(8,128)(2,1)S(1)} %get-tuple-element.134), channel_id=1, source_target_pairs={{0,2},{1,3},{2,0},{3,1},{4,6},{5,7},{6,4},{7,5},{8,10},{9,11},{10,... | collective-permute-start | bytes 1572872 | tf_op jit(solution)/shard_map/ppermute | solution.py:298
  97.7 11.9 %collective-permute-start.5 = (bf16[512,512]{1,0:T(8,128)(2,1)S(1)}, bf16[512,512]{1,0:T(8,128)(2,1)S(1)}, u32[]{:S(2)}, u32[]{:S(2)}) collective-permute-start(bf16[512,512]{1,0:T(8,128)(2,1)S(1)} %get-tuple-element.133), channel_id=1, source_target_pairs={{0,3},{1,0},{2,1},{3,2},{4,7},{5,4},{6,5},{7,6},{8,11},{9,8},{10,9... | collective-permute-start | bytes 1572872 | tf_op jit(solution)/shard_map/ppermute | solution.py:298
  100.1 36.3 %collective-permute-start.9 = (bf16[512,512]{1,0:T(8,128)(2,1)S(1)}, bf16[512,512]{1,0:T(8,128)(2,1)S(1)}, u32[]{:S(2)}, u32[]{:S(2)}) collective-permute-start(bf16[512,512]{1,0:T(8,128)(2,1)S(1)} %get-tuple-element.153), channel_id=1, source_target_pairs={{16,0},{17,1},{18,2},{19,3},{20,4},{21,5},{22,6},{23,7},{24,8},{25... | collective-permute-start | bytes 1572872 | tf_op jit(solution)/shard_map/ppermute | solution.py:302
  101.4 35.0 %collective-permute-start.8 = (bf16[512,512]{1,0:T(8,128)(2,1)S(1)}, bf16[512,512]{1,0:T(8,128)(2,1)S(1)}, u32[]{:S(2)}, u32[]{:S(2)}) collective-permute-start(bf16[512,512]{1,0:T(8,128)(2,1)S(1)} %get-tuple-element.152), channel_id=1, source_target_pairs={{8,0},{9,1},{10,2},{11,3},{12,4},{13,5},{14,6},{15,7},{16,8},{17,9... | collective-permute-start | bytes 1572872 | tf_op jit(solution)/shard_map/ppermute | solution.py:302
  104.8 6.5 %copy-start.6 = (bf16[512,512]{1,0:T(8,128)(2,1)}, bf16[512,512]{1,0:T(8,128)(2,1)S(1)}, u32[]{:S(2)}) copy-start(bf16[512,512]{1,0:T(8,128)(2,1)S(1)} %collective-permute-done.6.rest_1_) | copy-start | bytes 1572868
  109.6 3.1 %copy-start.17 = (bf16[512,512]{1,0:T(8,128)(2,1)S(1)}, bf16[512,512]{1,0:T(8,128)(2,1)}, u32[]{:S(2)}) copy-start(bf16[512,512]{1,0:T(8,128)(2,1)} %copy-done.16) | copy-start | bytes 1572868
  109.6 3.1 %copy-start.19 = (bf16[512,512]{1,0:T(8,128)(2,1)S(1)}, bf16[512,512]{1,0:T(8,128)(2,1)}, u32[]{:S(2)}) copy-start(bf16[512,512]{1,0:T(8,128)(2,1)} %copy-done.18) | copy-start | bytes 1572868
  111.4 26.6 %collective-permute-start.7 = (bf16[512,512]{1,0:T(8,128)(2,1)S(1)}, bf16[512,512]{1,0:T(8,128)(2,1)}, u32[]{:S(2)}, u32[]{:S(2)}) collective-permute-start(bf16[512,512]{1,0:T(8,128)(2,1)S(1)} %get-tuple-element.151), channel_id=1, source_target_pairs={{4,0},{5,1},{6,2},{7,3},{8,4},{9,5},{10,6},{11,7},{12,8},{13,9},{1... | collective-permute-start | bytes 1572872 | tf_op jit(solution)/shard_map/ppermute | solution.py:302
  112.7 10.3 %copy-start.1 = (bf16[1,512,512]{2,1,0:T(8,128)(2,1)S(1)}, bf16[1,512,512]{2,1,0:T(8,128)(2,1)}, u32[]{:S(2)}) copy-start(bf16[1,512,512]{2,1,0:T(8,128)(2,1)} %param.6) | copy-start | bytes 1572868
  130.1 38.5 %copy-start.7 = (bf16[512,512]{1,0:T(8,128)(2,1)S(1)}, bf16[512,512]{1,0:T(8,128)(2,1)}, u32[]{:S(2)}) copy-start(bf16[512,512]{1,0:T(8,128)(2,1)} %copy-done.6) | copy-start | bytes 1572868
  130.1 38.5 %copy-start.9 = (bf16[512,512]{1,0:T(8,128)(2,1)S(1)}, bf16[512,512]{1,0:T(8,128)(2,1)}, u32[]{:S(2)}) copy-start(bf16[512,512]{1,0:T(8,128)(2,1)} %copy-done.8) | copy-start | bytes 1572868
  130.1 38.5 %copy-start.15 = (f32[512,512]{1,0:T(8,128)S(1)}, f32[512,512]{1,0:T(8,128)}, u32[]{:S(2)}) copy-start(f32[512,512]{1,0:T(8,128)} %copy-done.14) | copy-start | bytes 3145732
  138.0 30.7 %copy-start.21 = (bf16[512,512]{1,0:T(8,128)(2,1)S(1)}, bf16[512,512]{1,0:T(8,128)(2,1)}, u32[]{:S(2)}) copy-start(bf16[512,512]{1,0:T(8,128)(2,1)} %copy-done.20) | copy-start | bytes 1572868
  138.0 30.7 %copy-start.23 = (bf16[512,512]{1,0:T(8,128)(2,1)S(1)}, bf16[512,512]{1,0:T(8,128)(2,1)}, u32[]{:S(2)}) copy-start(bf16[512,512]{1,0:T(8,128)(2,1)} %copy-done.22) | copy-start | bytes 1572868
  138.0 59.9 %all-to-all-start = ((bf16[128,16,512]{2,1,0:T(8,128)(2,1)}), bf16[128,16,512]{2,1,0:T(8,128)(2,1)}, u32[]{:S(2)}, u32[]{:S(2)}) async-start(bf16[128,16,512]{2,1,0:T(8,128)(2,1)} %weight_terms.1), calls=%async_computation | async-start | bytes 4194304 | tf_op jit(solution)/shard_map/all_to_all | solution.py:347
  (11 other events, 15.7 us)

commit v2 on v1

v2 whole, which is shorter than its diff:
```python
import functools

import jax
import jax.numpy as jnp
from jax import lax
from jax.experimental import pallas as pl
from jax.experimental.pallas import tpu as pltpu
from jax.sharding import PartitionSpec as P

HEADS = 8
SIZE = 64
F32 = jnp.float32
BF16 = jnp.bfloat16
LOW = -3.0e38
MIB = 2**20


def dot(left, right, left_dim, right_dim):
    return lax.dot_general(
        left, right, (((left_dim,), (right_dim,)), ((), ())), preferred_element_type=F32
    )


def whole(shape):
    return pl.BlockSpec(shape, lambda *_: (0,) * len(shape), pipeline_mode=pl.Buffered(1))


def head_rows(count, width):
    return pl.BlockSpec((count * SIZE, width), lambda h: (h, 0))


def head_stat(count, width):
    return pl.BlockSpec((count, 1, width), lambda h: (h, 0, 0))


SCALAR = pl.BlockSpec(memory_space=pltpu.SMEM)


def params(mib=16):
    return pltpu.CompilerParams(vmem_limit_bytes=mib * MIB)


def cost(microseconds):
    return pl.CostEstimate(flops=int(microseconds * 1.1e9), bytes_accessed=MIB, transcendentals=0)


def project_kernel(*refs):
    given, outs, scratch = refs[:6], refs[6:11], refs[11:]
    q_ref, do_ref, wq_t_ref, wk_t_ref, wv_t_ref = outs
    held, sems = scratch[:6], scratch[6]
    copies = [pltpu.make_async_copy(a, b, sems.at[i]) for i, (a, b) in enumerate(zip(given, held))]
    for copy in copies:
        copy.start()
    wo, cot, wq, x, wk, wv = held
    copies[0].wait()
    copies[1].wait()
    do_ref[...] = dot(wo[...], cot[...], 1, 1).astype(BF16)
    copies[2].wait()
    wq_t_ref[...] = wq[...].T
    copies[3].wait()
    q_ref[...] = dot(wq_t_ref[...], x[...], 1, 1).astype(BF16) * jnp.asarray(0.125, BF16)
    copies[4].wait()
    wk_t_ref[...] = wk[...].T
    copies[5].wait()
    wv_t_ref[...] = wv[...].T


def project(x, cot, w_query, w_key, w_value, w_out):
    n, d = x.shape
    square = jax.ShapeDtypeStruct((d, d), BF16)
    given = (w_out, cot, w_query, x, w_key, w_value)
    return pl.pallas_call(
        project_kernel,
        out_shape=(jax.ShapeDtypeStruct((d, n), BF16),) * 2 + (square,) * 3,
        in_specs=[pl.BlockSpec(memory_space=pltpu.HBM)] * 6,
        scratch_shapes=[pltpu.VMEM(a.shape, BF16) for a in given] + [pltpu.SemaphoreType.DMA((6,))],
        compiler_params=params(12),
        cost_estimate=cost(2.5),
        name="project",
    )(*given)


def forward_kernel(own, count, seen_ref, x_ref, wk_ref, wv_ref, q_ref, p_ref, m_ref, l_ref, o_ref, k_ref, v_ref):
    step = pl.program_id(0)
    seen = seen_ref[0] > 0

    @pl.when(jnp.logical_and(seen, step == 0))
    def _():
        k_ref[...] = dot(wk_ref[...], x_ref[...], 1, 1).astype(BF16)
        v_ref[...] = dot(wv_ref[...], x_ref[...], 1, 1).astype(BF16)

    @pl.when(seen)
    def _():
        n = q_ref.shape[1]
        chunk = n // 2 if own else n
        parts = [(j, start) for j in range(count) for start in range(0, n, chunk)]
        scores = []
        for j, start in parts:
            known = start + chunk if own else n
            keys = k_ref[pl.ds(pl.multiple_of((step * count + j) * SIZE, SIZE), SIZE), :known]
            scores.append(dot(keys, q_ref[j * SIZE : (j + 1) * SIZE, start : start + chunk], 0, 0))
        for (j, start), score in zip(parts, scores):
            known = start + chunk if own else n
            cols = slice(start, start + chunk)
            if own:
                at_key = lax.broadcasted_iota(jnp.int32, score.shape, 0)
                at_query = lax.broadcasted_iota(jnp.int32, score.shape, 1) + start
                score = jnp.where(at_key <= at_query, score, LOW)
            largest = jnp.max(score, axis=0, keepdims=True)
            weights = jnp.exp(score - largest).astype(BF16)
            p_ref[j, :known, cols] = weights
            if known < n:
                p_ref[j, known:, cols] = jnp.zeros((n - known, chunk), BF16)
            values = v_ref[pl.ds(pl.multiple_of((step * count + j) * SIZE, SIZE), SIZE), :known]
            values = jnp.concatenate([values, jnp.ones((16, known), BF16)], axis=0)
            mixed = dot(values, weights, 1, 0)
            m_ref[j, :, cols] = largest
            l_ref[j, :, cols] = mixed[SIZE : SIZE + 1, :]
            o_ref[j * SIZE : (j + 1) * SIZE, cols] = mixed[:SIZE, :]

    @pl.when(jnp.logical_not(seen))
    def _():
        m_ref[...] = jnp.full(m_ref.shape, LOW, F32)
        l_ref[...] = jnp.zeros(l_ref.shape, F32)
        o_ref[...] = jnp.zeros(o_ref.shape, F32)


def forward(own, seen, x, wk_t, wv_t, q_t):
    n, d = x.shape
    count = 4 if own else 2
    return pl.pallas_call(
        functools.partial(forward_kernel, own, count),
        grid=(HEADS // count,),
        out_shape=(
            jax.ShapeDtypeStruct((HEADS, n, n), BF16),
            jax.ShapeDtypeStruct((HEADS, 1, n), F32),
            jax.ShapeDtypeStruct((HEADS, 1, n), F32),
            jax.ShapeDtypeStruct((d, n), F32),
            jax.ShapeDtypeStruct((d, n), BF16),
            jax.ShapeDtypeStruct((d, n), BF16),
        ),
        in_specs=[SCALAR, whole((n, d)), whole((d, d)), whole((d, d)), head_rows(count, n)],
        out_specs=[
            pl.BlockSpec((count, n, n), lambda h: (h, 0, 0)),
            head_stat(count, n),
            head_stat(count, n),
            head_rows(count, n),
            whole((d, n)),
            whole((d, n)),
        ],
        compiler_params=params(11),
        cost_estimate=cost(4.5 if own else 6),
        name="forward_own" if own else "forward_far",
    )(seen, x, wk_t, wv_t, q_t)


def join_kernel(count, *refs):
    ms, ls, os = refs[:count], refs[count : 2 * count], refs[2 * count : 3 * count]
    do_ref, wo_ref, cot_ref = refs[3 * count : 3 * count + 3]
    att_ref, out_ref, delta_ref = refs[3 * count + 3 : 3 * count + 6]
    cs = refs[3 * count + 6 :]
    for head in range(HEADS):
        rows = slice(head * SIZE, (head + 1) * SIZE)
        largest = functools.reduce(jnp.maximum, [m[head] for m in ms])
        factors = [jnp.exp(m[head] - largest) for m in ms]
        total = functools.reduce(jnp.add, [f * l[head] for f, l in zip(factors, ls)])
        inverse = 1.0 / total
        mixed = None
        for f, o, c in zip(factors, os, cs):
            f = f * inverse
            c[head] = f
            term = o[rows, :] * f
            mixed = term if mixed is None else mixed + term
        attended = mixed.astype(BF16)
        att_ref[rows, :] = attended
        products = attended.astype(F32) * do_ref[rows, :].astype(F32)
        delta_ref[head] = jnp.sum(products, axis=0, keepdims=True)
    out_ref[...] = dot(att_ref[...], wo_ref[...], 0, 0).astype(BF16)


def join(stats, do_t, w_out, cot):
    d, n = do_t.shape
    count = len(stats)
    row = jax.ShapeDtypeStruct((HEADS, 1, n), F32)
    return pl.pallas_call(
        functools.partial(join_kernel, count),
        out_shape=(
            jax.ShapeDtypeStruct((d, n), BF16),
            jax.ShapeDtypeStruct((n, d), BF16),
            row,
        )
        + (row,) * count,
        compiler_params=params(),
        cost_estimate=cost(2),
        name="join",
    )(*[s[0] for s in stats], *[s[1] for s in stats], *[s[2] for s in stats], do_t, w_out, cot)


def backward_kernel(
    last, carried, seen_ref, p_ref, k_ref, v_ref, q_ref, do_ref, c_ref, delta_ref, wk_ref, wv_ref, wq_ref, acc_ref,
    *rest,
):
    carry_refs, rest = rest[:carried], rest[carried:]
    dq_ref, dk_ref, dv_ref, dx_ref, *scratch = rest
    step = pl.program_id(0)
    count = p_ref.shape[0]
    seen = seen_ref[0] > 0

    @pl.when(seen)
    def _():
        grads = []
        for j in range(count):
            rows = slice(j * SIZE, (j + 1) * SIZE)
            value_dots = dot(v_ref[rows, :], do_ref[rows, :], 0, 0)
            grads.append(p_ref[j] * (value_dots - delta_ref[j]).astype(BF16))
        for j in range(count):
            rows = slice(j * SIZE, (j + 1) * SIZE)
            out = pl.ds(pl.multiple_of((step * count + j) * SIZE, SIZE), SIZE)
            factor = c_ref[j]
            scaled_q = (q_ref[rows, :].astype(F32) * factor).astype(BF16)
            scaled_do = (do_ref[rows, :].astype(F32) * factor).astype(BF16)
            dq = acc_ref[rows, :] + dot(k_ref[rows, :], grads[j], 1, 0) * factor
            dq_ref[rows, :] = dq
            dk_ref[out, :] = dot(scaled_q, grads[j], 1, 1).astype(BF16)
            dv_ref[out, :] = dot(scaled_do, p_ref[j], 1, 1).astype(BF16)
            if last:
                scratch[0][out, :] = (dq * 0.125).astype(BF16)

    @pl.when(jnp.logical_not(seen))
    def _():
        out = pl.ds(pl.multiple_of(step * count * SIZE, count * SIZE), count * SIZE)
        dq_ref[...] = acc_ref[...]
        dk_ref[out, :] = jnp.zeros(k_ref.shape, BF16)
        dv_ref[out, :] = jnp.zeros(k_ref.shape, BF16)

    @pl.when(step == HEADS // count - 1)
    def _():
        total = dot(dk_ref[...], wk_ref[...], 0, 0) + dot(dv_ref[...], wv_ref[...], 0, 0)
        if last:
            total = total + dot(scratch[0][...], wq_ref[...], 0, 0)
        for place, carry_ref in enumerate(carry_refs):
            total = total + jnp.where(seen_ref[1 + place] > 0, carry_ref[...], 0).astype(F32)
        dx_ref[...] = total.astype(dx_ref.dtype)


def backward(last, seen, p, k, v, q_t, do_t, c, delta, wk_t, wv_t, wq_t, acc, *carry):
    d, n = q_t.shape
    count = 4
    return pl.pallas_call(
        functools.partial(backward_kernel, last, len(carry)),
        grid=(HEADS // count,),
        out_shape=(
            jax.ShapeDtypeStruct((d, n), F32),
            jax.ShapeDtypeStruct((d, n), BF16),
            jax.ShapeDtypeStruct((d, n), BF16),
            jax.ShapeDtypeStruct((n, d), F32 if last else BF16),
        ),
        in_specs=[
            SCALAR,
            pl.BlockSpec((count, n, n), lambda h: (h, 0, 0)),
            *[head_rows(count, n)] * 4,
            *[head_stat(count, n)] * 2,
            *[whole((d, d))] * 3,
            head_rows(count, n),
        ]
        + [whole((n, d))] * len(carry),
        out_specs=[head_rows(count, n), whole((d, n)), whole((d, n)), whole((n, d))],
        scratch_shapes=[pltpu.VMEM((d, n), BF16)] if last else [],
        compiler_params=params(13),
        cost_estimate=cost(5.5),
        name="backward_own" if last else "backward_far",
    )(seen, p, k, v, q_t, do_t, c, delta, wk_t, wv_t, wq_t, acc, *carry)


def added(parts, xs, total=None):
    for part, x in zip(parts, xs):
        term = dot(part[...], x[...], 1, 0)
        total = term if total is None else total + term
    return total


def early_kernel(count, *refs):
    xs, dks, dvs = refs[:count], refs[count : 2 * count], refs[2 * count : 3 * count]
    att_ref, cot_ref, g_ref = refs[3 * count :]
    g_ref[0] = added(dks, xs)
    g_ref[1] = added(dvs, xs)
    g_ref[2] = dot(cot_ref[...], att_ref[...], 0, 1)


def early_terms(xs, dks, dvs, att_t, cot):
    n, d = cot.shape
    return pl.pallas_call(
        functools.partial(early_kernel, len(xs)),
        out_shape=jax.ShapeDtypeStruct((3, d, d), F32),
        compiler_params=params(14),
        cost_estimate=cost(4),
        name="early_terms",
    )(*xs, *dks, *dvs, att_t, cot)


def weights_kernel(count, core_ref, *refs):
    xs, dks, dvs = refs[:count], refs[count : 2 * count], refs[2 * count : 3 * count]
    dq_ref, early_ref, keep_ref, give_ref, sums = refs[3 * count :]

    def keep(place, value):
        for owner in range(sums.shape[0]):
            sums[owner, 4 * place : 4 * place + 4, :] = value[4 * owner : 4 * owner + 4, :]

    keep(0, dot((dq_ref[...] * 0.125).astype(BF16), xs[0][...], 1, 0))
    keep(1, added(dks, xs, early_ref[0]))
    keep(2, added(dvs, xs, early_ref[1]))
    keep(3, early_ref[2])
    core = core_ref[0]
    for high in range(2):
        here = pl.ds(pl.multiple_of((2 * high + core) * 32, 32), 32)
        there = pl.ds(pl.multiple_of((2 * high + 1 - core) * 32, 32), 32)
        keep_ref[32 * high : 32 * high + 32] = sums[here].astype(BF16)
        give_ref[32 * high : 32 * high + 32] = sums[there].astype(BF16)


def weight_terms(core, xs, dks, dvs, dq, early):
    n, d = xs[0].shape
    half = jax.ShapeDtypeStruct((64, 16, d), BF16)
    return pl.pallas_call(
        functools.partial(weights_kernel, len(xs)),
        out_shape=(half, half),
        in_specs=[SCALAR] + [pl.BlockSpec(memory_space=pltpu.VMEM)] * (3 * len(xs) + 2),
        scratch_shapes=[pltpu.VMEM((128, 16, d), F32)],
        compiler_params=params(18),
        cost_estimate=cost(3.5),
        name="weight_terms",
    )(core, *xs, *dks, *dvs, dq, early)


def place(z, x, y):
    return (z % 2) * 16 + (x % 4) * 4 + y % 4


def y_ring(value, step):
    pairs = [(place(z, x, y), place(z, x, y + step)) for z in range(2) for x in range(4) for y in range(4)]
    return lax.ppermute(value, "ctx", pairs)


def shifted(value, step):
    return lax.ppermute(
        value, "ctx", [(i, i + step) for i in range(max(0, -step), min(32, 32 - step))]
    )


def body(series, w_query, w_key, w_value, w_out, cotangent):
    x = series[0]
    cot = cotangent[0]
    n, d = x.shape
    position = lax.axis_index("ctx")
    y = position % 4
    x4 = shifted(x, 4)
    q_t, do_t, wq_t, wk_t, wv_t = project(x, cot, w_query, w_key, w_value, w_out)
    order = (0, 4, 1, 2, 16, 8)
    seen = {p: (position >= p).astype(jnp.int32).reshape(1) for p in order}
    held = {0: forward(True, seen[0], x, wk_t, wv_t, q_t)}
    x4, later, _ = lax.optimization_barrier((x4, x, held[0][1]))
    x1 = y_ring(jnp.where(y == 3, x4, later), 1)
    x2 = y_ring(jnp.where(y >= 2, x4, later), 2)
    x16, x8 = shifted(later, 16), shifted(later, 8)
    blocks = {0: x, 1: x1, 2: x2, 4: x4, 8: x8, 16: x16}
    for p in order[1:]:
        held[p] = forward(False, seen[p], blocks[p], wk_t, wv_t, q_t)
    att_t, output, delta, *factors = join([held[p][1:4] for p in order], do_t, w_out, cot)
    factor = dict(zip(order, factors))
    dq = jnp.zeros((d, n), F32)
    dk, dv, dx = {}, {}, {}
    back = {}
    for p in (1, 2, 8, 16, 4, 0):
        weights, _, _, _, keys, values = held[p]
        flags, carry = seen[p], ()
        if p == 4:
            ready = (1, 2, 8, 16)
            early = early_terms(
                [blocks[i] for i in ready], [dk[i] for i in ready], [dv[i] for i in ready], att_t, cot
            )
            early, back[1], back[2] = lax.optimization_barrier((early, back[1], back[2]))
            wraps = jnp.stack([y == 3, y >= 2]).astype(jnp.int32)
            flags, carry = jnp.concatenate([flags, wraps]), (back[1], back[2])
        dq, dk[p], dv[p], dx[p] = backward(
            p == 0, flags, weights, keys, values, q_t, do_t, factor[p], delta, wk_t, wv_t, wq_t, dq, *carry
        )
        if p in (1, 2):
            back[p] = y_ring(dx[p], -p)
        elif p:
            back[p] = shifted(dx[p], -p)
    core = lax.axis_index("dp") % 2
    kept, given = weight_terms(
        core.astype(jnp.int32).reshape(1), [x, x4], [dk[0], dk[4]], [dv[0], dv[4]], dq, early
    )
    kept, given, back[4], back[8], back[16] = lax.optimization_barrier(
        (kept, given, back[4], back[8], back[16])
    )
    given = lax.ppermute(given, "dp", [(0, 1), (1, 0), (2, 3), (3, 2)])
    terms = (kept.astype(F32) + given.astype(F32)).astype(BF16)
    same_core = [[32 * i + j for i in (k, k + 2) for j in range(32)] for k in range(2)]
    terms = lax.all_to_all(terms, ("dp", "ctx"), 0, 0, axis_index_groups=same_core, tiled=True)
    grads = jnp.sum(terms.astype(F32), axis=0).reshape(4, 4, d).transpose(0, 2, 1)
    total = dx[0] + back[8].astype(F32) + back[16].astype(F32) + back[4].astype(F32)
    total = total + jnp.where(y < 3, back[1], 0).astype(F32) + jnp.where(y < 2, back[2], 0).astype(F32)
    input_grad = total.astype(BF16)
    return (output[None], input_grad[None], grads[0], grads[1], grads[2], grads[3])


def solution(mesh):
    return jax.shard_map(
        body,
        mesh=mesh,
        in_specs=(P("dp", "ctx", None), P(), P(), P(), P(), P("dp", "ctx", None)),
        out_specs=(
            P("dp", "ctx", None),
            P("dp", "ctx", None),
            P(None, ("dp", "ctx")),
            P(None, ("dp", "ctx")),
            P(None, ("dp", "ctx")),
            P(None, ("dp", "ctx")),
        ),
        check_vma=False,
    )
```

time: 201 us -> 157 us (0.78)
  starting transfers between devices: 86.8 us -> 56.8 us
  Pallas kernels: 36.4 us -> 23.3 us
  waiting for transfers between devices: 58 us -> 63 us
  local copies, waits for them, and re-layouts: 12.8 us -> 7.99 us
    ppermute x4, starting transfers between devices: 38.7 us -> 20.3 us  [y_ring(): return lax.ppermute(value, 'ctx', pairs)]
    ppermute x4, waiting for transfers between devices: 20 us -> 34.8 us  [y_ring(): return lax.ppermute(value, 'ctx', pairs)]
    all_to_all x1, starting transfers between devices: 30.6 us -> 19.4 us  [body(): lax.all_to_all(terms, ('dp', 'ctx'), 0, 0, axis_index_groups=same_core, t...]
    all_to_all x1, waiting for transfers between devices: 26.9 us -> 16.4 us  [body(): lax.all_to_all(terms, ('dp', 'ctx'), 0, 0, axis_index_groups=same_core, t...]
    pallas_call x7 -> x8, Pallas kernels: 18.3 us -> 8.62 us  [the longest x6 4.04 us: forward(): pl.pallas_call(functools.partial(forward_kernel, own, count), grid=(HEADS...]
    unnamed x51 -> x22, local copies, waits for them, and re-layouts: 12.1 us -> 7.25 us
    pallas_call x6, Pallas kernels: 15.5 us -> 11.1 us  [backward(): pl.pallas_call(functools.partial(backward_kernel, last, len(carry)), grid...]
    ppermute x0 -> x1, waiting for transfers between devices: none -> 2.66 us  [body(): given = lax.ppermute(given, 'dp', [(0, 1), (1, 0), (2, 3), (3, 2)])]
  transfers between devices with their start and end apart: 11 -> 12, of which waited for: 7 -> 8; matrix products, arithmetic and copies ran while one was open for 4% -> 2% of each run, Pallas kernels for 15% -> 12%
where the time goes in v2:
time: 157 us; the launch traced here: 156 us
  waiting for transfers between devices  63 us (40%)
  starting transfers between devices  56.8 us (36%)
  Pallas kernels  23.3 us (15%)
  local copies, waits for them, and re-layouts  7.99 us (5%)
  other arithmetic  4.4 us (3%)
    ppermute x4, waiting for transfers between devices, y_ring(): return lax.ppermute(value, 'ctx', pairs)  34.8 us
    ppermute x4, starting transfers between devices, y_ring(): return lax.ppermute(value, 'ctx', pairs)  20.3 us
    all_to_all x1, starting transfers between devices, body(): lax.all_to_all(terms, ('dp', 'ctx'), 0, 0, axis_index_groups=same_core, t...  19.4 us
    ppermute x6, starting transfers between devices, shifted(): lax.ppermute(value, 'ctx', [(i, i + step) for i in range(max(0, -step), m...  17.1 us
    all_to_all x1, waiting for transfers between devices, body(): lax.all_to_all(terms, ('dp', 'ctx'), 0, 0, axis_index_groups=same_core, t...  16.4 us
    pallas_call x6, Pallas kernels, backward(): pl.pallas_call(functools.partial(backward_kernel, last, len(carry)), grid...  11.1 us
    ppermute x6, waiting for transfers between devices, shifted(): lax.ppermute(value, 'ctx', [(i, i + step) for i in range(max(0, -step), m...  9.16 us
    unnamed x22, local copies, waits for them, and re-layouts  7.25 us
  transfers between devices with their start and end apart: 12, of which 8 were waited for; matrix products, arithmetic and copies ran while one was open for 2% of the time, Pallas kernels for 12%

profile of v2, /device:TPU:0, one launch (start us, length us, event | category | flops | bytes accessed | tf_op | source)
XLA Modules:
  0.0 156.4 jit_solution(952471619411650775)
XLA Ops:
  0.6 3.5 %collective-permute-start = (bf16[512,512]{1,0:T(8,128)(2,1)}, bf16[512,512]{1,0:T(8,128)(2,1)S(1)}, u32[]{:S(2)}, u32[]{:S(2)}) collective-permute-start(bf16[512,512]{1,0:T(8,128)(2,1)} %bitcast.23), channel_id=1, source_target_pairs={{0,4},{1,5},{2,6},{3,7},{4,8},{5,9},{6,10},{7,11},{8,12},{9,13},{1... | collective-permute-start | bytes 1572872 | tf_op jit(solution)/shard_map/ppermute | solution.py:345
  10.5 1.8 %project.1 = (bf16[512,512]{1,0:T(8,128)(2,1)S(1)}, bf16[512,512]{1,0:T(8,128)(2,1)S(1)}, bf16[512,512]{1,0:T(8,128)(2,1)S(1)}, bf16[512,512]{1,0:T(8,128)(2,1)S(1)}, bf16[512,512]{1,0:T(8,128)(2,1)S(1)}) custom-call(bf16[512,512]{1,0:T(8,128)(2,1)S(1)} %copy-done.5, bf16[512,512]{1,0:T(8,128)(2,1)S(1)} %bitcast.30, bf16[512,512]{1,0:T(8,128)(2,1)S(1)} %copy-done.2, ...), custom_call_target="tpu_custom_call" | custom-call | flops 2750000128 | bytes 1048576 | tf_op jit(solution)/shard_map/project/pallas_call | solution.py:72
  12.4 3.2 %forward_own.1 = (bf16[8,512,512]{2,1,0:T(8,128)(2,1)S(1)}, f32[8,1,512]{2,1,0:T(1,128)S(1)}, f32[8,1,512]{2,1,0:T(1,128)S(1)}, f32[512,512]{1,0:T(8,128)S(1)}, ...) custom-call(s32[1]{0:T(128)} %bitcast.seen_ref, bf16[512,512]{1,0:T(8,128)(2,1)S(1)} %bitcast.25, ...), custom_call_target="tpu_custom_call" | custom-call | flops 4950000128 | bytes 1048576 | tf_op jit(solution)/shard_map/forward_own/pallas_call | solution.py:131
  15.6 6.8 %collective-permute-start.3 = (bf16[512,512]{1,0:T(8,128)(2,1)S(1)}, bf16[512,512]{1,0:T(8,128)(2,1)S(1)}, u32[]{:S(2)}, u32[]{:S(2)}) collective-permute-start(bf16[512,512]{1,0:T(8,128)(2,1)S(1)} %bitcast.26), channel_id=1, source_target_pairs={{0,16},{1,17},{2,18},{3,19},{4,20},{5,21},{6,22},{7,23},{8,24},{9,... | collective-permute-start | bytes 1572872 | tf_op jit(solution)/shard_map/ppermute | solution.py:345
  22.4 2.9 %collective-permute-start.4 = (bf16[512,512]{1,0:T(8,128)(2,1)S(1)}, bf16[512,512]{1,0:T(8,128)(2,1)S(1)}, u32[]{:S(2)}, u32[]{:S(2)}) collective-permute-start(bf16[512,512]{1,0:T(8,128)(2,1)S(1)} %bitcast.27), channel_id=1, source_target_pairs={{0,8},{1,9},{2,10},{3,11},{4,12},{5,13},{6,14},{7,15},{8,16},{9,17... | collective-permute-start | bytes 1572872 | tf_op jit(solution)/shard_map/ppermute | solution.py:345
  25.4 3.3 %collective-permute-start.2 = (bf16[512,512]{1,0:T(8,128)(2,1)S(1)}, bf16[512,512]{1,0:T(8,128)(2,1)S(1)}, u32[]{:S(2)}, u32[]{:S(2)}) collective-permute-start(bf16[512,512]{1,0:T(8,128)(2,1)S(1)} %get-tuple-element.178), channel_id=1, source_target_pairs={{0,2},{1,3},{2,0},{3,1},{4,6},{5,7},{6,4},{7,5},{8,10},{9,11},{10,... | collective-permute-start | bytes 1572872 | tf_op jit(solution)/shard_map/ppermute | solution.py:341
  29.5 12.4 %collective-permute-done.2.x_ref.refs_1_ = bf16[512,512]{1,0:T(8,128)(2,1)S(1)} collective-permute-done((bf16[512,512]{1,0:T(8,128)(2,1)S(1)}, bf16[512,512]{1,0:T(8,128)(2,1)S(1)}, u32[]{:S(2)}, u32[]{:S(2)}) %collective-permute-start.2) | collective-permute-done | bytes 524320 | tf_op jit(solution)/shard_map/ppermute | solution.py:341
  42.0 8.4 %collective-permute-done.1.x_ref.refs_0_ = bf16[512,512]{1,0:T(8,128)(2,1)S(1)} collective-permute-done((bf16[512,512]{1,0:T(8,128)(2,1)S(1)}, bf16[512,512]{1,0:T(8,128)(2,1)S(1)}, u32[]{:S(2)}, u32[]{:S(2)}) %collective-permute-start.1) | collective-permute-done | bytes 524320 | tf_op jit(solution)/shard_map/ppermute | solution.py:341
  52.0 1.9 %join.1 = (bf16[512,512]{1,0:T(8,128)(2,1)S(1)}, bf16[512,512]{1,0:T(8,128)(2,1)}, f32[8,1,512]{2,1,0:T(1,128)S(1)}, f32[8,1,512]{2,1,0:T(1,128)S(1)}, f32[8,1,5...) custom-call(f32[8,1,512]{2,1,0:T(1,128)S(1)} %get-tuple-element.95.r, ...), custom_call_target="tpu_custom_call" | custom-call | flops 2200000000 | bytes 1048576 | tf_op jit(solution)/shard_map/join/pallas_call | solution.py:185
  56.0 16.3 %collective-permute-start.6 = (bf16[512,512]{1,0:T(8,128)(2,1)S(1)}, bf16[512,512]{1,0:T(8,128)(2,1)S(1)}, u32[]{:S(2)}, u32[]{:S(2)}) collective-permute-start(bf16[512,512]{1,0:T(8,128)(2,1)S(1)} %get-tuple-element.157), channel_id=1, source_target_pairs={{0,2},{1,3},{2,0},{3,1},{4,6},{5,7},{6,4},{7,5},{8,10},{9,11},{10,... | collective-permute-start | bytes 1572872 | tf_op jit(solution)/shard_map/ppermute | solution.py:341
  74.2 1.3 collective-permute-start.9
  75.5 1.3 collective-permute-start.8
  76.8 2.6 %early_terms.1.refs_7_ = f32[3,512,512]{2,1,0:T(8,128)S(1)} custom-call(bf16[512,512]{1,0:T(8,128)(2,1)S(1)} %collective-permute-done.1.x_ref.refs_0_, bf16[512,512]{1,0:T(8,128)(2,1)S(1)} %collective-permute-done.2.x_ref.refs_1_, bf16[512,512]{1,0:T(8,128)(2,1)S(1)} %collective-permute-done.4.x_ref.refs_2_, ...), custom_call_target="tpu_custom_call" | custom-call | flops 4400000000 | bytes 1048576 | tf_op jit(solution)/shard_map/early_terms/pallas_call | solution.py:292
  79.4 4.2 %collective-permute-done.6.rest_1_ = bf16[512,512]{1,0:T(8,128)(2,1)S(1)} collective-permute-done((bf16[512,512]{1,0:T(8,128)(2,1)S(1)}, bf16[512,512]{1,0:T(8,128)(2,1)S(1)}, u32[]{:S(2)}, u32[]{:S(2)}) %collective-permute-start.6) | collective-permute-done | bytes 524320 | tf_op jit(solution)/shard_map/ppermute | solution.py:341
  83.5 9.8 %collective-permute-done.5.rest_0_ = bf16[512,512]{1,0:T(8,128)(2,1)S(1)} collective-permute-done((bf16[512,512]{1,0:T(8,128)(2,1)S(1)}, bf16[512,512]{1,0:T(8,128)(2,1)S(1)}, u32[]{:S(2)}, u32[]{:S(2)}) %collective-permute-start.5) | collective-permute-done | bytes 524320 | tf_op jit(solution)/shard_map/ppermute | solution.py:341
  93.4 1.5 backward_far.9
  96.2 5.8 %backward_own.1 = (f32[512,512]{1,0:T(8,128)S(1)}, bf16[512,512]{1,0:T(8,128)(2,1)S(1)}, bf16[512,512]{1,0:T(8,128)(2,1)S(1)}, f32[512,512]{1,0:T(8,128)S(1)}) custom-call(s32[1]{0:T(128)} %bitcast.seen_ref, bf16[8,512,512]{2,1,0:T(8,128)(2,1)S(1)} %get-tuple-element.117.p_ref, bf16[512,512]{1,0:T(8,128)(2,1)S(1)} %get-tuple-element.118.k_ref, ...), custom_call_target="tpu_custom_call" | custom-call | flops 6049999872 | bytes 1048576 | tf_op jit(solution)/shard_map/backward_own/pallas_call | solution.py:249
  102.0 2.0 %weight_terms.1 = (bf16[64,16,512]{2,1,0:T(8,128)(2,1)S(1)}, bf16[64,16,512]{2,1,0:T(8,128)(2,1)S(1)}) custom-call(s32[1]{0:T(128)} %bitcast.11.core_ref, bf16[512,512]{1,0:T(8,128)(2,1)S(1)} %bitcast.29, bf16[512,512]{1,0:T(8,128)(2,1)S(1)} %collective-permute-done.x_ref.refs_1_, bf16[512,512]{1,0:T(8,128)(2,1)S(1)} %get-tuple-element.162.refs_2_, ...), custom_call_target="tpu_custom_call" | custom-call | flops 3849999872 | bytes 1048576 | tf_op jit(solution)/shard_map/weight_terms/pallas_call | solution.py:324
  104.0 9.1 %collective-permute-done.7 = bf16[512,512]{1,0:T(8,128)(2,1)} collective-permute-done((bf16[512,512]{1,0:T(8,128)(2,1)S(1)}, bf16[512,512]{1,0:T(8,128)(2,1)}, u32[]{:S(2)}, u32[]{:S(2)}) %collective-permute-start.7) | collective-permute-done | bytes 524320 | tf_op jit(solution)/shard_map/ppermute | solution.py:345
  113.1 2.7 %collective-permute-done.10 = bf16[64,16,512]{2,1,0:T(8,128)(2,1)S(1)} collective-permute-done((bf16[64,16,512]{2,1,0:T(8,128)(2,1)S(1)}, bf16[64,16,512]{2,1,0:T(8,128)(2,1)S(1)}, u32[]{:S(2)}, u32[]{:S(2)}) %collective-permute-start.10) | collective-permute-done | bytes 1048608 | tf_op jit(solution)/shard_map/ppermute | solution.py:398
  115.8 1.4 add_convert_fusion
  117.2 19.4 %all-to-all-start = ((bf16[64,16,512]{2,1,0:T(8,128)(2,1)}), bf16[64,16,512]{2,1,0:T(8,128)(2,1)S(1)}, u32[]{:S(2)}, u32[]{:S(2)}) async-start(bf16[64,16,512]{2,1,0:T(8,128)(2,1)} %add_convert_fusion), calls=%async_computation | async-start | bytes 2097152 | tf_op jit(solution)/shard_map/all_to_all | solution.py:401
  136.6 2.6 %fusion = bf16[1,512,512]{2,1,0:T(8,128)(2,1)} fusion(bf16[512,512]{1,0:T(8,128)(2,1)} %collective-permute-done.7, bf16[512,512]{1,0:T(8,128)(2,1)} %collective-permute-done.9, f32[512,512]{1,0:T(8,128)S(1)} %get-tuple-element.161, bf16[512,512]{1,0:T(8,128)(2,1)} %collective-permute-done.8, bf16[512,512]{1,0:T(8,128)(2,1)S(1)} %collective-permute-done.6.rest_1_, ...), kind=kLoop, calls=%fused_computation.3 | loop fusion | flops 3407872 | bytes 4194306 | tf_op jit(solution)/shard_map/broadcast_in_dim | solution.py:406
  139.2 16.4 %all-to-all-done = bf16[64,16,512]{2,1,0:T(8,128)(2,1)S(1)} async-done(((bf16[64,16,512]{2,1,0:T(8,128)(2,1)}), bf16[64,16,512]{2,1,0:T(8,128)(2,1)S(1)}, u32[]{:S(2)}, u32[]{:S(2)}) %all-to-all-start) | async-done | bytes 1048608 | tf_op jit(solution)/shard_map/all_to_all | solution.py:401
  (47 shorter events, 15.1 us)
Async XLA Ops:
  0.6 15.0 %collective-permute-start = (bf16[512,512]{1,0:T(8,128)(2,1)}, bf16[512,512]{1,0:T(8,128)(2,1)S(1)}, u32[]{:S(2)}, u32[]{:S(2)}) collective-permute-start(bf16[512,512]{1,0:T(8,128)(2,1)} %bitcast.23), channel_id=1, source_target_pairs={{0,4},{1,5},{2,6},{3,7},{4,8},{5,9},{6,10},{7,11},{8,12},{9,13},{1... | collective-permute-start | bytes 1572872 | tf_op jit(solution)/shard_map/ppermute | solution.py:345
  4.3 1.0 copy-start
  5.3 1.0 copy-start.2
  6.3 1.0 copy-start.3
  7.4 1.0 copy-start.4
  8.4 1.0 copy-start.5
  9.5 1.0 copy-start.7
  10.5 1.9 %copy-start.1 = (bf16[1,512,512]{2,1,0:T(8,128)(2,1)S(1)}, bf16[1,512,512]{2,1,0:T(8,128)(2,1)}, u32[]{:S(2)}) copy-start(bf16[1,512,512]{2,1,0:T(8,128)(2,1)} %param.6) | copy-start | bytes 1572868
  15.6 13.1 %copy-start.9 = (bf16[512,512]{1,0:T(8,128)(2,1)}, bf16[512,512]{1,0:T(8,128)(2,1)S(1)}, u32[]{:S(2)}) copy-start(bf16[512,512]{1,0:T(8,128)(2,1)S(1)} %get-tuple-element.119.v_ref) | copy-start | bytes 1572868
  15.6 35.0 %collective-permute-start.3 = (bf16[512,512]{1,0:T(8,128)(2,1)S(1)}, bf16[512,512]{1,0:T(8,128)(2,1)S(1)}, u32[]{:S(2)}, u32[]{:S(2)}) collective-permute-start(bf16[512,512]{1,0:T(8,128)(2,1)S(1)} %bitcast.26), channel_id=1, source_target_pairs={{0,16},{1,17},{2,18},{3,19},{4,20},{5,21},{6,22},{7,23},{8,24},{9,... | collective-permute-start | bytes 1572872 | tf_op jit(solution)/shard_map/ppermute | solution.py:345
  22.4 28.4 %collective-permute-start.4 = (bf16[512,512]{1,0:T(8,128)(2,1)S(1)}, bf16[512,512]{1,0:T(8,128)(2,1)S(1)}, u32[]{:S(2)}, u32[]{:S(2)}) collective-permute-start(bf16[512,512]{1,0:T(8,128)(2,1)S(1)} %bitcast.27), channel_id=1, source_target_pairs={{0,8},{1,9},{2,10},{3,11},{4,12},{5,13},{6,14},{7,15},{8,16},{9,17... | collective-permute-start | bytes 1572872 | tf_op jit(solution)/shard_map/ppermute | solution.py:345
  25.4 16.5 %collective-permute-start.2 = (bf16[512,512]{1,0:T(8,128)(2,1)S(1)}, bf16[512,512]{1,0:T(8,128)(2,1)S(1)}, u32[]{:S(2)}, u32[]{:S(2)}) collective-permute-start(bf16[512,512]{1,0:T(8,128)(2,1)S(1)} %get-tuple-element.178), channel_id=1, source_target_pairs={{0,2},{1,3},{2,0},{3,1},{4,6},{5,7},{6,4},{7,5},{8,10},{9,11},{10,... | collective-permute-start | bytes 1572872 | tf_op jit(solution)/shard_map/ppermute | solution.py:341
  28.7 21.8 %collective-permute-start.1 = (bf16[512,512]{1,0:T(8,128)(2,1)S(1)}, bf16[512,512]{1,0:T(8,128)(2,1)S(1)}, u32[]{:S(2)}, u32[]{:S(2)}) collective-permute-start(bf16[512,512]{1,0:T(8,128)(2,1)S(1)} %get-tuple-element.179), channel_id=1, source_target_pairs={{0,1},{1,2},{2,3},{3,0},{4,5},{5,6},{6,7},{7,4},{8,9},{9,10},{10,1... | collective-permute-start | bytes 1572872 | tf_op jit(solution)/shard_map/ppermute | solution.py:341
  50.8 1.0 copy-start.6
  50.8 1.2 copy-start.8
  56.0 27.6 %collective-permute-start.6 = (bf16[512,512]{1,0:T(8,128)(2,1)S(1)}, bf16[512,512]{1,0:T(8,128)(2,1)S(1)}, u32[]{:S(2)}, u32[]{:S(2)}) collective-permute-start(bf16[512,512]{1,0:T(8,128)(2,1)S(1)} %get-tuple-element.157), channel_id=1, source_target_pairs={{0,2},{1,3},{2,0},{3,1},{4,6},{5,7},{6,4},{7,5},{8,10},{9,11},{10,... | collective-permute-start | bytes 1572872 | tf_op jit(solution)/shard_map/ppermute | solution.py:341
  72.3 21.1 %collective-permute-start.5 = (bf16[512,512]{1,0:T(8,128)(2,1)S(1)}, bf16[512,512]{1,0:T(8,128)(2,1)S(1)}, u32[]{:S(2)}, u32[]{:S(2)}) collective-permute-start(bf16[512,512]{1,0:T(8,128)(2,1)S(1)} %get-tuple-element.156), channel_id=1, source_target_pairs={{0,3},{1,0},{2,1},{3,2},{4,7},{5,4},{6,5},{7,6},{8,11},{9,8},{10,9... | collective-permute-start | bytes 1572872 | tf_op jit(solution)/shard_map/ppermute | solution.py:341
  74.2 29.9 %collective-permute-start.9 = (bf16[512,512]{1,0:T(8,128)(2,1)S(1)}, bf16[512,512]{1,0:T(8,128)(2,1)}, u32[]{:S(2)}, u32[]{:S(2)}) collective-permute-start(bf16[512,512]{1,0:T(8,128)(2,1)S(1)} %get-tuple-element.172), channel_id=1, source_target_pairs={{16,0},{17,1},{18,2},{19,3},{20,4},{21,5},{22,6},{23,7},{24,8},{25... | collective-permute-start | bytes 1572872 | tf_op jit(solution)/shard_map/ppermute | solution.py:345
  75.5 28.6 %collective-permute-start.8 = (bf16[512,512]{1,0:T(8,128)(2,1)S(1)}, bf16[512,512]{1,0:T(8,128)(2,1)}, u32[]{:S(2)}, u32[]{:S(2)}) collective-permute-start(bf16[512,512]{1,0:T(8,128)(2,1)S(1)} %get-tuple-element.171), channel_id=1, source_target_pairs={{8,0},{9,1},{10,2},{11,3},{12,4},{13,5},{14,6},{15,7},{16,8},{17,9... | collective-permute-start | bytes 1572872 | tf_op jit(solution)/shard_map/ppermute | solution.py:345
  93.4 2.8 %copy-start.10 = (bf16[512,512]{1,0:T(8,128)(2,1)S(1)}, bf16[512,512]{1,0:T(8,128)(2,1)}, u32[]{:S(2)}) copy-start(bf16[512,512]{1,0:T(8,128)(2,1)} %copy-done.9) | copy-start | bytes 1572868
  94.9 18.2 %collective-permute-start.7 = (bf16[512,512]{1,0:T(8,128)(2,1)S(1)}, bf16[512,512]{1,0:T(8,128)(2,1)}, u32[]{:S(2)}, u32[]{:S(2)}) collective-permute-start(bf16[512,512]{1,0:T(8,128)(2,1)S(1)} %get-tuple-element.170), channel_id=1, source_target_pairs={{4,0},{5,1},{6,2},{7,3},{8,4},{9,5},{10,6},{11,7},{12,8},{13,9},{1... | collective-permute-start | bytes 1572872 | tf_op jit(solution)/shard_map/ppermute | solution.py:345
  113.1 2.7 %collective-permute-start.10 = (bf16[64,16,512]{2,1,0:T(8,128)(2,1)S(1)}, bf16[64,16,512]{2,1,0:T(8,128)(2,1)S(1)}, u32[]{:S(2)}, u32[]{:S(2)}) collective-permute-start(bf16[64,16,512]{2,1,0:T(8,128)(2,1)S(1)} %get-tuple-element.177), channel_id=1, source_target_pairs={{0,32},{32,0},{64,96},{96,64},{1,33},{33,1},{65,97},{97,65},{2,34}... | collective-permute-start | bytes 3145736 | tf_op jit(solution)/shard_map/ppermute | solution.py:398
  117.2 38.4 %all-to-all-start = ((bf16[64,16,512]{2,1,0:T(8,128)(2,1)}), bf16[64,16,512]{2,1,0:T(8,128)(2,1)S(1)}, u32[]{:S(2)}, u32[]{:S(2)}) async-start(bf16[64,16,512]{2,1,0:T(8,128)(2,1)} %add_convert_fusion), calls=%async_computation | async-start | bytes 2097152 | tf_op jit(solution)/shard_map/all_to_all | solution.py:401

commit v3 on v2

--- a/solution.py
+++ b/solution.py
@@ -44,40 +44,23 @@
     return pl.CostEstimate(flops=int(microseconds * 1.1e9), bytes_accessed=MIB, transcendentals=0)
 
 
-def project_kernel(*refs):
-    given, outs, scratch = refs[:6], refs[6:11], refs[11:]
-    q_ref, do_ref, wq_t_ref, wk_t_ref, wv_t_ref = outs
-    held, sems = scratch[:6], scratch[6]
-    copies = [pltpu.make_async_copy(a, b, sems.at[i]) for i, (a, b) in enumerate(zip(given, held))]
-    for copy in copies:
-        copy.start()
-    wo, cot, wq, x, wk, wv = held
-    copies[0].wait()
-    copies[1].wait()
-    do_ref[...] = dot(wo[...], cot[...], 1, 1).astype(BF16)
-    copies[2].wait()
-    wq_t_ref[...] = wq[...].T
-    copies[3].wait()
-    q_ref[...] = dot(wq_t_ref[...], x[...], 1, 1).astype(BF16) * jnp.asarray(0.125, BF16)
-    copies[4].wait()
-    wk_t_ref[...] = wk[...].T
-    copies[5].wait()
-    wv_t_ref[...] = wv[...].T
-
-
-def project(x, cot, w_query, w_key, w_value, w_out):
+def project_kernel(x_ref, wq_ref, wk_ref, wv_ref, q_ref, wq_t_ref, wk_t_ref, wv_t_ref):
+    wq_t_ref[...] = wq_ref[...].T
+    q_ref[...] = dot(wq_t_ref[...], x_ref[...], 1, 1).astype(BF16) * jnp.asarray(0.125, BF16)
+    wk_t_ref[...] = wk_ref[...].T
+    wv_t_ref[...] = wv_ref[...].T
+
+
+def project(x, w_query, w_key, w_value):
     n, d = x.shape
     square = jax.ShapeDtypeStruct((d, d), BF16)
-    given = (w_out, cot, w_query, x, w_key, w_value)
     return pl.pallas_call(
         project_kernel,
-        out_shape=(jax.ShapeDtypeStruct((d, n), BF16),) * 2 + (square,) * 3,
-        in_specs=[pl.BlockSpec(memory_space=pltpu.HBM)] * 6,
-        scratch_shapes=[pltpu.VMEM(a.shape, BF16) for a in given] + [pltpu.SemaphoreType.DMA((6,))],
+        out_shape=(jax.ShapeDtypeStruct((d, n), BF16),) + (square,) * 3,
         compiler_params=params(12),
-        cost_estimate=cost(2.5),
+        cost_estimate=cost(2),
         name="project",
-    )(*given)
+    )(x, w_query, w_key, w_value)
 
 
 def forward_kernel(own, count, seen_ref, x_ref, wk_ref, wv_ref, q_ref, p_ref, m_ref, l_ref, o_ref, k_ref, v_ref):
@@ -125,8 +108,9 @@
         o_ref[...] = jnp.zeros(o_ref.shape, F32)
 
 
-def forward(own, seen, x, wk_t, wv_t, q_t):
+def forward(block, seen, x, wk_t, wv_t, q_t):
     n, d = x.shape
+    own = block == 0
     count = 4 if own else 2
     return pl.pallas_call(
         functools.partial(forward_kernel, own, count),
@@ -150,15 +134,15 @@
         ],
         compiler_params=params(11),
         cost_estimate=cost(4.5 if own else 6),
-        name="forward_own" if own else "forward_far",
+        name=f"forward_{block}",
     )(seen, x, wk_t, wv_t, q_t)
 
 
 def join_kernel(count, *refs):
     ms, ls, os = refs[:count], refs[count : 2 * count], refs[2 * count : 3 * count]
-    do_ref, wo_ref, cot_ref = refs[3 * count : 3 * count + 3]
-    att_ref, out_ref, delta_ref = refs[3 * count + 3 : 3 * count + 6]
-    cs = refs[3 * count + 6 :]
+    wo_ref, cot_ref, do_ref, att_ref, delta_ref = refs[3 * count : 3 * count + 5]
+    cs = refs[3 * count + 5 :]
+    do_ref[...] = dot(wo_ref[...], cot_ref[...], 1, 1).astype(BF16)
     for head in range(HEADS):
         rows = slice(head * SIZE, (head + 1) * SIZE)
         largest = functools.reduce(jnp.maximum, [m[head] for m in ms])
@@ -175,33 +159,31 @@
         att_ref[rows, :] = attended
         products = attended.astype(F32) * do_ref[rows, :].astype(F32)
         delta_ref[head] = jnp.sum(products, axis=0, keepdims=True)
-    out_ref[...] = dot(att_ref[...], wo_ref[...], 0, 0).astype(BF16)
-
-
-def join(stats, do_t, w_out, cot):
-    d, n = do_t.shape
+
+
+def join(stats, w_out, cot):
+    n, d = cot.shape
     count = len(stats)
     row = jax.ShapeDtypeStruct((HEADS, 1, n), F32)
     return pl.pallas_call(
         functools.partial(join_kernel, count),
         out_shape=(
             jax.ShapeDtypeStruct((d, n), BF16),
-            jax.ShapeDtypeStruct((n, d), BF16),
+            jax.ShapeDtypeStruct((d, n), BF16),
             row,
         )
         + (row,) * count,
         compiler_params=params(),
-        cost_estimate=cost(2),
+        cost_estimate=cost(2.5),
         name="join",
-    )(*[s[0] for s in stats], *[s[1] for s in stats], *[s[2] for s in stats], do_t, w_out, cot)
+    )(*[s[0] for s in stats], *[s[1] for s in stats], *[s[2] for s in stats], w_out, cot)
 
 
 def backward_kernel(
-    last, carried, seen_ref, p_ref, k_ref, v_ref, q_ref, do_ref, c_ref, delta_ref, wk_ref, wv_ref, wq_ref, acc_ref,
-    *rest,
+    own, carried, seen_ref, p_ref, k_ref, v_ref, q_ref, do_ref, c_ref, delta_ref, wk_ref, wv_ref, acc_ref, *rest
 ):
     carry_refs, rest = rest[:carried], rest[carried:]
-    dq_ref, dk_ref, dv_ref, dx_ref, *scratch = rest
+    dq_ref, dk_ref, dv_ref, *dx_refs = rest
     step = pl.program_id(0)
     count = p_ref.shape[0]
     seen = seen_ref[0] > 0
@@ -219,12 +201,9 @@
             factor = c_ref[j]
             scaled_q = (q_ref[rows, :].astype(F32) * factor).astype(BF16)
             scaled_do = (do_ref[rows, :].astype(F32) * factor).astype(BF16)
-            dq = acc_ref[rows, :] + dot(k_ref[rows, :], grads[j], 1, 0) * factor
-            dq_ref[rows, :] = dq
+            dq_ref[rows, :] = acc_ref[rows, :] + dot(k_ref[rows, :], grads[j], 1, 0) * factor
             dk_ref[out, :] = dot(scaled_q, grads[j], 1, 1).astype(BF16)
             dv_ref[out, :] = dot(scaled_do, p_ref[j], 1, 1).astype(BF16)
-            if last:
-                scratch[0][out, :] = (dq * 0.125).astype(BF16)
 
     @pl.when(jnp.logical_not(seen))
     def _():
@@ -233,43 +212,65 @@
         dk_ref[out, :] = jnp.zeros(k_ref.shape, BF16)
         dv_ref[out, :] = jnp.zeros(k_ref.shape, BF16)
 
-    @pl.when(step == HEADS // count - 1)
-    def _():
-        total = dot(dk_ref[...], wk_ref[...], 0, 0) + dot(dv_ref[...], wv_ref[...], 0, 0)
-        if last:
-            total = total + dot(scratch[0][...], wq_ref[...], 0, 0)
-        for place, carry_ref in enumerate(carry_refs):
-            total = total + jnp.where(seen_ref[1 + place] > 0, carry_ref[...], 0).astype(F32)
-        dx_ref[...] = total.astype(dx_ref.dtype)
-
-
-def backward(last, seen, p, k, v, q_t, do_t, c, delta, wk_t, wv_t, wq_t, acc, *carry):
+    if not own:
+
+        @pl.when(step == HEADS // count - 1)
+        def _():
+            total = dot(dk_ref[...], wk_ref[...], 0, 0) + dot(dv_ref[...], wv_ref[...], 0, 0)
+            for place, carry_ref in enumerate(carry_refs):
+                total = total + jnp.where(seen_ref[1 + place] > 0, carry_ref[...], 0).astype(F32)
+            dx_refs[0][...] = total.astype(BF16)
+
+
+def backward(block, seen, p, k, v, q_t, do_t, c, delta, wk_t, wv_t, acc, *carry):
     d, n = q_t.shape
+    own = block == 0
     count = 4
     return pl.pallas_call(
-        functools.partial(backward_kernel, last, len(carry)),
+        functools.partial(backward_kernel, own, len(carry)),
         grid=(HEADS // count,),
-        out_shape=(
+        out_shape=[
             jax.ShapeDtypeStruct((d, n), F32),
             jax.ShapeDtypeStruct((d, n), BF16),
             jax.ShapeDtypeStruct((d, n), BF16),
-            jax.ShapeDtypeStruct((n, d), F32 if last else BF16),
-        ),
+        ]
+        + [jax.ShapeDtypeStruct((n, d), BF16)] * (not own),
         in_specs=[
             SCALAR,
             pl.BlockSpec((count, n, n), lambda h: (h, 0, 0)),
             *[head_rows(count, n)] * 4,
             *[head_stat(count, n)] * 2,
-            *[whole((d, d))] * 3,
+            *[whole((d, d))] * 2,
             head_rows(count, n),
         ]
         + [whole((n, d))] * len(carry),
-        out_specs=[head_rows(count, n), whole((d, n)), whole((d, n)), whole((n, d))],
-        scratch_shapes=[pltpu.VMEM((d, n), BF16)] if last else [],
+        out_specs=[head_rows(count, n), whole((d, n)), whole((d, n))] + [whole((n, d))] * (not own),
         compiler_params=params(13),
         cost_estimate=cost(5.5),
-        name="backward_own" if last else "backward_far",
-    )(seen, p, k, v, q_t, do_t, c, delta, wk_t, wv_t, wq_t, acc, *carry)
+        name=f"backward_{block}",
+    )(seen, p, k, v, q_t, do_t, c, delta, wk_t, wv_t, acc, *carry)
+
+
+def final_kernel(flag_ref, att_ref, wo_ref, dq_ref, dk_ref, dv_ref, wq_ref, wk_ref, wv_ref, *refs):
+    backs, (out_ref, grad_ref) = refs[:-2], refs[-2:]
+    out_ref[...] = dot(att_ref[...], wo_ref[...], 0, 0).astype(BF16)
+    total = dot((dq_ref[...] * 0.125).astype(BF16), wq_ref[...], 0, 0)
+    total = total + dot(dk_ref[...], wk_ref[...], 0, 0) + dot(dv_ref[...], wv_ref[...], 0, 0)
+    for place, back in enumerate(backs):
+        total = total + jnp.where(flag_ref[place] > 0, back[...], 0).astype(F32)
+    grad_ref[...] = total.astype(BF16)
+
+
+def finish(flags, att_t, w_out, dq, dk, dv, wq_t, wk_t, wv_t, *backs):
+    d, n = att_t.shape
+    return pl.pallas_call(
+        final_kernel,
+        out_shape=(jax.ShapeDtypeStruct((n, d), BF16),) * 2,
+        in_specs=[SCALAR] + [pl.BlockSpec(memory_space=pltpu.VMEM)] * (8 + len(backs)),
+        compiler_params=params(13),
+        cost_estimate=cost(40),
+        name="finish",
+    )(flags, att_t, w_out, dq, dk, dv, wq_t, wk_t, wv_t, *backs)
 
 
 def added(parts, xs, total=None):
@@ -332,12 +333,47 @@
     )(core, *xs, *dks, *dvs, dq, early)
 
 
+def either_kernel(flag_ref, first_ref, second_ref, out_ref):
+    @pl.when(flag_ref[0] > 0)
+    def _():
+        out_ref[...] = first_ref[...]
+
+    @pl.when(flag_ref[0] <= 0)
+    def _():
+        out_ref[...] = second_ref[...]
+
+
+def either(flag, first, second):
+    return pl.pallas_call(
+        either_kernel,
+        out_shape=jax.ShapeDtypeStruct(first.shape, first.dtype),
+        in_specs=[SCALAR] + [pl.BlockSpec(memory_space=pltpu.VMEM)] * 2,
+        compiler_params=params(4),
+        cost_estimate=cost(0.5),
+        name="either",
+    )(flag.astype(jnp.int32).reshape(1), first, second)
+
+
+def sum_kernel(first_ref, second_ref, out_ref):
+    out_ref[...] = (first_ref[...].astype(F32) + second_ref[...].astype(F32)).astype(BF16)
+
+
+def sum_of(first, second):
+    return pl.pallas_call(
+        sum_kernel,
+        out_shape=jax.ShapeDtypeStruct(first.shape, BF16),
+        compiler_params=params(6),
+        cost_estimate=cost(1),
+        name="sum_of",
+    )(first, second)
+
+
 def place(z, x, y):
     return (z % 2) * 16 + (x % 4) * 4 + y % 4
 
 
-def y_ring(value, step):
-    pairs = [(place(z, x, y), place(z, x, y + step)) for z in range(2) for x in range(4) for y in range(4)]
+def y_ring(value, step, sources=(0, 1, 2, 3)):
+    pairs = [(place(z, x, y), place(z, x, y + step)) for z in range(2) for x in range(4) for y in sources]
     return lax.ppermute(value, "ctx", pairs)
 
 
@@ -354,23 +390,24 @@
     position = lax.axis_index("ctx")
     y = position % 4
     x4 = shifted(x, 4)
-    q_t, do_t, wq_t, wk_t, wv_t = project(x, cot, w_query, w_key, w_value, w_out)
-    order = (0, 4, 1, 2, 16, 8)
+    x1, x2 = y_ring(x, 1, (0, 1, 2)), y_ring(x, 2, (0, 1))
+    q_t, wq_t, wk_t, wv_t = project(x, w_query, w_key, w_value)
+    order = (0, 4, 1, 16, 2, 8)
     seen = {p: (position >= p).astype(jnp.int32).reshape(1) for p in order}
-    held = {0: forward(True, seen[0], x, wk_t, wv_t, q_t)}
+    held = {0: forward(0, seen[0], x, wk_t, wv_t, q_t)}
     x4, later, _ = lax.optimization_barrier((x4, x, held[0][1]))
-    x1 = y_ring(jnp.where(y == 3, x4, later), 1)
-    x2 = y_ring(jnp.where(y >= 2, x4, later), 2)
+    x1 = either(y == 0, y_ring(x4, 1, (3,)), x1)
+    x2 = either(y < 2, y_ring(x4, 2, (2, 3)), x2)
     x16, x8 = shifted(later, 16), shifted(later, 8)
     blocks = {0: x, 1: x1, 2: x2, 4: x4, 8: x8, 16: x16}
     for p in order[1:]:
-        held[p] = forward(False, seen[p], blocks[p], wk_t, wv_t, q_t)
-    att_t, output, delta, *factors = join([held[p][1:4] for p in order], do_t, w_out, cot)
+        held[p] = forward(p, seen[p], blocks[p], wk_t, wv_t, q_t)
+    do_t, att_t, delta, *factors = join([held[p][1:4] for p in order], w_out, cot)
     factor = dict(zip(order, factors))
     dq = jnp.zeros((d, n), F32)
-    dk, dv, dx = {}, {}, {}
+    dk, dv = {}, {}
     back = {}
-    for p in (1, 2, 8, 16, 4, 0):
+    for p in (1, 2, 8, 16, 0, 4):
         weights, _, _, _, keys, values = held[p]
         flags, carry = seen[p], ()
         if p == 4:
@@ -381,28 +418,27 @@
             early, back[1], back[2] = lax.optimization_barrier((early, back[1], back[2]))
             wraps = jnp.stack([y == 3, y >= 2]).astype(jnp.int32)
             flags, carry = jnp.concatenate([flags, wraps]), (back[1], back[2])
-        dq, dk[p], dv[p], dx[p] = backward(
-            p == 0, flags, weights, keys, values, q_t, do_t, factor[p], delta, wk_t, wv_t, wq_t, dq, *carry
+        dq, dk[p], dv[p], *sent = backward(
+            p, flags, weights, keys, values, q_t, do_t, factor[p], delta, wk_t, wv_t, dq, *carry
         )
         if p in (1, 2):
-            back[p] = y_ring(dx[p], -p)
+            back[p] = y_ring(sent[0], -p)
         elif p:
-            back[p] = shifted(dx[p], -p)
+            back[p] = shifted(sent[0], -p)
     core = lax.axis_index("dp") % 2
     kept, given = weight_terms(
         core.astype(jnp.int32).reshape(1), [x, x4], [dk[0], dk[4]], [dv[0], dv[4]], dq, early
     )
-    kept, given, back[4], back[8], back[16] = lax.optimization_barrier(
-        (kept, given, back[4], back[8], back[16])
-    )
+    kept, given, back[8], back[16] = lax.optimization_barrier((kept, given, back[8], back[16]))
     given = lax.ppermute(given, "dp", [(0, 1), (1, 0), (2, 3), (3, 2)])
-    terms = (kept.astype(F32) + given.astype(F32)).astype(BF16)
+    terms = sum_of(kept, given)
     same_core = [[32 * i + j for i in (k, k + 2) for j in range(32)] for k in range(2)]
     terms = lax.all_to_all(terms, ("dp", "ctx"), 0, 0, axis_index_groups=same_core, tiled=True)
     grads = jnp.sum(terms.astype(F32), axis=0).reshape(4, 4, d).transpose(0, 2, 1)
-    total = dx[0] + back[8].astype(F32) + back[16].astype(F32) + back[4].astype(F32)
-    total = total + jnp.where(y < 3, back[1], 0).astype(F32) + jnp.where(y < 2, back[2], 0).astype(F32)
-    input_grad = total.astype(BF16)
+    flags = jnp.stack([y >= 0, y >= 0, y >= 0, y < 3, y < 2]).astype(jnp.int32)
+    output, input_grad = finish(
+        flags, att_t, w_out, dq, dk[0], dv[0], wq_t, wk_t, wv_t, back[4], back[8], back[16], back[1], back[2]
+    )
     return (output[None], input_grad[None], grads[0], grads[1], grads[2], grads[3])
 
 

time: 157 us -> 153 us (0.975)
  waiting for transfers between devices: 63 us -> 37.6 us
  local copies, waits for them, and re-layouts: 7.99 us -> 18.9 us
  starting transfers between devices: 56.8 us -> 66.6 us
  other arithmetic: 4.4 us -> 1.56 us
  Pallas kernels: 23.3 us -> 26 us
    ppermute x4 -> x6, waiting for transfers between devices: 34.8 us -> 23 us  [y_ring(): return lax.ppermute(value, 'ctx', pairs)]
    unnamed x22 -> x58, local copies, waits for them, and re-layouts: 7.25 us -> 18.1 us
    all_to_all x1, waiting for transfers between devices: 16.4 us -> 6.9 us  [body(): lax.all_to_all(terms, ('dp', 'ctx'), 0, 0, axis_index_groups=same_core, t...]
    pallas_call x6 -> x10, Pallas kernels: 11.1 us -> 15.8 us  [the longest x6 10.9 us: backward(): pl.pallas_call(functools.partial(backward_kernel, own, len(carry)), grid=...]
    ppermute x6, starting transfers between devices: 17.1 us -> 20.8 us  [shifted(): lax.ppermute(value, 'ctx', [(i, i + step) for i in range(max(0, -step), m...]
    ppermute x4 -> x6, starting transfers between devices: 20.3 us -> 23.5 us  [y_ring(): return lax.ppermute(value, 'ctx', pairs)]
    all_to_all x1, starting transfers between devices: 19.4 us -> 22.3 us  [body(): lax.all_to_all(terms, ('dp', 'ctx'), 0, 0, axis_index_groups=same_core, t...]
    broadcast_in_dim x1 -> x0, other arithmetic: 2.61 us -> none  [body(): input_grad[None]]
  transfers between devices with their start and end apart: 12 -> 14, of which waited for: 8 -> 7; matrix products, arithmetic and copies ran while one was open for 2% -> 0% of each run, Pallas kernels for 12% -> 15%
where the time goes in v3:
time: 153 us; the launch traced here: 152 us
  starting transfers between devices  66.6 us (44%)
  waiting for transfers between devices  37.6 us (25%)
  Pallas kernels  26 us (17%)
  local copies, waits for them, and re-layouts  18.9 us (12%)
  other arithmetic  1.56 us (1%)
    ppermute x6, starting transfers between devices, y_ring(): return lax.ppermute(value, 'ctx', pairs)  23.5 us
    ppermute x6, waiting for transfers between devices, y_ring(): return lax.ppermute(value, 'ctx', pairs)  23 us
    all_to_all x1, starting transfers between devices, body(): lax.all_to_all(terms, ('dp', 'ctx'), 0, 0, axis_index_groups=same_core, t...  22.3 us
    ppermute x6, starting transfers between devices, shifted(): lax.ppermute(value, 'ctx', [(i, i + step) for i in range(max(0, -step), m...  20.8 us
    unnamed x58, local copies, waits for them, and re-layouts  18.1 us
    pallas_call x6, Pallas kernels, backward(): pl.pallas_call(functools.partial(backward_kernel, own, len(carry)), grid=...  10.9 us
    all_to_all x1, waiting for transfers between devices, body(): lax.all_to_all(terms, ('dp', 'ctx'), 0, 0, axis_index_groups=same_core, t...  6.9 us
    ppermute x6, waiting for transfers between devices, shifted(): lax.ppermute(value, 'ctx', [(i, i + step) for i in range(max(0, -step), m...  6.74 us
  transfers between devices with their start and end apart: 14, of which 7 were waited for; matrix products, arithmetic and copies ran while one was open for 0% of the time, Pallas kernels for 15%

profile of v3, /device:TPU:0, one launch (start us, length us, event | category | flops | bytes accessed | tf_op | source)
XLA Modules:
  0.0 151.8 jit_solution(2464382827339046469)
XLA Ops:
  0.6 3.5 %collective-permute-start = (bf16[512,512]{1,0:T(8,128)(2,1)}, bf16[512,512]{1,0:T(8,128)(2,1)S(1)}, u32[]{:S(2)}, u32[]{:S(2)}) collective-permute-start(bf16[512,512]{1,0:T(8,128)(2,1)} %bitcast.28), channel_id=1, source_target_pairs={{0,4},{1,5},{2,6},{3,7},{4,8},{5,9},{6,10},{7,11},{8,12},{9,13},{1... | collective-permute-start | bytes 1572872 | tf_op jit(solution)/shard_map/ppermute | solution.py:381
  4.2 5.1 %collective-permute-start.5 = (bf16[512,512]{1,0:T(8,128)(2,1)}, bf16[512,512]{1,0:T(8,128)(2,1)S(1)}, u32[]{:S(2)}, u32[]{:S(2)}) collective-permute-start(bf16[512,512]{1,0:T(8,128)(2,1)} %bitcast.29), channel_id=1, source_target_pairs={{0,2},{1,3},{4,6},{5,7},{8,10},{9,11},{12,14},{13,15},{16,18},{17,... | collective-permute-start | bytes 1572872 | tf_op jit(solution)/shard_map/ppermute | solution.py:377
  9.3 2.6 %collective-permute-start.2 = (bf16[512,512]{1,0:T(8,128)(2,1)}, bf16[512,512]{1,0:T(8,128)(2,1)S(1)}, u32[]{:S(2)}, u32[]{:S(2)}) collective-permute-start(bf16[512,512]{1,0:T(8,128)(2,1)} %bitcast.30), channel_id=1, source_target_pairs={{0,1},{1,2},{2,3},{4,5},{5,6},{6,7},{8,9},{9,10},{10,11},{12,13},{... | collective-permute-start | bytes 1572872 | tf_op jit(solution)/shard_map/ppermute | solution.py:377
  17.2 3.2 %forward_0.1 = (bf16[8,512,512]{2,1,0:T(8,128)(2,1)S(1)}, f32[8,1,512]{2,1,0:T(1,128)S(1)}, f32[8,1,512]{2,1,0:T(1,128)S(1)}, f32[512,512]{1,0:T(8,128)S(1)}, bf...) custom-call(s32[1]{0:T(128)} %bitcast.3.seen_ref, bf16[512,512]{1,0:T(8,128)(2,1)S(1)} %bitcast.32, ...), custom_call_target="tpu_custom_call" | custom-call | flops 4950000128 | bytes 1048576 | tf_op jit(solution)/shard_map/forward_0/pallas_call | solution.py:115
  20.5 1.3 collective-permute-start.4
  21.8 1.3 collective-permute-start.1
  23.1 4.6 %collective-permute-start.6 = (bf16[512,512]{1,0:T(8,128)(2,1)S(1)}, bf16[512,512]{1,0:T(8,128)(2,1)S(1)}, u32[]{:S(2)}, u32[]{:S(2)}) collective-permute-start(bf16[512,512]{1,0:T(8,128)(2,1)S(1)} %bitcast.33), channel_id=1, source_target_pairs={{0,8},{1,9},{2,10},{3,11},{4,12},{5,13},{6,14},{7,15},{8,16},{9,17... | collective-permute-start | bytes 1572872 | tf_op jit(solution)/shard_map/ppermute | solution.py:381
  27.9 8.5 %collective-permute-start.3 = (bf16[512,512]{1,0:T(8,128)(2,1)S(1)}, bf16[512,512]{1,0:T(8,128)(2,1)S(1)}, u32[]{:S(2)}, u32[]{:S(2)}) collective-permute-start(bf16[512,512]{1,0:T(8,128)(2,1)S(1)} %bitcast.34), channel_id=1, source_target_pairs={{0,16},{1,17},{2,18},{3,19},{4,20},{5,21},{6,22},{7,23},{8,24},{9,... | collective-permute-start | bytes 1572872 | tf_op jit(solution)/shard_map/ppermute | solution.py:381
  37.0 10.9 %collective-permute-done.1.first_ref = bf16[512,512]{1,0:T(8,128)(2,1)S(1)} collective-permute-done((bf16[512,512]{1,0:T(8,128)(2,1)S(1)}, bf16[512,512]{1,0:T(8,128)(2,1)S(1)}, u32[]{:S(2)}, u32[]{:S(2)}) %collective-permute-start.1) | collective-permute-done | bytes 524320 | tf_op jit(solution)/shard_map/ppermute | solution.py:377
  48.6 2.3 %collective-permute-done.3.x_ref.refs_3_ = bf16[512,512]{1,0:T(8,128)(2,1)S(1)} collective-permute-done((bf16[512,512]{1,0:T(8,128)(2,1)S(1)}, bf16[512,512]{1,0:T(8,128)(2,1)S(1)}, u32[]{:S(2)}, u32[]{:S(2)}) %collective-permute-start.3) | collective-permute-done | bytes 524320 | tf_op jit(solution)/shard_map/ppermute | solution.py:381
  55.0 12.5 %collective-permute-start.8 = (bf16[512,512]{1,0:T(8,128)(2,1)S(1)}, bf16[512,512]{1,0:T(8,128)(2,1)S(1)}, u32[]{:S(2)}, u32[]{:S(2)}) collective-permute-start(bf16[512,512]{1,0:T(8,128)(2,1)S(1)} %get-tuple-element.155), channel_id=1, source_target_pairs={{0,2},{1,3},{2,0},{3,1},{4,6},{5,7},{6,4},{7,5},{8,10},{9,11},{10,... | collective-permute-start | bytes 1572872 | tf_op jit(solution)/shard_map/ppermute | solution.py:377
  70.1 1.3 collective-permute-start.11
  71.4 1.3 collective-permute-start.10
  72.7 2.6 %early_terms.1.refs_7_ = f32[3,512,512]{2,1,0:T(8,128)S(1)} custom-call(bf16[512,512]{1,0:T(8,128)(2,1)S(1)} %either.2.x_ref.refs_0_, bf16[512,512]{1,0:T(8,128)(2,1)S(1)} %either.3.x_ref.refs_1_, bf16[512,512]{1,0:T(8,128)(2,1)S(1)} %collective-permute-done.6.x_ref.refs_2_, bf16[512,512]{1,0:T(8,128)(2,1)S(1)} %collective-permute-done.3.x_ref.refs_3_, ...), custom_call_target="tpu_custom_call" | custom-call | flops 4400000000 | bytes 1048576 | tf_op jit(solution)/shard_map/early_terms/pallas_call | solution.py:293
  75.3 4.8 %backward_0.1 = (f32[512,512]{1,0:T(8,128)S(1)}, bf16[512,512]{1,0:T(8,128)(2,1)S(1)}, bf16[512,512]{1,0:T(8,128)(2,1)S(1)}) custom-call(s32[1]{0:T(128)} %bitcast.3.seen_ref, bf16[8,512,512]{2,1,0:T(8,128)(2,1)S(1)} %get-tuple-element.121.p_ref, bf16[512,512]{1,0:T(8,128)(2,1)S(1)} %get-tuple-element.122.k_ref, ...), custom_call_target="tpu_custom_call" | custom-call | flops 6049999872 | bytes 1048576 | tf_op jit(solution)/shard_map/backward_0/pallas_call | solution.py:229
  80.1 11.8 %collective-permute-done.7.rest_0_.refs_3_ = bf16[512,512]{1,0:T(8,128)(2,1)S(1)} collective-permute-done((bf16[512,512]{1,0:T(8,128)(2,1)S(1)}, bf16[512,512]{1,0:T(8,128)(2,1)S(1)}, u32[]{:S(2)}, u32[]{:S(2)}) %collective-permute-start.7) | collective-permute-done | bytes 524320 | tf_op jit(solution)/shard_map/ppermute | solution.py:377
  91.8 2.3 %backward_4.1 = (f32[512,512]{1,0:T(8,128)S(1)}, bf16[512,512]{1,0:T(8,128)(2,1)S(1)}, bf16[512,512]{1,0:T(8,128)(2,1)S(1)}, bf16[512,512]{1,0:T(8,128)(2,1)}) custom-call(s32[3]{0:T(128)S(1)} %pad_add_fusion.seen_ref, bf16[8,512,512]{2,1,0:T(8,128)(2,1)S(1)} %get-tuple-element.115.p_ref, bf16[512,512]{1,0:T(8,128)(2,1)S(1)} %get-tuple-element.116.k_ref, ...), custom_call_target="tpu_custom_call" | custom-call | flops 6049999872 | bytes 1048576 | tf_op jit(solution)/shard_map/backward_4/pallas_call | solution.py:229
  94.2 2.0 %weight_terms.1 = (bf16[64,16,512]{2,1,0:T(8,128)(2,1)S(1)}, bf16[64,16,512]{2,1,0:T(8,128)(2,1)S(1)}) custom-call(s32[1]{0:T(128)} %bitcast.14.core_ref, bf16[512,512]{1,0:T(8,128)(2,1)S(1)} %bitcast.35, bf16[512,512]{1,0:T(8,128)(2,1)S(1)} %collective-permute-done.x_ref.refs_1_, bf16[512,512]{1,0:T(8,128)(2,1)S(1)} %get-tuple-element.159.refs_2_.dk_ref, ...), custom_call_target="tpu_custom_call" | custom-call | flops 3849999872 | bytes 1048576 | tf_op jit(solution)/shard_map/weight_terms/pallas_call | solution.py:325
  97.2 4.5 %collective-permute-done.11.refs_2_ = bf16[512,512]{1,0:T(8,128)(2,1)S(1)} collective-permute-done((bf16[512,512]{1,0:T(8,128)(2,1)S(1)}, bf16[512,512]{1,0:T(8,128)(2,1)S(1)}, u32[]{:S(2)}, u32[]{:S(2)}) %collective-permute-start.11) | collective-permute-done | bytes 524320 | tf_op jit(solution)/shard_map/ppermute | solution.py:381
  103.4 1.5 %collective-permute-start.9 = (bf16[512,512]{1,0:T(8,128)(2,1)}, bf16[512,512]{1,0:T(8,128)(2,1)}, u32[]{:S(2)}, u32[]{:S(2)}) collective-permute-start(bf16[512,512]{1,0:T(8,128)(2,1)} %get-tuple-element.162), channel_id=1, source_target_pairs={{4,0},{5,1},{6,2},{7,3},{8,4},{9,5},{10,6},{11,7},{12,8},{13,9},{1... | collective-permute-start | bytes 1572872 | tf_op jit(solution)/shard_map/ppermute | solution.py:381
  108.5 22.3 %all-to-all-start = ((bf16[64,16,512]{2,1,0:T(8,128)(2,1)}), bf16[64,16,512]{2,1,0:T(8,128)(2,1)}, u32[]{:S(2)}, u32[]{:S(2)}) async-start(bf16[64,16,512]{2,1,0:T(8,128)(2,1)} %sum_of.1), calls=%async_computation | async-start | bytes 2097152 | tf_op jit(solution)/shard_map/all_to_all | solution.py:436
  139.4 3.5 %finish.1 = (bf16[512,512]{1,0:T(8,128)(2,1)}, bf16[512,512]{1,0:T(8,128)(2,1)}) custom-call(s32[5]{0:T(128)S(1)} %convert_element_type.6.flag_ref, bf16[512,512]{1,0:T(8,128)(2,1)S(1)} %copy-done.16, bf16[512,512]{1,0:T(8,128)(2,1)S(1)} %copy-done.6, f32[512,512]{1,0:T(8,128)S(1)} %copy-done.18, bf16[512,512]{1,0:T(8,128)(2,1)S(1)} %copy-done.26, ...), custom_call_target="tpu_custom_call" | custom-call | flops 44000002048 | bytes 1048576 | tf_op jit(solution)/shard_map/finish/pallas_call | solution.py:266
  142.9 6.9 %all-to-all-done = bf16[64,16,512]{2,1,0:T(8,128)(2,1)} async-done(((bf16[64,16,512]{2,1,0:T(8,128)(2,1)}), bf16[64,16,512]{2,1,0:T(8,128)(2,1)}, u32[]{:S(2)}, u32[]{:S(2)}) %all-to-all-start) | async-done | bytes 1048608 | tf_op jit(solution)/shard_map/all_to_all | solution.py:436
  149.8 1.4 convert_reduce_fusion
  (90 shorter events, 28.7 us)
Async XLA Ops:
  0.6 19.8 %collective-permute-start = (bf16[512,512]{1,0:T(8,128)(2,1)}, bf16[512,512]{1,0:T(8,128)(2,1)S(1)}, u32[]{:S(2)}, u32[]{:S(2)}) collective-permute-start(bf16[512,512]{1,0:T(8,128)(2,1)} %bitcast.28), channel_id=1, source_target_pairs={{0,4},{1,5},{2,6},{3,7},{4,8},{5,9},{6,10},{7,11},{8,12},{9,13},{1... | collective-permute-start | bytes 1572872 | tf_op jit(solution)/shard_map/ppermute | solution.py:381
  4.2 23.8 %collective-permute-start.5 = (bf16[512,512]{1,0:T(8,128)(2,1)}, bf16[512,512]{1,0:T(8,128)(2,1)S(1)}, u32[]{:S(2)}, u32[]{:S(2)}) collective-permute-start(bf16[512,512]{1,0:T(8,128)(2,1)} %bitcast.29), channel_id=1, source_target_pairs={{0,2},{1,3},{4,6},{5,7},{8,10},{9,11},{12,14},{13,15},{16,18},{17,... | collective-permute-start | bytes 1572872 | tf_op jit(solution)/shard_map/ppermute | solution.py:377
  9.3 27.7 %collective-permute-start.2 = (bf16[512,512]{1,0:T(8,128)(2,1)}, bf16[512,512]{1,0:T(8,128)(2,1)S(1)}, u32[]{:S(2)}, u32[]{:S(2)}) collective-permute-start(bf16[512,512]{1,0:T(8,128)(2,1)} %bitcast.30), channel_id=1, source_target_pairs={{0,1},{1,2},{2,3},{4,5},{5,6},{6,7},{8,9},{9,10},{10,11},{12,13},{... | collective-permute-start | bytes 1572872 | tf_op jit(solution)/shard_map/ppermute | solution.py:377
  16.7 3.7 %copy-start.19 = (bf16[512,512]{1,0:T(8,128)(2,1)}, bf16[512,512]{1,0:T(8,128)(2,1)S(1)}, u32[]{:S(2)}) copy-start(bf16[512,512]{1,0:T(8,128)(2,1)S(1)} %get-tuple-element.161.wq_ref) | copy-start | bytes 1572868
  16.7 75.1 %copy-start.21 = (bf16[512,512]{1,0:T(8,128)(2,1)}, bf16[512,512]{1,0:T(8,128)(2,1)S(1)}, u32[]{:S(2)}) copy-start(bf16[512,512]{1,0:T(8,128)(2,1)S(1)} %get-tuple-element.91.wk_ref) | copy-start | bytes 1572868
  16.7 75.1 %copy-start.23 = (bf16[512,512]{1,0:T(8,128)(2,1)}, bf16[512,512]{1,0:T(8,128)(2,1)S(1)}, u32[]{:S(2)}) copy-start(bf16[512,512]{1,0:T(8,128)(2,1)S(1)} %get-tuple-element.92.wv_ref) | copy-start | bytes 1572868
  20.5 16.3 %collective-permute-start.4 = (bf16[512,512]{1,0:T(8,128)(2,1)S(1)}, bf16[512,512]{1,0:T(8,128)(2,1)S(1)}, u32[]{:S(2)}, u32[]{:S(2)}) collective-permute-start(bf16[512,512]{1,0:T(8,128)(2,1)S(1)} %collective-permute-done.x_ref.refs_1_), channel_id=1, source_target_pairs={{2,0},{3,1},{6,4},{7,5},{10,8},{11,9},{14,12},{15,13},{18,16},{19,... | collective-permute-start | bytes 1572872 | tf_op jit(solution)/shard_map/ppermute | solution.py:377
  21.8 26.2 %collective-permute-start.1 = (bf16[512,512]{1,0:T(8,128)(2,1)S(1)}, bf16[512,512]{1,0:T(8,128)(2,1)S(1)}, u32[]{:S(2)}, u32[]{:S(2)}) collective-permute-start(bf16[512,512]{1,0:T(8,128)(2,1)S(1)} %collective-permute-done.x_ref.refs_1_), channel_id=1, source_target_pairs={{3,0},{7,4},{11,8},{15,12},{19,16},{23,20},{27,24},{31,28},{35,32}... | collective-permute-start | bytes 1572872 | tf_op jit(solution)/shard_map/ppermute | solution.py:377
  23.1 25.3 %collective-permute-start.6 = (bf16[512,512]{1,0:T(8,128)(2,1)S(1)}, bf16[512,512]{1,0:T(8,128)(2,1)S(1)}, u32[]{:S(2)}, u32[]{:S(2)}) collective-permute-start(bf16[512,512]{1,0:T(8,128)(2,1)S(1)} %bitcast.33), channel_id=1, source_target_pairs={{0,8},{1,9},{2,10},{3,11},{4,12},{5,13},{6,14},{7,15},{8,16},{9,17... | collective-permute-start | bytes 1572872 | tf_op jit(solution)/shard_map/ppermute | solution.py:381
  27.9 22.9 %collective-permute-start.3 = (bf16[512,512]{1,0:T(8,128)(2,1)S(1)}, bf16[512,512]{1,0:T(8,128)(2,1)S(1)}, u32[]{:S(2)}, u32[]{:S(2)}) collective-permute-start(bf16[512,512]{1,0:T(8,128)(2,1)S(1)} %bitcast.34), channel_id=1, source_target_pairs={{0,16},{1,17},{2,18},{3,19},{4,20},{5,21},{6,22},{7,23},{8,24},{9,... | collective-permute-start | bytes 1572872 | tf_op jit(solution)/shard_map/ppermute | solution.py:381
  53.0 19.7 %copy-start.15 = (bf16[512,512]{1,0:T(8,128)(2,1)}, bf16[512,512]{1,0:T(8,128)(2,1)S(1)}, u32[]{:S(2)}) copy-start(bf16[512,512]{1,0:T(8,128)(2,1)S(1)} %get-tuple-element.114.refs_12_.att_ref) | copy-start | bytes 1572868
  55.0 25.0 %collective-permute-start.8 = (bf16[512,512]{1,0:T(8,128)(2,1)S(1)}, bf16[512,512]{1,0:T(8,128)(2,1)S(1)}, u32[]{:S(2)}, u32[]{:S(2)}) collective-permute-start(bf16[512,512]{1,0:T(8,128)(2,1)S(1)} %get-tuple-element.155), channel_id=1, source_target_pairs={{0,2},{1,3},{2,0},{3,1},{4,6},{5,7},{6,4},{7,5},{8,10},{9,11},{10,... | collective-permute-start | bytes 1572872 | tf_op jit(solution)/shard_map/ppermute | solution.py:377
  67.6 24.3 %collective-permute-start.7 = (bf16[512,512]{1,0:T(8,128)(2,1)S(1)}, bf16[512,512]{1,0:T(8,128)(2,1)S(1)}, u32[]{:S(2)}, u32[]{:S(2)}) collective-permute-start(bf16[512,512]{1,0:T(8,128)(2,1)S(1)} %get-tuple-element.154), channel_id=1, source_target_pairs={{0,3},{1,0},{2,1},{3,2},{4,7},{5,4},{6,5},{7,6},{8,11},{9,8},{10,9... | collective-permute-start | bytes 1572872 | tf_op jit(solution)/shard_map/ppermute | solution.py:377
  70.1 31.6 %collective-permute-start.11 = (bf16[512,512]{1,0:T(8,128)(2,1)S(1)}, bf16[512,512]{1,0:T(8,128)(2,1)S(1)}, u32[]{:S(2)}, u32[]{:S(2)}) collective-permute-start(bf16[512,512]{1,0:T(8,128)(2,1)S(1)} %get-tuple-element.169), channel_id=1, source_target_pairs={{16,0},{17,1},{18,2},{19,3},{20,4},{21,5},{22,6},{23,7},{24,8},{25... | collective-permute-start | bytes 1572872 | tf_op jit(solution)/shard_map/ppermute | solution.py:381
  71.4 31.2 %collective-permute-start.10 = (bf16[512,512]{1,0:T(8,128)(2,1)S(1)}, bf16[512,512]{1,0:T(8,128)(2,1)S(1)}, u32[]{:S(2)}, u32[]{:S(2)}) collective-permute-start(bf16[512,512]{1,0:T(8,128)(2,1)S(1)} %get-tuple-element.168), channel_id=1, source_target_pairs={{8,0},{9,1},{10,2},{11,3},{12,4},{13,5},{14,6},{15,7},{16,8},{17,9... | collective-permute-start | bytes 1572872 | tf_op jit(solution)/shard_map/ppermute | solution.py:381
  80.0 14.1 %copy-start.25 = (bf16[512,512]{1,0:T(8,128)(2,1)}, bf16[512,512]{1,0:T(8,128)(2,1)S(1)}, u32[]{:S(2)}) copy-start(bf16[512,512]{1,0:T(8,128)(2,1)S(1)} %get-tuple-element.159.refs_2_.dk_ref) | copy-start | bytes 1572868
  80.1 14.1 %copy-start.27 = (bf16[512,512]{1,0:T(8,128)(2,1)}, bf16[512,512]{1,0:T(8,128)(2,1)S(1)}, u32[]{:S(2)}) copy-start(bf16[512,512]{1,0:T(8,128)(2,1)S(1)} %get-tuple-element.160.refs_4_.dv_ref) | copy-start | bytes 1572868
  91.8 2.3 %copy-start.7 = (bf16[512,512]{1,0:T(8,128)(2,1)}, bf16[512,512]{1,0:T(8,128)(2,1)S(1)}, u32[]{:S(2)}) copy-start(bf16[512,512]{1,0:T(8,128)(2,1)S(1)} %collective-permute-done.7.rest_0_.refs_3_) | copy-start | bytes 1572868
  94.2 2.0 %copy-start.17 = (f32[512,512]{1,0:T(8,128)}, f32[512,512]{1,0:T(8,128)S(1)}, u32[]{:S(2)}) copy-start(f32[512,512]{1,0:T(8,128)S(1)} %get-tuple-element.158.refs_6_.dq_ref) | copy-start | bytes 3145732
  103.4 2.7 %collective-permute-start.12 = (bf16[64,16,512]{2,1,0:T(8,128)(2,1)S(1)}, bf16[64,16,512]{2,1,0:T(8,128)(2,1)S(1)}, u32[]{:S(2)}, u32[]{:S(2)}) collective-permute-start(bf16[64,16,512]{2,1,0:T(8,128)(2,1)S(1)} %get-tuple-element.175), channel_id=1, source_target_pairs={{0,32},{32,0},{64,96},{96,64},{1,33},{33,1},{65,97},{97,65},{2,34}... | collective-permute-start | bytes 3145736 | tf_op jit(solution)/shard_map/ppermute | solution.py:433
  103.4 27.5 %collective-permute-start.9 = (bf16[512,512]{1,0:T(8,128)(2,1)}, bf16[512,512]{1,0:T(8,128)(2,1)}, u32[]{:S(2)}, u32[]{:S(2)}) collective-permute-start(bf16[512,512]{1,0:T(8,128)(2,1)} %get-tuple-element.162), channel_id=1, source_target_pairs={{4,0},{5,1},{6,2},{7,3},{8,4},{9,5},{10,6},{11,7},{12,8},{13,9},{1... | collective-permute-start | bytes 1572872 | tf_op jit(solution)/shard_map/ppermute | solution.py:381
  107.3 23.6 %copy-start.8 = (bf16[512,512]{1,0:T(8,128)(2,1)S(1)}, bf16[512,512]{1,0:T(8,128)(2,1)}, u32[]{:S(2)}) copy-start(bf16[512,512]{1,0:T(8,128)(2,1)} %copy-done.7) | copy-start | bytes 1572868
  107.3 23.6 %copy-start.10 = (bf16[512,512]{1,0:T(8,128)(2,1)S(1)}, bf16[512,512]{1,0:T(8,128)(2,1)}, u32[]{:S(2)}) copy-start(bf16[512,512]{1,0:T(8,128)(2,1)} %copy-done.9) | copy-start | bytes 1572868
  108.5 41.3 %all-to-all-start = ((bf16[64,16,512]{2,1,0:T(8,128)(2,1)}), bf16[64,16,512]{2,1,0:T(8,128)(2,1)}, u32[]{:S(2)}, u32[]{:S(2)}) async-start(bf16[64,16,512]{2,1,0:T(8,128)(2,1)} %sum_of.1), calls=%async_computation | async-start | bytes 2097152 | tf_op jit(solution)/shard_map/all_to_all | solution.py:436
  (19 other events, 19.9 us)

commit v4 on v3

--- a/solution.py
+++ b/solution.py
@@ -180,10 +180,9 @@
 
 
 def backward_kernel(
-    own, carried, seen_ref, p_ref, k_ref, v_ref, q_ref, do_ref, c_ref, delta_ref, wk_ref, wv_ref, acc_ref, *rest
+    sends, seen_ref, p_ref, k_ref, v_ref, q_ref, do_ref, c_ref, delta_ref, wk_ref, wv_ref, acc_ref,
+    dq_ref, dk_ref, dv_ref, *dx_refs,
 ):
-    carry_refs, rest = rest[:carried], rest[carried:]
-    dq_ref, dk_ref, dv_ref, *dx_refs = rest
     step = pl.program_id(0)
     count = p_ref.shape[0]
     seen = seen_ref[0] > 0
@@ -212,29 +211,27 @@
         dk_ref[out, :] = jnp.zeros(k_ref.shape, BF16)
         dv_ref[out, :] = jnp.zeros(k_ref.shape, BF16)
 
-    if not own:
+    if sends:
 
         @pl.when(step == HEADS // count - 1)
         def _():
             total = dot(dk_ref[...], wk_ref[...], 0, 0) + dot(dv_ref[...], wv_ref[...], 0, 0)
-            for place, carry_ref in enumerate(carry_refs):
-                total = total + jnp.where(seen_ref[1 + place] > 0, carry_ref[...], 0).astype(F32)
             dx_refs[0][...] = total.astype(BF16)
 
 
-def backward(block, seen, p, k, v, q_t, do_t, c, delta, wk_t, wv_t, acc, *carry):
+def backward(block, seen, p, k, v, q_t, do_t, c, delta, wk_t, wv_t, acc):
     d, n = q_t.shape
-    own = block == 0
+    sends = block not in (0, 4)
     count = 4
     return pl.pallas_call(
-        functools.partial(backward_kernel, own, len(carry)),
+        functools.partial(backward_kernel, sends),
         grid=(HEADS // count,),
         out_shape=[
             jax.ShapeDtypeStruct((d, n), F32),
             jax.ShapeDtypeStruct((d, n), BF16),
             jax.ShapeDtypeStruct((d, n), BF16),
         ]
-        + [jax.ShapeDtypeStruct((n, d), BF16)] * (not own),
+        + [jax.ShapeDtypeStruct((n, d), BF16)] * sends,
         in_specs=[
             SCALAR,
             pl.BlockSpec((count, n, n), lambda h: (h, 0, 0)),
@@ -242,35 +239,53 @@
             *[head_stat(count, n)] * 2,
             *[whole((d, d))] * 2,
             head_rows(count, n),
-        ]
-        + [whole((n, d))] * len(carry),
-        out_specs=[head_rows(count, n), whole((d, n)), whole((d, n))] + [whole((n, d))] * (not own),
+        ],
+        out_specs=[head_rows(count, n), whole((d, n)), whole((d, n))] + [whole((n, d))] * sends,
         compiler_params=params(13),
         cost_estimate=cost(5.5),
         name=f"backward_{block}",
-    )(seen, p, k, v, q_t, do_t, c, delta, wk_t, wv_t, acc, *carry)
-
-
-def final_kernel(flag_ref, att_ref, wo_ref, dq_ref, dk_ref, dv_ref, wq_ref, wk_ref, wv_ref, *refs):
-    backs, (out_ref, grad_ref) = refs[:-2], refs[-2:]
+    )(seen, p, k, v, q_t, do_t, c, delta, wk_t, wv_t, acc)
+
+
+def returned_kernel(flag_ref, dk_ref, dv_ref, wk_ref, wv_ref, *refs):
+    one, two, eight, sixteen, sent_ref, sum_ref = refs
+    total = dot(dk_ref[...], wk_ref[...], 0, 0) + dot(dv_ref[...], wv_ref[...], 0, 0)
+    total = total + jnp.where(flag_ref[0] > 0, one[...], 0).astype(F32)
+    total = total + jnp.where(flag_ref[1] > 0, two[...], 0).astype(F32)
+    sent_ref[...] = total.astype(BF16)
+    kept = eight[...].astype(F32) + sixteen[...].astype(F32)
+    kept = kept + jnp.where(flag_ref[0] > 0, 0, one[...]).astype(F32)
+    sum_ref[...] = kept + jnp.where(flag_ref[1] > 0, 0, two[...]).astype(F32)
+
+
+def returned(flags, dk, dv, wk_t, wv_t, *backs):
+    d, n = dk.shape
+    return pl.pallas_call(
+        returned_kernel,
+        out_shape=(jax.ShapeDtypeStruct((n, d), BF16), jax.ShapeDtypeStruct((n, d), F32)),
+        in_specs=[SCALAR] + [pl.BlockSpec(memory_space=pltpu.VMEM)] * 8,
+        compiler_params=params(10),
+        cost_estimate=cost(20),
+        name="returned",
+    )(flags, dk, dv, wk_t, wv_t, *backs)
+
+
+def final_kernel(att_ref, wo_ref, dq_ref, dk_ref, dv_ref, wq_ref, wk_ref, wv_ref, sum_ref, four, out_ref, grad_ref):
     out_ref[...] = dot(att_ref[...], wo_ref[...], 0, 0).astype(BF16)
     total = dot((dq_ref[...] * 0.125).astype(BF16), wq_ref[...], 0, 0)
     total = total + dot(dk_ref[...], wk_ref[...], 0, 0) + dot(dv_ref[...], wv_ref[...], 0, 0)
-    for place, back in enumerate(backs):
-        total = total + jnp.where(flag_ref[place] > 0, back[...], 0).astype(F32)
-    grad_ref[...] = total.astype(BF16)
-
-
-def finish(flags, att_t, w_out, dq, dk, dv, wq_t, wk_t, wv_t, *backs):
+    grad_ref[...] = (total + sum_ref[...] + four[...].astype(F32)).astype(BF16)
+
+
+def finish(att_t, w_out, dq, dk, dv, wq_t, wk_t, wv_t, total, four):
     d, n = att_t.shape
     return pl.pallas_call(
         final_kernel,
         out_shape=(jax.ShapeDtypeStruct((n, d), BF16),) * 2,
-        in_specs=[SCALAR] + [pl.BlockSpec(memory_space=pltpu.VMEM)] * (8 + len(backs)),
         compiler_params=params(13),
         cost_estimate=cost(40),
         name="finish",
-    )(flags, att_t, w_out, dq, dk, dv, wq_t, wk_t, wv_t, *backs)
+    )(att_t, w_out, dq, dk, dv, wq_t, wk_t, wv_t, total, four)
 
 
 def added(parts, xs, total=None):
@@ -390,17 +405,18 @@
     position = lax.axis_index("ctx")
     y = position % 4
     x4 = shifted(x, 4)
-    x1, x2 = y_ring(x, 1, (0, 1, 2)), y_ring(x, 2, (0, 1))
+    x1, x2 = shifted(x, 1), y_ring(x, 2, (0, 1))
     q_t, wq_t, wk_t, wv_t = project(x, w_query, w_key, w_value)
     order = (0, 4, 1, 16, 2, 8)
     seen = {p: (position >= p).astype(jnp.int32).reshape(1) for p in order}
     held = {0: forward(0, seen[0], x, wk_t, wv_t, q_t)}
     x4, later, _ = lax.optimization_barrier((x4, x, held[0][1]))
-    x1 = either(y == 0, y_ring(x4, 1, (3,)), x1)
     x2 = either(y < 2, y_ring(x4, 2, (2, 3)), x2)
-    x16, x8 = shifted(later, 16), shifted(later, 8)
+    held[4] = forward(4, seen[4], x4, wk_t, wv_t, q_t)
+    latest, _ = lax.optimization_barrier((later, held[4][1]))
+    x16, x8 = shifted(later, 16), shifted(latest, 8)
     blocks = {0: x, 1: x1, 2: x2, 4: x4, 8: x8, 16: x16}
-    for p in order[1:]:
+    for p in order[2:]:
         held[p] = forward(p, seen[p], blocks[p], wk_t, wv_t, q_t)
     do_t, att_t, delta, *factors = join([held[p][1:4] for p in order], w_out, cot)
     factor = dict(zip(order, factors))
@@ -409,36 +425,29 @@
     back = {}
     for p in (1, 2, 8, 16, 0, 4):
         weights, _, _, _, keys, values = held[p]
-        flags, carry = seen[p], ()
-        if p == 4:
-            ready = (1, 2, 8, 16)
-            early = early_terms(
-                [blocks[i] for i in ready], [dk[i] for i in ready], [dv[i] for i in ready], att_t, cot
-            )
-            early, back[1], back[2] = lax.optimization_barrier((early, back[1], back[2]))
-            wraps = jnp.stack([y == 3, y >= 2]).astype(jnp.int32)
-            flags, carry = jnp.concatenate([flags, wraps]), (back[1], back[2])
         dq, dk[p], dv[p], *sent = backward(
-            p, flags, weights, keys, values, q_t, do_t, factor[p], delta, wk_t, wv_t, dq, *carry
+            p, seen[p], weights, keys, values, q_t, do_t, factor[p], delta, wk_t, wv_t, dq
         )
         if p in (1, 2):
             back[p] = y_ring(sent[0], -p)
-        elif p:
+        elif sent:
             back[p] = shifted(sent[0], -p)
+    dk[1], back[1], back[2] = lax.optimization_barrier((dk[1], back[1], back[2]))
+    ready = (1, 2, 8, 16)
+    early = early_terms([blocks[i] for i in ready], [dk[i] for i in ready], [dv[i] for i in ready], att_t, cot)
     core = lax.axis_index("dp") % 2
     kept, given = weight_terms(
         core.astype(jnp.int32).reshape(1), [x, x4], [dk[0], dk[4]], [dv[0], dv[4]], dq, early
     )
-    kept, given, back[8], back[16] = lax.optimization_barrier((kept, given, back[8], back[16]))
+    wraps = jnp.stack([y == 3, y >= 2]).astype(jnp.int32)
+    sent, total = returned(wraps, dk[4], dv[4], wk_t, wv_t, back[1], back[2], back[8], back[16])
+    back[4] = shifted(sent, -4)
     given = lax.ppermute(given, "dp", [(0, 1), (1, 0), (2, 3), (3, 2)])
     terms = sum_of(kept, given)
     same_core = [[32 * i + j for i in (k, k + 2) for j in range(32)] for k in range(2)]
     terms = lax.all_to_all(terms, ("dp", "ctx"), 0, 0, axis_index_groups=same_core, tiled=True)
     grads = jnp.sum(terms.astype(F32), axis=0).reshape(4, 4, d).transpose(0, 2, 1)
-    flags = jnp.stack([y >= 0, y >= 0, y >= 0, y < 3, y < 2]).astype(jnp.int32)
-    output, input_grad = finish(
-        flags, att_t, w_out, dq, dk[0], dv[0], wq_t, wk_t, wv_t, back[4], back[8], back[16], back[1], back[2]
-    )
+    output, input_grad = finish(att_t, w_out, dq, dk[0], dv[0], wq_t, wk_t, wv_t, total, back[4])
     return (output[None], input_grad[None], grads[0], grads[1], grads[2], grads[3])
 
 

time: 153 us -> 142 us (0.928)
  starting transfers between devices: 66.6 us -> 55.3 us
  waiting for transfers between devices: 37.6 us -> 45.4 us
  local copies, waits for them, and re-layouts: 18.9 us -> 13.8 us
  Pallas kernels: 26 us -> 24.1 us
    ppermute x6 -> x7, waiting for transfers between devices: 6.74 us -> 18.3 us  [shifted(): lax.ppermute(value, 'ctx', [(i, i + step) for i in range(max(0, -step), m...]
    ppermute x6 -> x4, starting transfers between devices: 23.5 us -> 12.2 us  [y_ring(): return lax.ppermute(value, 'ctx', pairs)]
    unnamed x58 -> x38, local copies, waits for them, and re-layouts: 18.1 us -> 13.1 us
    ppermute x6 -> x4, waiting for transfers between devices: 23 us -> 19.3 us  [y_ring(): return lax.ppermute(value, 'ctx', pairs)]
    all_to_all x1, starting transfers between devices: 22.3 us -> 19.6 us  [body(): lax.all_to_all(terms, ('dp', 'ctx'), 0, 0, axis_index_groups=same_core, t...]
    ppermute x6 -> x7, starting transfers between devices: 20.8 us -> 23.4 us  [shifted(): lax.ppermute(value, 'ctx', [(i, i + step) for i in range(max(0, -step), m...]
    pallas_call x6 -> x7, Pallas kernels: 10.9 us -> 10.5 us  [the longest x6 8.78 us: backward(): pl.pallas_call(functools.partial(backward_kernel, sends), grid=(HEADS //...]
  transfers between devices with their start and end apart: 14 -> 13, of which waited for: 7 -> 6; matrix products, arithmetic and copies ran while one was open for 0% -> 0% of each run, Pallas kernels for 15% -> 15%
where the time goes in v4:
time: 142 us; the launch traced here: 141 us
  starting transfers between devices  55.3 us (39%)
  waiting for transfers between devices  45.4 us (32%)
  Pallas kernels  24.1 us (17%)
  local copies, waits for them, and re-layouts  13.8 us (10%)
  other arithmetic  1.48 us (1%)
    ppermute x7, starting transfers between devices, shifted(): lax.ppermute(value, 'ctx', [(i, i + step) for i in range(max(0, -step), m...  23.4 us
    all_to_all x1, starting transfers between devices, body(): lax.all_to_all(terms, ('dp', 'ctx'), 0, 0, axis_index_groups=same_core, t...  19.6 us
    ppermute x4, waiting for transfers between devices, y_ring(): return lax.ppermute(value, 'ctx', pairs)  19.3 us
    ppermute x7, waiting for transfers between devices, shifted(): lax.ppermute(value, 'ctx', [(i, i + step) for i in range(max(0, -step), m...  18.3 us
    unnamed x38, local copies, waits for them, and re-layouts  13.1 us
    ppermute x4, starting transfers between devices, y_ring(): return lax.ppermute(value, 'ctx', pairs)  12.2 us
    pallas_call x6, Pallas kernels, backward(): pl.pallas_call(functools.partial(backward_kernel, sends), grid=(HEADS //...  8.78 us
    all_to_all x1, waiting for transfers between devices, body(): lax.all_to_all(terms, ('dp', 'ctx'), 0, 0, axis_index_groups=same_core, t...  7.81 us
  transfers between devices with their start and end apart: 13, of which 6 were waited for; matrix products, arithmetic and copies ran while one was open for 0% of the time, Pallas kernels for 15%

profile of v4, /device:TPU:0, one launch (start us, length us, event | category | flops | bytes accessed | tf_op | source)
XLA Modules:
  0.0 141.2 jit_solution(1937564556955362889)
XLA Ops:
  0.6 3.5 %collective-permute-start = (bf16[512,512]{1,0:T(8,128)(2,1)}, bf16[512,512]{1,0:T(8,128)(2,1)S(1)}, u32[]{:S(2)}, u32[]{:S(2)}) collective-permute-start(bf16[512,512]{1,0:T(8,128)(2,1)} %bitcast.25), channel_id=1, source_target_pairs={{0,4},{1,5},{2,6},{3,7},{4,8},{5,9},{6,10},{7,11},{8,12},{9,13},{1... | collective-permute-start | bytes 1572872 | tf_op jit(solution)/shard_map/ppermute | solution.py:396
  4.2 5.1 %collective-permute-start.4 = (bf16[512,512]{1,0:T(8,128)(2,1)}, bf16[512,512]{1,0:T(8,128)(2,1)S(1)}, u32[]{:S(2)}, u32[]{:S(2)}) collective-permute-start(bf16[512,512]{1,0:T(8,128)(2,1)} %bitcast.26), channel_id=1, source_target_pairs={{0,2},{1,3},{4,6},{5,7},{8,10},{9,11},{12,14},{13,15},{16,18},{17,... | collective-permute-start | bytes 1572872 | tf_op jit(solution)/shard_map/ppermute | solution.py:392
  9.3 2.6 %collective-permute-start.1 = (bf16[512,512]{1,0:T(8,128)(2,1)}, bf16[512,512]{1,0:T(8,128)(2,1)S(1)}, u32[]{:S(2)}, u32[]{:S(2)}) collective-permute-start(bf16[512,512]{1,0:T(8,128)(2,1)} %bitcast.27), channel_id=1, source_target_pairs={{0,1},{1,2},{2,3},{3,4},{4,5},{5,6},{6,7},{7,8},{8,9},{9,10},{10,1... | collective-permute-start | bytes 1572872 | tf_op jit(solution)/shard_map/ppermute | solution.py:396
  17.2 3.1 %forward_0.1 = (bf16[8,512,512]{2,1,0:T(8,128)(2,1)S(1)}, f32[8,1,512]{2,1,0:T(1,128)S(1)}, f32[8,1,512]{2,1,0:T(1,128)S(1)}, f32[512,512]{1,0:T(8,128)S(1)}, bf...) custom-call(s32[1]{0:T(128)} %bitcast.seen_ref, bf16[512,512]{1,0:T(8,128)(2,1)S(1)} %bitcast.29, ...), custom_call_target="tpu_custom_call" | custom-call | flops 4950000128 | bytes 1048576 | tf_op jit(solution)/shard_map/forward_0/pallas_call | solution.py:115
  20.3 1.3 collective-permute-start.3
  21.6 3.8 %collective-permute-start.2 = (bf16[512,512]{1,0:T(8,128)(2,1)S(1)}, bf16[512,512]{1,0:T(8,128)(2,1)S(1)}, u32[]{:S(2)}, u32[]{:S(2)}) collective-permute-start(bf16[512,512]{1,0:T(8,128)(2,1)S(1)} %bitcast.30), channel_id=1, source_target_pairs={{0,16},{1,17},{2,18},{3,19},{4,20},{5,21},{6,22},{7,23},{8,24},{9,... | collective-permute-start | bytes 1572872 | tf_op jit(solution)/shard_map/ppermute | solution.py:396
  25.6 9.3 %collective-permute-start.5 = (bf16[512,512]{1,0:T(8,128)(2,1)S(1)}, bf16[512,512]{1,0:T(8,128)(2,1)S(1)}, u32[]{:S(2)}, u32[]{:S(2)}) collective-permute-start(bf16[512,512]{1,0:T(8,128)(2,1)S(1)} %bitcast.31), channel_id=1, source_target_pairs={{0,8},{1,9},{2,10},{3,11},{4,12},{5,13},{6,14},{7,15},{8,16},{9,17... | collective-permute-start | bytes 1572872 | tf_op jit(solution)/shard_map/ppermute | solution.py:396
  35.2 8.8 %collective-permute-done.3.first_ref = bf16[512,512]{1,0:T(8,128)(2,1)S(1)} collective-permute-done((bf16[512,512]{1,0:T(8,128)(2,1)S(1)}, bf16[512,512]{1,0:T(8,128)(2,1)S(1)}, u32[]{:S(2)}, u32[]{:S(2)}) %collective-permute-start.3) | collective-permute-done | bytes 524320 | tf_op jit(solution)/shard_map/ppermute | solution.py:392
  45.1 9.2 %collective-permute-done.2.x_ref.refs_3_ = bf16[512,512]{1,0:T(8,128)(2,1)S(1)} collective-permute-done((bf16[512,512]{1,0:T(8,128)(2,1)S(1)}, bf16[512,512]{1,0:T(8,128)(2,1)S(1)}, u32[]{:S(2)}, u32[]{:S(2)}) %collective-permute-start.2) | collective-permute-done | bytes 524320 | tf_op jit(solution)/shard_map/ppermute | solution.py:396
  58.5 5.8 %collective-permute-start.7 = (bf16[512,512]{1,0:T(8,128)(2,1)S(1)}, bf16[512,512]{1,0:T(8,128)(2,1)S(1)}, u32[]{:S(2)}, u32[]{:S(2)}) collective-permute-start(bf16[512,512]{1,0:T(8,128)(2,1)S(1)} %get-tuple-element.153), channel_id=1, source_target_pairs={{0,2},{1,3},{2,0},{3,1},{4,6},{5,7},{6,4},{7,5},{8,10},{9,11},{10,... | collective-permute-start | bytes 1572872 | tf_op jit(solution)/shard_map/ppermute | solution.py:392
  66.2 1.3 collective-permute-start.9
  67.5 1.3 collective-permute-start.8
  68.8 4.8 %backward_0.1 = (f32[512,512]{1,0:T(8,128)S(1)}, bf16[512,512]{1,0:T(8,128)(2,1)S(1)}, bf16[512,512]{1,0:T(8,128)(2,1)S(1)}) custom-call(s32[1]{0:T(128)} %bitcast.seen_ref, bf16[8,512,512]{2,1,0:T(8,128)(2,1)S(1)} %get-tuple-element.120.p_ref, bf16[512,512]{1,0:T(8,128)(2,1)S(1)} %get-tuple-element.121.k_ref, ...), custom_call_target="tpu_custom_call" | custom-call | flops 6049999872 | bytes 1048576 | tf_op jit(solution)/shard_map/backward_0/pallas_call | solution.py:226
  73.8 10.5 %collective-permute-done.6.refs_0_ = bf16[512,512]{1,0:T(8,128)(2,1)S(1)} collective-permute-done((bf16[512,512]{1,0:T(8,128)(2,1)S(1)}, bf16[512,512]{1,0:T(8,128)(2,1)S(1)}, u32[]{:S(2)}, u32[]{:S(2)}) %collective-permute-start.6) | collective-permute-done | bytes 524320 | tf_op jit(solution)/shard_map/ppermute | solution.py:392
  84.4 2.6 %early_terms.1.refs_7_ = f32[3,512,512]{2,1,0:T(8,128)S(1)} custom-call(bf16[512,512]{1,0:T(8,128)(2,1)S(1)} %collective-permute-done.1.x_ref.refs_0_, bf16[512,512]{1,0:T(8,128)(2,1)S(1)} %either.1.x_ref.refs_1_, bf16[512,512]{1,0:T(8,128)(2,1)S(1)} %collective-permute-done.5.x_ref.refs_2_, bf16[512,512]{1,0:T(8,128)(2,1)S(1)} %collective-permute-done.2.x_ref.refs_3_, ...), custom_call_target="tpu_custom_call" | custom-call | flops 4400000000 | bytes 1048576 | tf_op jit(solution)/shard_map/early_terms/pallas_call | solution.py:308
  87.0 2.0 %weight_terms.1 = (bf16[64,16,512]{2,1,0:T(8,128)(2,1)S(1)}, bf16[64,16,512]{2,1,0:T(8,128)(2,1)S(1)}) custom-call(s32[1]{0:T(128)} %bitcast.13.core_ref, bf16[512,512]{1,0:T(8,128)(2,1)S(1)} %bitcast.32, bf16[512,512]{1,0:T(8,128)(2,1)S(1)} %collective-permute-done.x_ref.refs_1_, bf16[512,512]{1,0:T(8,128)(2,1)S(1)} %get-tuple-element.146.dk_ref.refs_2_, ...), custom_call_target="tpu_custom_call" | custom-call | flops 3849999872 | bytes 1048576 | tf_op jit(solution)/shard_map/weight_terms/pallas_call | solution.py:340
  89.1 8.6 %collective-permute-done.9.refs_3_ = bf16[512,512]{1,0:T(8,128)(2,1)S(1)} collective-permute-done((bf16[512,512]{1,0:T(8,128)(2,1)S(1)}, bf16[512,512]{1,0:T(8,128)(2,1)S(1)}, u32[]{:S(2)}, u32[]{:S(2)}) %collective-permute-start.9) | collective-permute-done | bytes 524320 | tf_op jit(solution)/shard_map/ppermute | solution.py:396
  97.6 1.7 %returned.1 = (bf16[512,512]{1,0:T(8,128)(2,1)S(1)}, f32[512,512]{1,0:T(8,128)S(1)}) custom-call(s32[2]{0:T(128)S(1)} %add_convert_fusion.flag_ref, bf16[512,512]{1,0:T(8,128)(2,1)S(1)} %get-tuple-element.149.dk_ref.refs_3_, bf16[512,512]{1,0:T(8,128)(2,1)S(1)} %get-tuple-element.150.dv_ref.refs_5_, bf16[512,512]{1,0:T(8,128)(2,1)S(1)} %get-tuple-element.89.wk_ref, ...), custom_call_target="tpu_custom_call" | custom-call | flops 22000001024 | bytes 1048576 | tf_op jit(solution)/shard_map/returned/pallas_call | solution.py:263
  100.4 1.5 %collective-permute-start.10 = (bf16[512,512]{1,0:T(8,128)(2,1)S(1)}, bf16[512,512]{1,0:T(8,128)(2,1)S(1)}, u32[]{:S(2)}, u32[]{:S(2)}) collective-permute-start(bf16[512,512]{1,0:T(8,128)(2,1)S(1)} %get-tuple-element.159), channel_id=1, source_target_pairs={{4,0},{5,1},{6,2},{7,3},{8,4},{9,5},{10,6},{11,7},{12,8},{13,9},{1... | collective-permute-start | bytes 1572872 | tf_op jit(solution)/shard_map/ppermute | solution.py:396
  101.9 1.2 sum_of.1
  103.2 19.6 %all-to-all-start = ((bf16[64,16,512]{2,1,0:T(8,128)(2,1)}), bf16[64,16,512]{2,1,0:T(8,128)(2,1)}, u32[]{:S(2)}, u32[]{:S(2)}) async-start(bf16[64,16,512]{2,1,0:T(8,128)(2,1)} %sum_of.1), calls=%async_computation | async-start | bytes 2097152 | tf_op jit(solution)/shard_map/all_to_all | solution.py:448
  129.3 2.1 %finish.1 = (bf16[512,512]{1,0:T(8,128)(2,1)}, bf16[512,512]{1,0:T(8,128)(2,1)}) custom-call(bf16[512,512]{1,0:T(8,128)(2,1)S(1)} %get-tuple-element.113.att_ref.refs_12_, bf16[512,512]{1,0:T(8,128)(2,1)S(1)} %copy-done.6, f32[512,512]{1,0:T(8,128)S(1)} %get-tuple-element.145.dq_ref.refs_6_, bf16[512,512]{1,0:T(8,128)(2,1)S(1)} %copy-done.14, ...), custom_call_target="tpu_custom_call" | custom-call | flops 44000002048 | bytes 1048576 | tf_op jit(solution)/shard_map/finish/pallas_call | solution.py:282
  131.3 7.8 %all-to-all-done = bf16[64,16,512]{2,1,0:T(8,128)(2,1)} async-done(((bf16[64,16,512]{2,1,0:T(8,128)(2,1)}), bf16[64,16,512]{2,1,0:T(8,128)(2,1)}, u32[]{:S(2)}, u32[]{:S(2)}) %all-to-all-start) | async-done | bytes 1048608 | tf_op jit(solution)/shard_map/all_to_all | solution.py:448
  139.2 1.4 convert_reduce_fusion
  (65 shorter events, 21.2 us)
Async XLA Ops:
  0.6 19.7 %collective-permute-start = (bf16[512,512]{1,0:T(8,128)(2,1)}, bf16[512,512]{1,0:T(8,128)(2,1)S(1)}, u32[]{:S(2)}, u32[]{:S(2)}) collective-permute-start(bf16[512,512]{1,0:T(8,128)(2,1)} %bitcast.25), channel_id=1, source_target_pairs={{0,4},{1,5},{2,6},{3,7},{4,8},{5,9},{6,10},{7,11},{8,12},{9,13},{1... | collective-permute-start | bytes 1572872 | tf_op jit(solution)/shard_map/ppermute | solution.py:396
  4.2 31.0 %collective-permute-start.4 = (bf16[512,512]{1,0:T(8,128)(2,1)}, bf16[512,512]{1,0:T(8,128)(2,1)S(1)}, u32[]{:S(2)}, u32[]{:S(2)}) collective-permute-start(bf16[512,512]{1,0:T(8,128)(2,1)} %bitcast.26), channel_id=1, source_target_pairs={{0,2},{1,3},{4,6},{5,7},{8,10},{9,11},{12,14},{13,15},{16,18},{17,... | collective-permute-start | bytes 1572872 | tf_op jit(solution)/shard_map/ppermute | solution.py:392
  9.3 25.7 %collective-permute-start.1 = (bf16[512,512]{1,0:T(8,128)(2,1)}, bf16[512,512]{1,0:T(8,128)(2,1)S(1)}, u32[]{:S(2)}, u32[]{:S(2)}) collective-permute-start(bf16[512,512]{1,0:T(8,128)(2,1)} %bitcast.27), channel_id=1, source_target_pairs={{0,1},{1,2},{2,3},{3,4},{4,5},{5,6},{6,7},{7,8},{8,9},{9,10},{10,1... | collective-permute-start | bytes 1572872 | tf_op jit(solution)/shard_map/ppermute | solution.py:396
  11.9 1.0 copy-start
  13.0 1.0 copy-start.1
  14.0 1.0 copy-start.2
  16.6 3.7 %copy-start.7 = (bf16[512,512]{1,0:T(8,128)(2,1)}, bf16[512,512]{1,0:T(8,128)(2,1)S(1)}, u32[]{:S(2)}) copy-start(bf16[512,512]{1,0:T(8,128)(2,1)S(1)} %get-tuple-element.148.wq_ref) | copy-start | bytes 1572868
  16.6 81.0 %copy-start.9 = (bf16[512,512]{1,0:T(8,128)(2,1)}, bf16[512,512]{1,0:T(8,128)(2,1)S(1)}, u32[]{:S(2)}) copy-start(bf16[512,512]{1,0:T(8,128)(2,1)S(1)} %get-tuple-element.89.wk_ref) | copy-start | bytes 1572868
  16.6 81.0 %copy-start.11 = (bf16[512,512]{1,0:T(8,128)(2,1)}, bf16[512,512]{1,0:T(8,128)(2,1)S(1)}, u32[]{:S(2)}) copy-start(bf16[512,512]{1,0:T(8,128)(2,1)S(1)} %get-tuple-element.90.wv_ref) | copy-start | bytes 1572868
  20.3 23.6 %collective-permute-start.3 = (bf16[512,512]{1,0:T(8,128)(2,1)S(1)}, bf16[512,512]{1,0:T(8,128)(2,1)S(1)}, u32[]{:S(2)}, u32[]{:S(2)}) collective-permute-start(bf16[512,512]{1,0:T(8,128)(2,1)S(1)} %collective-permute-done.x_ref.refs_1_), channel_id=1, source_target_pairs={{2,0},{3,1},{6,4},{7,5},{10,8},{11,9},{14,12},{15,13},{18,16},{19,... | collective-permute-start | bytes 1572872 | tf_op jit(solution)/shard_map/ppermute | solution.py:392
  21.6 32.7 %collective-permute-start.2 = (bf16[512,512]{1,0:T(8,128)(2,1)S(1)}, bf16[512,512]{1,0:T(8,128)(2,1)S(1)}, u32[]{:S(2)}, u32[]{:S(2)}) collective-permute-start(bf16[512,512]{1,0:T(8,128)(2,1)S(1)} %bitcast.30), channel_id=1, source_target_pairs={{0,16},{1,17},{2,18},{3,19},{4,20},{5,21},{6,22},{7,23},{8,24},{9,... | collective-permute-start | bytes 1572872 | tf_op jit(solution)/shard_map/ppermute | solution.py:396
  25.6 19.3 %collective-permute-start.5 = (bf16[512,512]{1,0:T(8,128)(2,1)S(1)}, bf16[512,512]{1,0:T(8,128)(2,1)S(1)}, u32[]{:S(2)}, u32[]{:S(2)}) collective-permute-start(bf16[512,512]{1,0:T(8,128)(2,1)S(1)} %bitcast.31), channel_id=1, source_target_pairs={{0,8},{1,9},{2,10},{3,11},{4,12},{5,13},{6,14},{7,15},{8,16},{9,17... | collective-permute-start | bytes 1572872 | tf_op jit(solution)/shard_map/ppermute | solution.py:396
  54.3 1.2 copy-start.6
  58.5 15.3 %collective-permute-start.7 = (bf16[512,512]{1,0:T(8,128)(2,1)S(1)}, bf16[512,512]{1,0:T(8,128)(2,1)S(1)}, u32[]{:S(2)}, u32[]{:S(2)}) collective-permute-start(bf16[512,512]{1,0:T(8,128)(2,1)S(1)} %get-tuple-element.153), channel_id=1, source_target_pairs={{0,2},{1,3},{2,0},{3,1},{4,6},{5,7},{6,4},{7,5},{8,10},{9,11},{10,... | collective-permute-start | bytes 1572872 | tf_op jit(solution)/shard_map/ppermute | solution.py:392
  64.3 20.1 %collective-permute-start.6 = (bf16[512,512]{1,0:T(8,128)(2,1)S(1)}, bf16[512,512]{1,0:T(8,128)(2,1)S(1)}, u32[]{:S(2)}, u32[]{:S(2)}) collective-permute-start(bf16[512,512]{1,0:T(8,128)(2,1)S(1)} %get-tuple-element.152), channel_id=1, source_target_pairs={{0,3},{1,0},{2,1},{3,2},{4,7},{5,4},{6,5},{7,6},{8,11},{9,8},{10,9... | collective-permute-start | bytes 1572872 | tf_op jit(solution)/shard_map/ppermute | solution.py:392
  66.2 31.4 %collective-permute-start.9 = (bf16[512,512]{1,0:T(8,128)(2,1)S(1)}, bf16[512,512]{1,0:T(8,128)(2,1)S(1)}, u32[]{:S(2)}, u32[]{:S(2)}) collective-permute-start(bf16[512,512]{1,0:T(8,128)(2,1)S(1)} %get-tuple-element.157), channel_id=1, source_target_pairs={{16,0},{17,1},{18,2},{19,3},{20,4},{21,5},{22,6},{23,7},{24,8},{25... | collective-permute-start | bytes 1572872 | tf_op jit(solution)/shard_map/ppermute | solution.py:396
  67.5 30.1 %collective-permute-start.8 = (bf16[512,512]{1,0:T(8,128)(2,1)S(1)}, bf16[512,512]{1,0:T(8,128)(2,1)S(1)}, u32[]{:S(2)}, u32[]{:S(2)}) collective-permute-start(bf16[512,512]{1,0:T(8,128)(2,1)S(1)} %get-tuple-element.156), channel_id=1, source_target_pairs={{8,0},{9,1},{10,2},{11,3},{12,4},{13,5},{14,6},{15,7},{16,8},{17,9... | collective-permute-start | bytes 1572872 | tf_op jit(solution)/shard_map/ppermute | solution.py:396
  73.6 13.4 %copy-start.13 = (bf16[512,512]{1,0:T(8,128)(2,1)}, bf16[512,512]{1,0:T(8,128)(2,1)S(1)}, u32[]{:S(2)}) copy-start(bf16[512,512]{1,0:T(8,128)(2,1)S(1)} %get-tuple-element.146.dk_ref.refs_2_) | copy-start | bytes 1572868
  73.6 13.4 %copy-start.15 = (bf16[512,512]{1,0:T(8,128)(2,1)}, bf16[512,512]{1,0:T(8,128)(2,1)S(1)}, u32[]{:S(2)}) copy-start(bf16[512,512]{1,0:T(8,128)(2,1)S(1)} %get-tuple-element.147.dv_ref.refs_4_) | copy-start | bytes 1572868
  89.0 13.0 %collective-permute-start.11 = (bf16[64,16,512]{2,1,0:T(8,128)(2,1)S(1)}, bf16[64,16,512]{2,1,0:T(8,128)(2,1)S(1)}, u32[]{:S(2)}, u32[]{:S(2)}) collective-permute-start(bf16[64,16,512]{2,1,0:T(8,128)(2,1)S(1)} %get-tuple-element.171), channel_id=1, source_target_pairs={{0,32},{32,0},{64,96},{96,64},{1,33},{33,1},{65,97},{97,65},{2,34}... | collective-permute-start | bytes 3145736 | tf_op jit(solution)/shard_map/ppermute | solution.py:445
  100.4 22.5 %collective-permute-start.10 = (bf16[512,512]{1,0:T(8,128)(2,1)S(1)}, bf16[512,512]{1,0:T(8,128)(2,1)S(1)}, u32[]{:S(2)}, u32[]{:S(2)}) collective-permute-start(bf16[512,512]{1,0:T(8,128)(2,1)S(1)} %get-tuple-element.159), channel_id=1, source_target_pairs={{4,0},{5,1},{6,2},{7,3},{8,4},{9,5},{10,6},{11,7},{12,8},{13,9},{1... | collective-permute-start | bytes 1572872 | tf_op jit(solution)/shard_map/ppermute | solution.py:396
  103.2 36.0 %all-to-all-start = ((bf16[64,16,512]{2,1,0:T(8,128)(2,1)}), bf16[64,16,512]{2,1,0:T(8,128)(2,1)}, u32[]{:S(2)}, u32[]{:S(2)}) async-start(bf16[64,16,512]{2,1,0:T(8,128)(2,1)} %sum_of.1), calls=%async_computation | async-start | bytes 2097152 | tf_op jit(solution)/shard_map/all_to_all | solution.py:448
  122.8 1.0 copy-start.8
  128.1 1.2 copy-start.18
  (8 other events, 8.3 us)

commit v5 on v4

--- a/solution.py
+++ b/solution.py
@@ -180,15 +180,14 @@
 
 
 def backward_kernel(
-    sends, seen_ref, p_ref, k_ref, v_ref, q_ref, do_ref, c_ref, delta_ref, wk_ref, wv_ref, acc_ref,
+    own, sends, seen_ref, p_ref, k_ref, v_ref, q_ref, do_ref, c_ref, delta_ref, wk_ref, wv_ref, acc_ref,
     dq_ref, dk_ref, dv_ref, *dx_refs,
 ):
     step = pl.program_id(0)
     count = p_ref.shape[0]
     seen = seen_ref[0] > 0
 
-    @pl.when(seen)
-    def _():
+    def far_block():
         grads = []
         for j in range(count):
             rows = slice(j * SIZE, (j + 1) * SIZE)
@@ -204,6 +203,35 @@
             dk_ref[out, :] = dot(scaled_q, grads[j], 1, 1).astype(BF16)
             dv_ref[out, :] = dot(scaled_do, p_ref[j], 1, 1).astype(BF16)
 
+    def own_block():
+        n = q_ref.shape[1]
+        half = n // 2
+        parts = ((0, half, half), (half, n, n))
+        grads = []
+        for j in range(count):
+            rows = slice(j * SIZE, (j + 1) * SIZE)
+            for start, stop, known in parts:
+                value_dots = dot(v_ref[rows, :known], do_ref[rows, start:stop], 0, 0)
+                delta = delta_ref[j, :, start:stop]
+                grads.append(p_ref[j, :known, start:stop] * (value_dots - delta).astype(BF16))
+        for j in range(count):
+            rows = slice(j * SIZE, (j + 1) * SIZE)
+            out = pl.ds(pl.multiple_of((step * count + j) * SIZE, SIZE), SIZE)
+            dks, dvs = [], []
+            for (start, stop, known), grad in zip(parts, grads[2 * j : 2 * j + 2]):
+                factor = c_ref[j, :, start:stop]
+                scaled_q = (q_ref[rows, start:stop].astype(F32) * factor).astype(BF16)
+                scaled_do = (do_ref[rows, start:stop].astype(F32) * factor).astype(BF16)
+                dq = dot(k_ref[rows, :known], grad, 1, 0) * factor
+                dq_ref[rows, start:stop] = acc_ref[rows, start:stop] + dq
+                dks.append(dot(scaled_q, grad, 1, 1))
+                dvs.append(dot(scaled_do, p_ref[j, :known, start:stop], 1, 1))
+            for ref, (first, second) in ((dk_ref, dks), (dv_ref, dvs)):
+                ref[out, :half] = (first + second[:, :half]).astype(BF16)
+                ref[out, half:] = second[:, half:].astype(BF16)
+
+    pl.when(seen)(own_block if own else far_block)
+
     @pl.when(jnp.logical_not(seen))
     def _():
         out = pl.ds(pl.multiple_of(step * count * SIZE, count * SIZE), count * SIZE)
@@ -224,7 +252,7 @@
     sends = block not in (0, 4)
     count = 4
     return pl.pallas_call(
-        functools.partial(backward_kernel, sends),
+        functools.partial(backward_kernel, block == 0, sends),
         grid=(HEADS // count,),
         out_shape=[
             jax.ShapeDtypeStruct((d, n), F32),
@@ -423,7 +451,7 @@
     dq = jnp.zeros((d, n), F32)
     dk, dv = {}, {}
     back = {}
-    for p in (1, 2, 8, 16, 0, 4):
+    for p in (1, 2, 16, 8, 0, 4):
         weights, _, _, _, keys, values = held[p]
         dq, dk[p], dv[p], *sent = backward(
             p, seen[p], weights, keys, values, q_t, do_t, factor[p], delta, wk_t, wv_t, dq
@@ -435,6 +463,7 @@
     dk[1], back[1], back[2] = lax.optimization_barrier((dk[1], back[1], back[2]))
     ready = (1, 2, 8, 16)
     early = early_terms([blocks[i] for i in ready], [dk[i] for i in ready], [dv[i] for i in ready], att_t, cot)
+    early, back[16] = lax.optimization_barrier((early, back[16]))
     core = lax.axis_index("dp") % 2
     kept, given = weight_terms(
         core.astype(jnp.int32).reshape(1), [x, x4], [dk[0], dk[4]], [dv[0], dv[4]], dq, early

time: 142 us -> 141 us (level)
    ppermute x7, waiting for transfers between devices: 18.3 us -> 14.7 us  [shifted(): lax.ppermute(value, 'ctx', [(i, i + step) for i in range(max(0, -step), m...]
    all_to_all x1, waiting for transfers between devices: 7.81 us -> 10.4 us  [body(): lax.all_to_all(terms, ('dp', 'ctx'), 0, 0, axis_index_groups=same_core, t...]
  transfers between devices with their start and end apart: 13 -> 13, of which waited for: 6 -> 7; matrix products, arithmetic and copies ran while one was open for 0% -> 0% of each run, Pallas kernels for 15% -> 14%
where the time goes in v5:
time: 141 us; the launch traced here: 140 us
  starting transfers between devices  55.3 us (39%)
  waiting for transfers between devices  45.5 us (32%)
  Pallas kernels  22.8 us (16%)
  local copies, waits for them, and re-layouts  13.8 us (10%)
  other arithmetic  1.48 us (1%)
    ppermute x7, starting transfers between devices, shifted(): lax.ppermute(value, 'ctx', [(i, i + step) for i in range(max(0, -step), m...  23.3 us
    ppermute x4, waiting for transfers between devices, y_ring(): return lax.ppermute(value, 'ctx', pairs)  20.4 us
    all_to_all x1, starting transfers between devices, body(): lax.all_to_all(terms, ('dp', 'ctx'), 0, 0, axis_index_groups=same_core, t...  19.7 us
    ppermute x7, waiting for transfers between devices, shifted(): lax.ppermute(value, 'ctx', [(i, i + step) for i in range(max(0, -step), m...  14.7 us
    unnamed x38, local copies, waits for them, and re-layouts  13.1 us
    ppermute x4, starting transfers between devices, y_ring(): return lax.ppermute(value, 'ctx', pairs)  12.2 us
    all_to_all x1, waiting for transfers between devices, body(): lax.all_to_all(terms, ('dp', 'ctx'), 0, 0, axis_index_groups=same_core, t...  10.4 us
    pallas_call x6, Pallas kernels, backward(): pl.pallas_call(functools.partial(backward_kernel, block == 0, sends), gri...  7.48 us
  transfers between devices with their start and end apart: 13, of which 7 were waited for; matrix products, arithmetic and copies ran while one was open for 0% of the time, Pallas kernels for 14%

profile of v5, /device:TPU:0, one launch (start us, length us, event | category | flops | bytes accessed | tf_op | source)
XLA Modules:
  0.0 140.0 jit_solution(17079712641471487128)
XLA Ops:
  0.6 3.5 %collective-permute-start = (bf16[512,512]{1,0:T(8,128)(2,1)}, bf16[512,512]{1,0:T(8,128)(2,1)S(1)}, u32[]{:S(2)}, u32[]{:S(2)}) collective-permute-start(bf16[512,512]{1,0:T(8,128)(2,1)} %bitcast.25), channel_id=1, source_target_pairs={{0,4},{1,5},{2,6},{3,7},{4,8},{5,9},{6,10},{7,11},{8,12},{9,13},{1... | collective-permute-start | bytes 1572872 | tf_op jit(solution)/shard_map/ppermute | solution.py:424
  4.2 5.1 %collective-permute-start.4 = (bf16[512,512]{1,0:T(8,128)(2,1)}, bf16[512,512]{1,0:T(8,128)(2,1)S(1)}, u32[]{:S(2)}, u32[]{:S(2)}) collective-permute-start(bf16[512,512]{1,0:T(8,128)(2,1)} %bitcast.26), channel_id=1, source_target_pairs={{0,2},{1,3},{4,6},{5,7},{8,10},{9,11},{12,14},{13,15},{16,18},{17,... | collective-permute-start | bytes 1572872 | tf_op jit(solution)/shard_map/ppermute | solution.py:420
  9.3 2.6 %collective-permute-start.1 = (bf16[512,512]{1,0:T(8,128)(2,1)}, bf16[512,512]{1,0:T(8,128)(2,1)S(1)}, u32[]{:S(2)}, u32[]{:S(2)}) collective-permute-start(bf16[512,512]{1,0:T(8,128)(2,1)} %bitcast.27), channel_id=1, source_target_pairs={{0,1},{1,2},{2,3},{3,4},{4,5},{5,6},{6,7},{7,8},{8,9},{9,10},{10,1... | collective-permute-start | bytes 1572872 | tf_op jit(solution)/shard_map/ppermute | solution.py:424
  17.2 3.1 %forward_0.1 = (bf16[8,512,512]{2,1,0:T(8,128)(2,1)S(1)}, f32[8,1,512]{2,1,0:T(1,128)S(1)}, f32[8,1,512]{2,1,0:T(1,128)S(1)}, f32[512,512]{1,0:T(8,128)S(1)}, bf...) custom-call(s32[1]{0:T(128)} %bitcast.seen_ref, bf16[512,512]{1,0:T(8,128)(2,1)S(1)} %bitcast.29, ...), custom_call_target="tpu_custom_call" | custom-call | flops 4950000128 | bytes 1048576 | tf_op jit(solution)/shard_map/forward_0/pallas_call | solution.py:115
  20.3 1.3 collective-permute-start.3
  21.6 3.8 %collective-permute-start.2 = (bf16[512,512]{1,0:T(8,128)(2,1)S(1)}, bf16[512,512]{1,0:T(8,128)(2,1)S(1)}, u32[]{:S(2)}, u32[]{:S(2)}) collective-permute-start(bf16[512,512]{1,0:T(8,128)(2,1)S(1)} %bitcast.30), channel_id=1, source_target_pairs={{0,16},{1,17},{2,18},{3,19},{4,20},{5,21},{6,22},{7,23},{8,24},{9,... | collective-permute-start | bytes 1572872 | tf_op jit(solution)/shard_map/ppermute | solution.py:424
  25.6 9.3 %collective-permute-start.5 = (bf16[512,512]{1,0:T(8,128)(2,1)S(1)}, bf16[512,512]{1,0:T(8,128)(2,1)S(1)}, u32[]{:S(2)}, u32[]{:S(2)}) collective-permute-start(bf16[512,512]{1,0:T(8,128)(2,1)S(1)} %bitcast.31), channel_id=1, source_target_pairs={{0,8},{1,9},{2,10},{3,11},{4,12},{5,13},{6,14},{7,15},{8,16},{9,17... | collective-permute-start | bytes 1572872 | tf_op jit(solution)/shard_map/ppermute | solution.py:424
  35.2 8.8 %collective-permute-done.3.first_ref = bf16[512,512]{1,0:T(8,128)(2,1)S(1)} collective-permute-done((bf16[512,512]{1,0:T(8,128)(2,1)S(1)}, bf16[512,512]{1,0:T(8,128)(2,1)S(1)}, u32[]{:S(2)}, u32[]{:S(2)}) %collective-permute-start.3) | collective-permute-done | bytes 524320 | tf_op jit(solution)/shard_map/ppermute | solution.py:420
  45.1 9.2 %collective-permute-done.2.x_ref.refs_3_ = bf16[512,512]{1,0:T(8,128)(2,1)S(1)} collective-permute-done((bf16[512,512]{1,0:T(8,128)(2,1)S(1)}, bf16[512,512]{1,0:T(8,128)(2,1)S(1)}, u32[]{:S(2)}, u32[]{:S(2)}) %collective-permute-start.2) | collective-permute-done | bytes 524320 | tf_op jit(solution)/shard_map/ppermute | solution.py:424
  58.5 5.8 %collective-permute-start.7 = (bf16[512,512]{1,0:T(8,128)(2,1)S(1)}, bf16[512,512]{1,0:T(8,128)(2,1)S(1)}, u32[]{:S(2)}, u32[]{:S(2)}) collective-permute-start(bf16[512,512]{1,0:T(8,128)(2,1)S(1)} %get-tuple-element.155), channel_id=1, source_target_pairs={{0,2},{1,3},{2,0},{3,1},{4,6},{5,7},{6,4},{7,5},{8,10},{9,11},{10,... | collective-permute-start | bytes 1572872 | tf_op jit(solution)/shard_map/ppermute | solution.py:420
  65.2 1.5 %collective-permute-start.9 = (bf16[512,512]{1,0:T(8,128)(2,1)S(1)}, bf16[512,512]{1,0:T(8,128)(2,1)S(1)}, u32[]{:S(2)}, u32[]{:S(2)}) collective-permute-start(bf16[512,512]{1,0:T(8,128)(2,1)S(1)} %get-tuple-element.167), channel_id=1, source_target_pairs={{16,0},{17,1},{18,2},{19,3},{20,4},{21,5},{22,6},{23,7},{24,8},{25... | collective-permute-start | bytes 1572872 | tf_op jit(solution)/shard_map/ppermute | solution.py:424
  67.7 1.3 collective-permute-start.8
  69.0 3.4 %backward_0.1 = (f32[512,512]{1,0:T(8,128)S(1)}, bf16[512,512]{1,0:T(8,128)(2,1)S(1)}, bf16[512,512]{1,0:T(8,128)(2,1)S(1)}) custom-call(s32[1]{0:T(128)} %bitcast.seen_ref, bf16[8,512,512]{2,1,0:T(8,128)(2,1)S(1)} %get-tuple-element.122.p_ref, bf16[512,512]{1,0:T(8,128)(2,1)S(1)} %get-tuple-element.123.k_ref, ...), custom_call_target="tpu_custom_call" | custom-call | flops 6049999872 | bytes 1048576 | tf_op jit(solution)/shard_map/backward_0/pallas_call | solution.py:254
  73.0 11.3 %collective-permute-done.6.refs_0_ = bf16[512,512]{1,0:T(8,128)(2,1)S(1)} collective-permute-done((bf16[512,512]{1,0:T(8,128)(2,1)S(1)}, bf16[512,512]{1,0:T(8,128)(2,1)S(1)}, u32[]{:S(2)}, u32[]{:S(2)}) %collective-permute-start.6) | collective-permute-done | bytes 524320 | tf_op jit(solution)/shard_map/ppermute | solution.py:420
  84.3 2.6 %early_terms.1.refs_7_ = f32[3,512,512]{2,1,0:T(8,128)S(1)} custom-call(bf16[512,512]{1,0:T(8,128)(2,1)S(1)} %collective-permute-done.1.x_ref.refs_0_, bf16[512,512]{1,0:T(8,128)(2,1)S(1)} %either.1.x_ref.refs_1_, bf16[512,512]{1,0:T(8,128)(2,1)S(1)} %collective-permute-done.5.x_ref.refs_2_, bf16[512,512]{1,0:T(8,128)(2,1)S(1)} %collective-permute-done.2.x_ref.refs_3_, ...), custom_call_target="tpu_custom_call" | custom-call | flops 4400000000 | bytes 1048576 | tf_op jit(solution)/shard_map/early_terms/pallas_call | solution.py:336
  86.9 5.0 %collective-permute-done.9.refs_3_ = bf16[512,512]{1,0:T(8,128)(2,1)S(1)} collective-permute-done((bf16[512,512]{1,0:T(8,128)(2,1)S(1)}, bf16[512,512]{1,0:T(8,128)(2,1)S(1)}, u32[]{:S(2)}, u32[]{:S(2)}) %collective-permute-start.9) | collective-permute-done | bytes 524320 | tf_op jit(solution)/shard_map/ppermute | solution.py:424
  91.9 2.0 %weight_terms.1 = (bf16[64,16,512]{2,1,0:T(8,128)(2,1)S(1)}, bf16[64,16,512]{2,1,0:T(8,128)(2,1)S(1)}) custom-call(s32[1]{0:T(128)} %bitcast.13.core_ref, bf16[512,512]{1,0:T(8,128)(2,1)S(1)} %bitcast.32, bf16[512,512]{1,0:T(8,128)(2,1)S(1)} %collective-permute-done.x_ref.refs_1_, bf16[512,512]{1,0:T(8,128)(2,1)S(1)} %get-tuple-element.148.dk_ref.refs_2_, ...), custom_call_target="tpu_custom_call" | custom-call | flops 3849999872 | bytes 1048576 | tf_op jit(solution)/shard_map/weight_terms/pallas_call | solution.py:368
  94.0 1.7 %returned.1 = (bf16[512,512]{1,0:T(8,128)(2,1)S(1)}, f32[512,512]{1,0:T(8,128)S(1)}) custom-call(s32[2]{0:T(128)S(1)} %add_convert_fusion.flag_ref, bf16[512,512]{1,0:T(8,128)(2,1)S(1)} %get-tuple-element.151.dk_ref.refs_3_, bf16[512,512]{1,0:T(8,128)(2,1)S(1)} %get-tuple-element.152.dv_ref.refs_5_, bf16[512,512]{1,0:T(8,128)(2,1)S(1)} %get-tuple-element.91.wk_ref, ...), custom_call_target="tpu_custom_call" | custom-call | flops 22000001024 | bytes 1048576 | tf_op jit(solution)/shard_map/returned/pallas_call | solution.py:291
  96.8 1.3 collective-permute-start.10
  98.1 1.2 sum_of.1
  99.3 19.7 %all-to-all-start = ((bf16[64,16,512]{2,1,0:T(8,128)(2,1)}), bf16[64,16,512]{2,1,0:T(8,128)(2,1)}, u32[]{:S(2)}, u32[]{:S(2)}) async-start(bf16[64,16,512]{2,1,0:T(8,128)(2,1)} %sum_of.1), calls=%async_computation | async-start | bytes 2097152 | tf_op jit(solution)/shard_map/all_to_all | solution.py:477
  125.5 2.1 %finish.1 = (bf16[512,512]{1,0:T(8,128)(2,1)}, bf16[512,512]{1,0:T(8,128)(2,1)}) custom-call(bf16[512,512]{1,0:T(8,128)(2,1)S(1)} %get-tuple-element.115.refs_12_.att_ref, bf16[512,512]{1,0:T(8,128)(2,1)S(1)} %copy-done.6, f32[512,512]{1,0:T(8,128)S(1)} %get-tuple-element.147.dq_ref.refs_6_, bf16[512,512]{1,0:T(8,128)(2,1)S(1)} %copy-done.14, ...), custom_call_target="tpu_custom_call" | custom-call | flops 44000002048 | bytes 1048576 | tf_op jit(solution)/shard_map/finish/pallas_call | solution.py:310
  127.6 10.4 %all-to-all-done = bf16[64,16,512]{2,1,0:T(8,128)(2,1)} async-done(((bf16[64,16,512]{2,1,0:T(8,128)(2,1)}), bf16[64,16,512]{2,1,0:T(8,128)(2,1)}, u32[]{:S(2)}, u32[]{:S(2)}) %all-to-all-start) | async-done | bytes 1048608 | tf_op jit(solution)/shard_map/all_to_all | solution.py:477
  138.0 1.4 %convert_reduce_fusion = f32[16,512]{1,0:T(8,128)S(1)} fusion(bf16[64,16,512]{2,1,0:T(8,128)(2,1)} %all-to-all-done), kind=kLoop, calls=%fused_computation | loop fusion | flops 1040384 | bytes 1081344 | tf_op jit(solution)/shard_map/reduce_sum | solution.py:478
  (65 shorter events, 21.5 us)
Async XLA Ops:
  0.6 19.7 %collective-permute-start = (bf16[512,512]{1,0:T(8,128)(2,1)}, bf16[512,512]{1,0:T(8,128)(2,1)S(1)}, u32[]{:S(2)}, u32[]{:S(2)}) collective-permute-start(bf16[512,512]{1,0:T(8,128)(2,1)} %bitcast.25), channel_id=1, source_target_pairs={{0,4},{1,5},{2,6},{3,7},{4,8},{5,9},{6,10},{7,11},{8,12},{9,13},{1... | collective-permute-start | bytes 1572872 | tf_op jit(solution)/shard_map/ppermute | solution.py:424
  4.2 31.0 %collective-permute-start.4 = (bf16[512,512]{1,0:T(8,128)(2,1)}, bf16[512,512]{1,0:T(8,128)(2,1)S(1)}, u32[]{:S(2)}, u32[]{:S(2)}) collective-permute-start(bf16[512,512]{1,0:T(8,128)(2,1)} %bitcast.26), channel_id=1, source_target_pairs={{0,2},{1,3},{4,6},{5,7},{8,10},{9,11},{12,14},{13,15},{16,18},{17,... | collective-permute-start | bytes 1572872 | tf_op jit(solution)/shard_map/ppermute | solution.py:420
  9.3 25.7 %collective-permute-start.1 = (bf16[512,512]{1,0:T(8,128)(2,1)}, bf16[512,512]{1,0:T(8,128)(2,1)S(1)}, u32[]{:S(2)}, u32[]{:S(2)}) collective-permute-start(bf16[512,512]{1,0:T(8,128)(2,1)} %bitcast.27), channel_id=1, source_target_pairs={{0,1},{1,2},{2,3},{3,4},{4,5},{5,6},{6,7},{7,8},{8,9},{9,10},{10,1... | collective-permute-start | bytes 1572872 | tf_op jit(solution)/shard_map/ppermute | solution.py:424
  11.9 1.0 copy-start
  13.0 1.0 copy-start.1
  14.0 1.0 copy-start.2
  16.6 3.7 %copy-start.7 = (bf16[512,512]{1,0:T(8,128)(2,1)}, bf16[512,512]{1,0:T(8,128)(2,1)S(1)}, u32[]{:S(2)}) copy-start(bf16[512,512]{1,0:T(8,128)(2,1)S(1)} %get-tuple-element.150.wq_ref) | copy-start | bytes 1572868
  16.6 77.4 %copy-start.9 = (bf16[512,512]{1,0:T(8,128)(2,1)}, bf16[512,512]{1,0:T(8,128)(2,1)S(1)}, u32[]{:S(2)}) copy-start(bf16[512,512]{1,0:T(8,128)(2,1)S(1)} %get-tuple-element.91.wk_ref) | copy-start | bytes 1572868
  16.6 77.4 %copy-start.11 = (bf16[512,512]{1,0:T(8,128)(2,1)}, bf16[512,512]{1,0:T(8,128)(2,1)S(1)}, u32[]{:S(2)}) copy-start(bf16[512,512]{1,0:T(8,128)(2,1)S(1)} %get-tuple-element.92.wv_ref) | copy-start | bytes 1572868
  20.3 23.6 %collective-permute-start.3 = (bf16[512,512]{1,0:T(8,128)(2,1)S(1)}, bf16[512,512]{1,0:T(8,128)(2,1)S(1)}, u32[]{:S(2)}, u32[]{:S(2)}) collective-permute-start(bf16[512,512]{1,0:T(8,128)(2,1)S(1)} %collective-permute-done.x_ref.refs_1_), channel_id=1, source_target_pairs={{2,0},{3,1},{6,4},{7,5},{10,8},{11,9},{14,12},{15,13},{18,16},{19,... | collective-permute-start | bytes 1572872 | tf_op jit(solution)/shard_map/ppermute | solution.py:420
  21.6 32.7 %collective-permute-start.2 = (bf16[512,512]{1,0:T(8,128)(2,1)S(1)}, bf16[512,512]{1,0:T(8,128)(2,1)S(1)}, u32[]{:S(2)}, u32[]{:S(2)}) collective-permute-start(bf16[512,512]{1,0:T(8,128)(2,1)S(1)} %bitcast.30), channel_id=1, source_target_pairs={{0,16},{1,17},{2,18},{3,19},{4,20},{5,21},{6,22},{7,23},{8,24},{9,... | collective-permute-start | bytes 1572872 | tf_op jit(solution)/shard_map/ppermute | solution.py:424
  25.6 19.3 %collective-permute-start.5 = (bf16[512,512]{1,0:T(8,128)(2,1)S(1)}, bf16[512,512]{1,0:T(8,128)(2,1)S(1)}, u32[]{:S(2)}, u32[]{:S(2)}) collective-permute-start(bf16[512,512]{1,0:T(8,128)(2,1)S(1)} %bitcast.31), channel_id=1, source_target_pairs={{0,8},{1,9},{2,10},{3,11},{4,12},{5,13},{6,14},{7,15},{8,16},{9,17... | collective-permute-start | bytes 1572872 | tf_op jit(solution)/shard_map/ppermute | solution.py:424
  54.3 1.2 copy-start.6
  58.5 14.5 %collective-permute-start.7 = (bf16[512,512]{1,0:T(8,128)(2,1)S(1)}, bf16[512,512]{1,0:T(8,128)(2,1)S(1)}, u32[]{:S(2)}, u32[]{:S(2)}) collective-permute-start(bf16[512,512]{1,0:T(8,128)(2,1)S(1)} %get-tuple-element.155), channel_id=1, source_target_pairs={{0,2},{1,3},{2,0},{3,1},{4,6},{5,7},{6,4},{7,5},{8,10},{9,11},{10,... | collective-permute-start | bytes 1572872 | tf_op jit(solution)/shard_map/ppermute | solution.py:420
  64.3 20.0 %collective-permute-start.6 = (bf16[512,512]{1,0:T(8,128)(2,1)S(1)}, bf16[512,512]{1,0:T(8,128)(2,1)S(1)}, u32[]{:S(2)}, u32[]{:S(2)}) collective-permute-start(bf16[512,512]{1,0:T(8,128)(2,1)S(1)} %get-tuple-element.154), channel_id=1, source_target_pairs={{0,3},{1,0},{2,1},{3,2},{4,7},{5,4},{6,5},{7,6},{8,11},{9,8},{10,9... | collective-permute-start | bytes 1572872 | tf_op jit(solution)/shard_map/ppermute | solution.py:420
  65.2 26.7 %collective-permute-start.9 = (bf16[512,512]{1,0:T(8,128)(2,1)S(1)}, bf16[512,512]{1,0:T(8,128)(2,1)S(1)}, u32[]{:S(2)}, u32[]{:S(2)}) collective-permute-start(bf16[512,512]{1,0:T(8,128)(2,1)S(1)} %get-tuple-element.167), channel_id=1, source_target_pairs={{16,0},{17,1},{18,2},{19,3},{20,4},{21,5},{22,6},{23,7},{24,8},{25... | collective-permute-start | bytes 1572872 | tf_op jit(solution)/shard_map/ppermute | solution.py:424
  67.7 26.3 %collective-permute-start.8 = (bf16[512,512]{1,0:T(8,128)(2,1)S(1)}, bf16[512,512]{1,0:T(8,128)(2,1)S(1)}, u32[]{:S(2)}, u32[]{:S(2)}) collective-permute-start(bf16[512,512]{1,0:T(8,128)(2,1)S(1)} %get-tuple-element.158), channel_id=1, source_target_pairs={{8,0},{9,1},{10,2},{11,3},{12,4},{13,5},{14,6},{15,7},{16,8},{17,9... | collective-permute-start | bytes 1572872 | tf_op jit(solution)/shard_map/ppermute | solution.py:424
  72.5 19.5 %copy-start.13 = (bf16[512,512]{1,0:T(8,128)(2,1)}, bf16[512,512]{1,0:T(8,128)(2,1)S(1)}, u32[]{:S(2)}) copy-start(bf16[512,512]{1,0:T(8,128)(2,1)S(1)} %get-tuple-element.148.dk_ref.refs_2_) | copy-start | bytes 1572868
  72.5 19.4 %copy-start.15 = (bf16[512,512]{1,0:T(8,128)(2,1)}, bf16[512,512]{1,0:T(8,128)(2,1)S(1)}, u32[]{:S(2)}) copy-start(bf16[512,512]{1,0:T(8,128)(2,1)S(1)} %get-tuple-element.149.dv_ref.refs_4_) | copy-start | bytes 1572868
  93.9 4.2 %collective-permute-start.11 = (bf16[64,16,512]{2,1,0:T(8,128)(2,1)S(1)}, bf16[64,16,512]{2,1,0:T(8,128)(2,1)S(1)}, u32[]{:S(2)}, u32[]{:S(2)}) collective-permute-start(bf16[64,16,512]{2,1,0:T(8,128)(2,1)S(1)} %get-tuple-element.175), channel_id=1, source_target_pairs={{0,32},{32,0},{64,96},{96,64},{1,33},{33,1},{65,97},{97,65},{2,34}... | collective-permute-start | bytes 3145736 | tf_op jit(solution)/shard_map/ppermute | solution.py:474
  96.8 22.3 %collective-permute-start.10 = (bf16[512,512]{1,0:T(8,128)(2,1)S(1)}, bf16[512,512]{1,0:T(8,128)(2,1)S(1)}, u32[]{:S(2)}, u32[]{:S(2)}) collective-permute-start(bf16[512,512]{1,0:T(8,128)(2,1)S(1)} %get-tuple-element.170), channel_id=1, source_target_pairs={{4,0},{5,1},{6,2},{7,3},{8,4},{9,5},{10,6},{11,7},{12,8},{13,9},{1... | collective-permute-start | bytes 1572872 | tf_op jit(solution)/shard_map/ppermute | solution.py:424
  99.3 38.6 %all-to-all-start = ((bf16[64,16,512]{2,1,0:T(8,128)(2,1)}), bf16[64,16,512]{2,1,0:T(8,128)(2,1)}, u32[]{:S(2)}, u32[]{:S(2)}) async-start(bf16[64,16,512]{2,1,0:T(8,128)(2,1)} %sum_of.1), calls=%async_computation | async-start | bytes 2097152 | tf_op jit(solution)/shard_map/all_to_all | solution.py:477
  119.1 1.0 copy-start.8
  124.3 1.2 copy-start.18
  (8 other events, 8.3 us)

commit v6 on v5

--- a/solution.py
+++ b/solution.py
@@ -283,14 +283,15 @@
     sent_ref[...] = total.astype(BF16)
     kept = eight[...].astype(F32) + sixteen[...].astype(F32)
     kept = kept + jnp.where(flag_ref[0] > 0, 0, one[...]).astype(F32)
-    sum_ref[...] = kept + jnp.where(flag_ref[1] > 0, 0, two[...]).astype(F32)
+    kept = kept + jnp.where(flag_ref[1] > 0, 0, two[...]).astype(F32)
+    sum_ref[...] = kept.astype(BF16)
 
 
 def returned(flags, dk, dv, wk_t, wv_t, *backs):
     d, n = dk.shape
     return pl.pallas_call(
         returned_kernel,
-        out_shape=(jax.ShapeDtypeStruct((n, d), BF16), jax.ShapeDtypeStruct((n, d), F32)),
+        out_shape=(jax.ShapeDtypeStruct((n, d), BF16),) * 2,
         in_specs=[SCALAR] + [pl.BlockSpec(memory_space=pltpu.VMEM)] * 8,
         compiler_params=params(10),
         cost_estimate=cost(20),
@@ -302,7 +303,7 @@
     out_ref[...] = dot(att_ref[...], wo_ref[...], 0, 0).astype(BF16)
     total = dot((dq_ref[...] * 0.125).astype(BF16), wq_ref[...], 0, 0)
     total = total + dot(dk_ref[...], wk_ref[...], 0, 0) + dot(dv_ref[...], wv_ref[...], 0, 0)
-    grad_ref[...] = (total + sum_ref[...] + four[...].astype(F32)).astype(BF16)
+    grad_ref[...] = (total + sum_ref[...].astype(F32) + four[...].astype(F32)).astype(BF16)
 
 
 def finish(att_t, w_out, dq, dk, dv, wq_t, wk_t, wv_t, total, four):

time: 141 us -> 141 us (level)
  no operation moved by 1% of the time
where the time goes in v6:
time: 141 us; the launch traced here: 140 us
  starting transfers between devices  55.3 us (39%)
  waiting for transfers between devices  45.7 us (32%)
  Pallas kernels  22.9 us (16%)
  local copies, waits for them, and re-layouts  13.4 us (10%)
  other arithmetic  1.48 us (1%)
    ppermute x7, starting transfers between devices, shifted(): lax.ppermute(value, 'ctx', [(i, i + step) for i in range(max(0, -step), m...  23.3 us
    ppermute x4, waiting for transfers between devices, y_ring(): return lax.ppermute(value, 'ctx', pairs)  20.4 us
    all_to_all x1, starting transfers between devices, body(): lax.all_to_all(terms, ('dp', 'ctx'), 0, 0, axis_index_groups=same_core, t...  19.7 us
    ppermute x7, waiting for transfers between devices, shifted(): lax.ppermute(value, 'ctx', [(i, i + step) for i in range(max(0, -step), m...  14.7 us
    unnamed x38, local copies, waits for them, and re-layouts  12.7 us
    ppermute x4, starting transfers between devices, y_ring(): return lax.ppermute(value, 'ctx', pairs)  12.2 us
    all_to_all x1, waiting for transfers between devices, body(): lax.all_to_all(terms, ('dp', 'ctx'), 0, 0, axis_index_groups=same_core, t...  10.6 us
    pallas_call x6, Pallas kernels, backward(): pl.pallas_call(functools.partial(backward_kernel, block == 0, sends), gri...  7.48 us
  transfers between devices with their start and end apart: 13, of which 7 were waited for; matrix products, arithmetic and copies ran while one was open for 0% of the time, Pallas kernels for 14%

profile of v6, /device:TPU:0, one launch (start us, length us, event | category | flops | bytes accessed | tf_op | source)
XLA Modules:
  0.0 139.9 jit_solution(10985537465751785054)
XLA Ops:
  0.6 3.5 %collective-permute-start = (bf16[512,512]{1,0:T(8,128)(2,1)}, bf16[512,512]{1,0:T(8,128)(2,1)S(1)}, u32[]{:S(2)}, u32[]{:S(2)}) collective-permute-start(bf16[512,512]{1,0:T(8,128)(2,1)} %bitcast.25), channel_id=1, source_target_pairs={{0,4},{1,5},{2,6},{3,7},{4,8},{5,9},{6,10},{7,11},{8,12},{9,13},{1... | collective-permute-start | bytes 1572872 | tf_op jit(solution)/shard_map/ppermute | solution.py:425
  4.2 5.1 %collective-permute-start.4 = (bf16[512,512]{1,0:T(8,128)(2,1)}, bf16[512,512]{1,0:T(8,128)(2,1)S(1)}, u32[]{:S(2)}, u32[]{:S(2)}) collective-permute-start(bf16[512,512]{1,0:T(8,128)(2,1)} %bitcast.26), channel_id=1, source_target_pairs={{0,2},{1,3},{4,6},{5,7},{8,10},{9,11},{12,14},{13,15},{16,18},{17,... | collective-permute-start | bytes 1572872 | tf_op jit(solution)/shard_map/ppermute | solution.py:421
  9.3 2.6 %collective-permute-start.1 = (bf16[512,512]{1,0:T(8,128)(2,1)}, bf16[512,512]{1,0:T(8,128)(2,1)S(1)}, u32[]{:S(2)}, u32[]{:S(2)}) collective-permute-start(bf16[512,512]{1,0:T(8,128)(2,1)} %bitcast.27), channel_id=1, source_target_pairs={{0,1},{1,2},{2,3},{3,4},{4,5},{5,6},{6,7},{7,8},{8,9},{9,10},{10,1... | collective-permute-start | bytes 1572872 | tf_op jit(solution)/shard_map/ppermute | solution.py:425
  17.2 3.1 %forward_0.1 = (bf16[8,512,512]{2,1,0:T(8,128)(2,1)S(1)}, f32[8,1,512]{2,1,0:T(1,128)S(1)}, f32[8,1,512]{2,1,0:T(1,128)S(1)}, f32[512,512]{1,0:T(8,128)S(1)}, bf...) custom-call(s32[1]{0:T(128)} %bitcast.seen_ref, bf16[512,512]{1,0:T(8,128)(2,1)S(1)} %bitcast.29, ...), custom_call_target="tpu_custom_call" | custom-call | flops 4950000128 | bytes 1048576 | tf_op jit(solution)/shard_map/forward_0/pallas_call | solution.py:115
  20.3 1.3 collective-permute-start.3
  21.6 3.8 %collective-permute-start.2 = (bf16[512,512]{1,0:T(8,128)(2,1)S(1)}, bf16[512,512]{1,0:T(8,128)(2,1)S(1)}, u32[]{:S(2)}, u32[]{:S(2)}) collective-permute-start(bf16[512,512]{1,0:T(8,128)(2,1)S(1)} %bitcast.30), channel_id=1, source_target_pairs={{0,16},{1,17},{2,18},{3,19},{4,20},{5,21},{6,22},{7,23},{8,24},{9,... | collective-permute-start | bytes 1572872 | tf_op jit(solution)/shard_map/ppermute | solution.py:425
  25.6 9.3 %collective-permute-start.5 = (bf16[512,512]{1,0:T(8,128)(2,1)S(1)}, bf16[512,512]{1,0:T(8,128)(2,1)S(1)}, u32[]{:S(2)}, u32[]{:S(2)}) collective-permute-start(bf16[512,512]{1,0:T(8,128)(2,1)S(1)} %bitcast.31), channel_id=1, source_target_pairs={{0,8},{1,9},{2,10},{3,11},{4,12},{5,13},{6,14},{7,15},{8,16},{9,17... | collective-permute-start | bytes 1572872 | tf_op jit(solution)/shard_map/ppermute | solution.py:425
  35.2 8.8 %collective-permute-done.3.first_ref = bf16[512,512]{1,0:T(8,128)(2,1)S(1)} collective-permute-done((bf16[512,512]{1,0:T(8,128)(2,1)S(1)}, bf16[512,512]{1,0:T(8,128)(2,1)S(1)}, u32[]{:S(2)}, u32[]{:S(2)}) %collective-permute-start.3) | collective-permute-done | bytes 524320 | tf_op jit(solution)/shard_map/ppermute | solution.py:421
  45.1 9.2 %collective-permute-done.2.x_ref.refs_3_ = bf16[512,512]{1,0:T(8,128)(2,1)S(1)} collective-permute-done((bf16[512,512]{1,0:T(8,128)(2,1)S(1)}, bf16[512,512]{1,0:T(8,128)(2,1)S(1)}, u32[]{:S(2)}, u32[]{:S(2)}) %collective-permute-start.2) | collective-permute-done | bytes 524320 | tf_op jit(solution)/shard_map/ppermute | solution.py:425
  58.5 5.8 %collective-permute-start.7 = (bf16[512,512]{1,0:T(8,128)(2,1)S(1)}, bf16[512,512]{1,0:T(8,128)(2,1)S(1)}, u32[]{:S(2)}, u32[]{:S(2)}) collective-permute-start(bf16[512,512]{1,0:T(8,128)(2,1)S(1)} %get-tuple-element.155), channel_id=1, source_target_pairs={{0,2},{1,3},{2,0},{3,1},{4,6},{5,7},{6,4},{7,5},{8,10},{9,11},{10,... | collective-permute-start | bytes 1572872 | tf_op jit(solution)/shard_map/ppermute | solution.py:421
  65.2 1.5 %collective-permute-start.9 = (bf16[512,512]{1,0:T(8,128)(2,1)S(1)}, bf16[512,512]{1,0:T(8,128)(2,1)S(1)}, u32[]{:S(2)}, u32[]{:S(2)}) collective-permute-start(bf16[512,512]{1,0:T(8,128)(2,1)S(1)} %get-tuple-element.167), channel_id=1, source_target_pairs={{16,0},{17,1},{18,2},{19,3},{20,4},{21,5},{22,6},{23,7},{24,8},{25... | collective-permute-start | bytes 1572872 | tf_op jit(solution)/shard_map/ppermute | solution.py:425
  67.7 1.3 collective-permute-start.8
  69.0 3.4 %backward_0.1 = (f32[512,512]{1,0:T(8,128)S(1)}, bf16[512,512]{1,0:T(8,128)(2,1)S(1)}, bf16[512,512]{1,0:T(8,128)(2,1)S(1)}) custom-call(s32[1]{0:T(128)} %bitcast.seen_ref, bf16[8,512,512]{2,1,0:T(8,128)(2,1)S(1)} %get-tuple-element.122.p_ref, bf16[512,512]{1,0:T(8,128)(2,1)S(1)} %get-tuple-element.123.k_ref, ...), custom_call_target="tpu_custom_call" | custom-call | flops 6049999872 | bytes 1048576 | tf_op jit(solution)/shard_map/backward_0/pallas_call | solution.py:254
  73.0 11.3 %collective-permute-done.6.refs_0_ = bf16[512,512]{1,0:T(8,128)(2,1)S(1)} collective-permute-done((bf16[512,512]{1,0:T(8,128)(2,1)S(1)}, bf16[512,512]{1,0:T(8,128)(2,1)S(1)}, u32[]{:S(2)}, u32[]{:S(2)}) %collective-permute-start.6) | collective-permute-done | bytes 524320 | tf_op jit(solution)/shard_map/ppermute | solution.py:421
  84.3 2.6 %early_terms.1.refs_7_ = f32[3,512,512]{2,1,0:T(8,128)S(1)} custom-call(bf16[512,512]{1,0:T(8,128)(2,1)S(1)} %collective-permute-done.1.x_ref.refs_0_, bf16[512,512]{1,0:T(8,128)(2,1)S(1)} %either.1.x_ref.refs_1_, bf16[512,512]{1,0:T(8,128)(2,1)S(1)} %collective-permute-done.5.x_ref.refs_2_, bf16[512,512]{1,0:T(8,128)(2,1)S(1)} %collective-permute-done.2.x_ref.refs_3_, ...), custom_call_target="tpu_custom_call" | custom-call | flops 4400000000 | bytes 1048576 | tf_op jit(solution)/shard_map/early_terms/pallas_call | solution.py:337
  86.9 5.0 %collective-permute-done.9.refs_3_ = bf16[512,512]{1,0:T(8,128)(2,1)S(1)} collective-permute-done((bf16[512,512]{1,0:T(8,128)(2,1)S(1)}, bf16[512,512]{1,0:T(8,128)(2,1)S(1)}, u32[]{:S(2)}, u32[]{:S(2)}) %collective-permute-start.9) | collective-permute-done | bytes 524320 | tf_op jit(solution)/shard_map/ppermute | solution.py:425
  91.9 2.0 %weight_terms.1 = (bf16[64,16,512]{2,1,0:T(8,128)(2,1)S(1)}, bf16[64,16,512]{2,1,0:T(8,128)(2,1)S(1)}) custom-call(s32[1]{0:T(128)} %bitcast.13.core_ref, bf16[512,512]{1,0:T(8,128)(2,1)S(1)} %bitcast.32, bf16[512,512]{1,0:T(8,128)(2,1)S(1)} %collective-permute-done.x_ref.refs_1_, bf16[512,512]{1,0:T(8,128)(2,1)S(1)} %get-tuple-element.148.dk_ref.refs_2_, ...), custom_call_target="tpu_custom_call" | custom-call | flops 3849999872 | bytes 1048576 | tf_op jit(solution)/shard_map/weight_terms/pallas_call | solution.py:369
  94.0 1.8 %returned.1 = (bf16[512,512]{1,0:T(8,128)(2,1)S(1)}, bf16[512,512]{1,0:T(8,128)(2,1)S(1)}) custom-call(s32[2]{0:T(128)S(1)} %add_convert_fusion.flag_ref, bf16[512,512]{1,0:T(8,128)(2,1)S(1)} %get-tuple-element.151.dk_ref.refs_3_, bf16[512,512]{1,0:T(8,128)(2,1)S(1)} %get-tuple-element.152.dv_ref.refs_5_, bf16[512,512]{1,0:T(8,128)(2,1)S(1)} %get-tuple-element.91.wk_ref, ...), custom_call_target="tpu_custom_call" | custom-call | flops 22000001024 | bytes 1048576 | tf_op jit(solution)/shard_map/returned/pallas_call | solution.py:292
  96.7 1.3 collective-permute-start.10
  98.0 1.3 sum_of.1
  99.2 19.7 %all-to-all-start = ((bf16[64,16,512]{2,1,0:T(8,128)(2,1)}), bf16[64,16,512]{2,1,0:T(8,128)(2,1)}, u32[]{:S(2)}, u32[]{:S(2)}) async-start(bf16[64,16,512]{2,1,0:T(8,128)(2,1)} %sum_of.1), calls=%async_computation | async-start | bytes 2097152 | tf_op jit(solution)/shard_map/all_to_all | solution.py:478
  125.2 2.1 %finish.1 = (bf16[512,512]{1,0:T(8,128)(2,1)}, bf16[512,512]{1,0:T(8,128)(2,1)}) custom-call(bf16[512,512]{1,0:T(8,128)(2,1)S(1)} %get-tuple-element.115.refs_12_.att_ref, bf16[512,512]{1,0:T(8,128)(2,1)S(1)} %copy-done.6, f32[512,512]{1,0:T(8,128)S(1)} %get-tuple-element.147.dq_ref.refs_6_, bf16[512,512]{1,0:T(8,128)(2,1)S(1)} %copy-done.14, ...), custom_call_target="tpu_custom_call" | custom-call | flops 44000002048 | bytes 1048576 | tf_op jit(solution)/shard_map/finish/pallas_call | solution.py:311
  127.3 10.6 %all-to-all-done = bf16[64,16,512]{2,1,0:T(8,128)(2,1)} async-done(((bf16[64,16,512]{2,1,0:T(8,128)(2,1)}), bf16[64,16,512]{2,1,0:T(8,128)(2,1)}, u32[]{:S(2)}, u32[]{:S(2)}) %all-to-all-start) | async-done | bytes 1048608 | tf_op jit(solution)/shard_map/all_to_all | solution.py:478
  137.9 1.4 %convert_reduce_fusion = f32[16,512]{1,0:T(8,128)S(1)} fusion(bf16[64,16,512]{2,1,0:T(8,128)(2,1)} %all-to-all-done), kind=kLoop, calls=%fused_computation | loop fusion | flops 1040384 | bytes 1081344 | tf_op jit(solution)/shard_map/reduce_sum | solution.py:479
  (65 shorter events, 21.1 us)
Async XLA Ops:
  0.6 19.7 %collective-permute-start = (bf16[512,512]{1,0:T(8,128)(2,1)}, bf16[512,512]{1,0:T(8,128)(2,1)S(1)}, u32[]{:S(2)}, u32[]{:S(2)}) collective-permute-start(bf16[512,512]{1,0:T(8,128)(2,1)} %bitcast.25), channel_id=1, source_target_pairs={{0,4},{1,5},{2,6},{3,7},{4,8},{5,9},{6,10},{7,11},{8,12},{9,13},{1... | collective-permute-start | bytes 1572872 | tf_op jit(solution)/shard_map/ppermute | solution.py:425
  4.2 31.0 %collective-permute-start.4 = (bf16[512,512]{1,0:T(8,128)(2,1)}, bf16[512,512]{1,0:T(8,128)(2,1)S(1)}, u32[]{:S(2)}, u32[]{:S(2)}) collective-permute-start(bf16[512,512]{1,0:T(8,128)(2,1)} %bitcast.26), channel_id=1, source_target_pairs={{0,2},{1,3},{4,6},{5,7},{8,10},{9,11},{12,14},{13,15},{16,18},{17,... | collective-permute-start | bytes 1572872 | tf_op jit(solution)/shard_map/ppermute | solution.py:421
  9.3 25.7 %collective-permute-start.1 = (bf16[512,512]{1,0:T(8,128)(2,1)}, bf16[512,512]{1,0:T(8,128)(2,1)S(1)}, u32[]{:S(2)}, u32[]{:S(2)}) collective-permute-start(bf16[512,512]{1,0:T(8,128)(2,1)} %bitcast.27), channel_id=1, source_target_pairs={{0,1},{1,2},{2,3},{3,4},{4,5},{5,6},{6,7},{7,8},{8,9},{9,10},{10,1... | collective-permute-start | bytes 1572872 | tf_op jit(solution)/shard_map/ppermute | solution.py:425
  11.9 1.0 copy-start
  13.0 1.0 copy-start.1
  14.0 1.0 copy-start.2
  15.1 1.0 copy-start.4
  16.6 3.7 %copy-start.7 = (bf16[512,512]{1,0:T(8,128)(2,1)}, bf16[512,512]{1,0:T(8,128)(2,1)S(1)}, u32[]{:S(2)}) copy-start(bf16[512,512]{1,0:T(8,128)(2,1)S(1)} %get-tuple-element.150.wq_ref) | copy-start | bytes 1572868
  16.6 77.4 %copy-start.9 = (bf16[512,512]{1,0:T(8,128)(2,1)}, bf16[512,512]{1,0:T(8,128)(2,1)S(1)}, u32[]{:S(2)}) copy-start(bf16[512,512]{1,0:T(8,128)(2,1)S(1)} %get-tuple-element.91.wk_ref) | copy-start | bytes 1572868
  16.6 77.4 %copy-start.11 = (bf16[512,512]{1,0:T(8,128)(2,1)}, bf16[512,512]{1,0:T(8,128)(2,1)S(1)}, u32[]{:S(2)}) copy-start(bf16[512,512]{1,0:T(8,128)(2,1)S(1)} %get-tuple-element.92.wv_ref) | copy-start | bytes 1572868
  20.3 23.6 %collective-permute-start.3 = (bf16[512,512]{1,0:T(8,128)(2,1)S(1)}, bf16[512,512]{1,0:T(8,128)(2,1)S(1)}, u32[]{:S(2)}, u32[]{:S(2)}) collective-permute-start(bf16[512,512]{1,0:T(8,128)(2,1)S(1)} %collective-permute-done.x_ref.refs_1_), channel_id=1, source_target_pairs={{2,0},{3,1},{6,4},{7,5},{10,8},{11,9},{14,12},{15,13},{18,16},{19,... | collective-permute-start | bytes 1572872 | tf_op jit(solution)/shard_map/ppermute | solution.py:421
  21.6 32.7 %collective-permute-start.2 = (bf16[512,512]{1,0:T(8,128)(2,1)S(1)}, bf16[512,512]{1,0:T(8,128)(2,1)S(1)}, u32[]{:S(2)}, u32[]{:S(2)}) collective-permute-start(bf16[512,512]{1,0:T(8,128)(2,1)S(1)} %bitcast.30), channel_id=1, source_target_pairs={{0,16},{1,17},{2,18},{3,19},{4,20},{5,21},{6,22},{7,23},{8,24},{9,... | collective-permute-start | bytes 1572872 | tf_op jit(solution)/shard_map/ppermute | solution.py:425
  25.6 19.3 %collective-permute-start.5 = (bf16[512,512]{1,0:T(8,128)(2,1)S(1)}, bf16[512,512]{1,0:T(8,128)(2,1)S(1)}, u32[]{:S(2)}, u32[]{:S(2)}) collective-permute-start(bf16[512,512]{1,0:T(8,128)(2,1)S(1)} %bitcast.31), channel_id=1, source_target_pairs={{0,8},{1,9},{2,10},{3,11},{4,12},{5,13},{6,14},{7,15},{8,16},{9,17... | collective-permute-start | bytes 1572872 | tf_op jit(solution)/shard_map/ppermute | solution.py:425
  54.3 1.2 copy-start.6
  58.5 14.5 %collective-permute-start.7 = (bf16[512,512]{1,0:T(8,128)(2,1)S(1)}, bf16[512,512]{1,0:T(8,128)(2,1)S(1)}, u32[]{:S(2)}, u32[]{:S(2)}) collective-permute-start(bf16[512,512]{1,0:T(8,128)(2,1)S(1)} %get-tuple-element.155), channel_id=1, source_target_pairs={{0,2},{1,3},{2,0},{3,1},{4,6},{5,7},{6,4},{7,5},{8,10},{9,11},{10,... | collective-permute-start | bytes 1572872 | tf_op jit(solution)/shard_map/ppermute | solution.py:421
  64.3 20.0 %collective-permute-start.6 = (bf16[512,512]{1,0:T(8,128)(2,1)S(1)}, bf16[512,512]{1,0:T(8,128)(2,1)S(1)}, u32[]{:S(2)}, u32[]{:S(2)}) collective-permute-start(bf16[512,512]{1,0:T(8,128)(2,1)S(1)} %get-tuple-element.154), channel_id=1, source_target_pairs={{0,3},{1,0},{2,1},{3,2},{4,7},{5,4},{6,5},{7,6},{8,11},{9,8},{10,9... | collective-permute-start | bytes 1572872 | tf_op jit(solution)/shard_map/ppermute | solution.py:421
  65.2 26.7 %collective-permute-start.9 = (bf16[512,512]{1,0:T(8,128)(2,1)S(1)}, bf16[512,512]{1,0:T(8,128)(2,1)S(1)}, u32[]{:S(2)}, u32[]{:S(2)}) collective-permute-start(bf16[512,512]{1,0:T(8,128)(2,1)S(1)} %get-tuple-element.167), channel_id=1, source_target_pairs={{16,0},{17,1},{18,2},{19,3},{20,4},{21,5},{22,6},{23,7},{24,8},{25... | collective-permute-start | bytes 1572872 | tf_op jit(solution)/shard_map/ppermute | solution.py:425
  67.7 26.3 %collective-permute-start.8 = (bf16[512,512]{1,0:T(8,128)(2,1)S(1)}, bf16[512,512]{1,0:T(8,128)(2,1)S(1)}, u32[]{:S(2)}, u32[]{:S(2)}) collective-permute-start(bf16[512,512]{1,0:T(8,128)(2,1)S(1)} %get-tuple-element.158), channel_id=1, source_target_pairs={{8,0},{9,1},{10,2},{11,3},{12,4},{13,5},{14,6},{15,7},{16,8},{17,9... | collective-permute-start | bytes 1572872 | tf_op jit(solution)/shard_map/ppermute | solution.py:425
  72.5 19.5 %copy-start.13 = (bf16[512,512]{1,0:T(8,128)(2,1)}, bf16[512,512]{1,0:T(8,128)(2,1)S(1)}, u32[]{:S(2)}) copy-start(bf16[512,512]{1,0:T(8,128)(2,1)S(1)} %get-tuple-element.148.dk_ref.refs_2_) | copy-start | bytes 1572868
  72.5 19.4 %copy-start.15 = (bf16[512,512]{1,0:T(8,128)(2,1)}, bf16[512,512]{1,0:T(8,128)(2,1)S(1)}, u32[]{:S(2)}) copy-start(bf16[512,512]{1,0:T(8,128)(2,1)S(1)} %get-tuple-element.149.dv_ref.refs_4_) | copy-start | bytes 1572868
  93.9 4.0 %collective-permute-start.11 = (bf16[64,16,512]{2,1,0:T(8,128)(2,1)S(1)}, bf16[64,16,512]{2,1,0:T(8,128)(2,1)S(1)}, u32[]{:S(2)}, u32[]{:S(2)}) collective-permute-start(bf16[64,16,512]{2,1,0:T(8,128)(2,1)S(1)} %get-tuple-element.175), channel_id=1, source_target_pairs={{0,32},{32,0},{64,96},{96,64},{1,33},{33,1},{65,97},{97,65},{2,34}... | collective-permute-start | bytes 3145736 | tf_op jit(solution)/shard_map/ppermute | solution.py:475
  96.7 22.3 %collective-permute-start.10 = (bf16[512,512]{1,0:T(8,128)(2,1)S(1)}, bf16[512,512]{1,0:T(8,128)(2,1)S(1)}, u32[]{:S(2)}, u32[]{:S(2)}) collective-permute-start(bf16[512,512]{1,0:T(8,128)(2,1)S(1)} %get-tuple-element.170), channel_id=1, source_target_pairs={{4,0},{5,1},{6,2},{7,3},{8,4},{9,5},{10,6},{11,7},{12,8},{13,9},{1... | collective-permute-start | bytes 1572872 | tf_op jit(solution)/shard_map/ppermute | solution.py:425
  99.2 38.6 %all-to-all-start = ((bf16[64,16,512]{2,1,0:T(8,128)(2,1)}), bf16[64,16,512]{2,1,0:T(8,128)(2,1)}, u32[]{:S(2)}, u32[]{:S(2)}) async-start(bf16[64,16,512]{2,1,0:T(8,128)(2,1)} %sum_of.1), calls=%async_computation | async-start | bytes 2097152 | tf_op jit(solution)/shard_map/all_to_all | solution.py:478
  119.0 1.0 copy-start.8
  (8 other events, 8.1 us)
